TPU v7x, 32 devices: a whole 2x2x4 slice. The times are simulated.
32 devices in a mesh: fsdp: 8 (over z, y), sub: 4 (over x, core).
Axes of the slice: x: 2, y: 2, z: 4, core: 2. Of those that a mesh axis runs over, the one named last changes fastest.
Arguments:
- code_vectors: bfloat16 [32768, 32], P(('fsdp', 'sub')), may hold values from -6 to 6
- scale_ids: int32 [32768], P(('fsdp', 'sub')), may hold values from 0 to 9, as said below
- segment_ids: int32 [32768], P(('fsdp', 'sub')), may hold values from 0 to 1, as said below
- real_mask: int32 [32768], P(('fsdp', 'sub')), may hold values from 0 to 1, as said below
- labels: int32 [64], P(('fsdp', 'sub')), may hold values from 0 to 999
- targets: int32 [32768], P(('fsdp', 'sub')), may hold values from 0 to 4095
- loss_weight: int32 [32768], P(('fsdp', 'sub')), may hold values from 0 to 9, as said below
- tables: float32 [1024, 1042], P(('fsdp', 'sub')), may hold values from -10 to 10
- vectors: float32 [1024, 9], P(('fsdp', 'sub')), may hold values from -1.2 to 1.6
- ada_weight: float32 [1024, 6144], P(('fsdp', 'sub')), may hold values from -0.15625 to 0.15625
- qkv_weight: float32 [1024, 3072], P(('fsdp', 'sub')), may hold values from -0.3125 to 0.3125
- out_weight: float32 [1024, 1024], P(('fsdp', 'sub')), may hold values from -1.25 to 1.25
- up_weight: float32 [1024, 4096], P(('fsdp', 'sub')), may hold values from -0.3125 to 0.3125
- down_weight: float32 [4096, 1024], P(('fsdp', 'sub')), may hold values from -0.15625 to 0.15625
- head_weight: float32 [1024, 4096], P(('fsdp', 'sub')), may hold values from -0.3125 to 0.3125
- tables_moment: float32 [1024], P(('fsdp', 'sub')), may hold values from 5.79834e-09 to 2.319336e-08
- ada_moment: float32 [1024], P(('fsdp', 'sub')), may hold values from 5.79834e-09 to 2.319336e-08
- qkv_moment: float32 [1024], P(('fsdp', 'sub')), may hold values from 5.79834e-09 to 2.319336e-08
- out_moment: float32 [1024], P(('fsdp', 'sub')), may hold values from 5.79834e-09 to 2.319336e-08
- up_moment: float32 [1024], P(('fsdp', 'sub')), may hold values from 5.79834e-09 to 2.319336e-08
- down_moment: float32 [4096], P(('fsdp', 'sub')), may hold values from 5.79834e-09 to 2.319336e-08
- head_moment: float32 [1024], P(('fsdp', 'sub')), may hold values from 5.79834e-09 to 2.319336e-08
- vector_moment: float32 [1024, 9], P(('fsdp', 'sub')), may hold values from 5.79834e-09 to 2.319336e-08
- column_moment: float32 [20498], replicated, may hold values from 5.79834e-09 to 2.319336e-08
Outputs:
- loss_sum: float32 [], replicated
- weight_total: float32 [], replicated
- tables_grad: float32 [1024, 1042], P(('fsdp', 'sub'))
- tables_stat: float32 [1024], P(('fsdp', 'sub'))
- tables_next: float32 [1024, 1042], P(('fsdp', 'sub'))
- vectors_grad: float32 [1024, 9], P(('fsdp', 'sub'))
- vectors_stat: float32 [1024, 9], P(('fsdp', 'sub'))
- vectors_next: float32 [1024, 9], P(('fsdp', 'sub'))
- ada_grad: float32 [1024, 6144], P(('fsdp', 'sub'))
- ada_stat: float32 [1024], P(('fsdp', 'sub'))
- ada_next: float32 [1024, 6144], P(('fsdp', 'sub'))
- qkv_grad: float32 [1024, 3072], P(('fsdp', 'sub'))
- qkv_stat: float32 [1024], P(('fsdp', 'sub'))
- qkv_next: float32 [1024, 3072], P(('fsdp', 'sub'))
- out_grad: float32 [1024, 1024], P(('fsdp', 'sub'))
- out_stat: float32 [1024], P(('fsdp', 'sub'))
- out_next: float32 [1024, 1024], P(('fsdp', 'sub'))
- up_grad: float32 [1024, 4096], P(('fsdp', 'sub'))
- up_stat: float32 [1024], P(('fsdp', 'sub'))
- up_next: float32 [1024, 4096], P(('fsdp', 'sub'))
- down_grad: float32 [4096, 1024], P(('fsdp', 'sub'))
- down_stat: float32 [4096], P(('fsdp', 'sub'))
- down_next: float32 [4096, 1024], P(('fsdp', 'sub'))
- head_grad: float32 [1024, 4096], P(('fsdp', 'sub'))
- head_stat: float32 [1024], P(('fsdp', 'sub'))
- head_next: float32 [1024, 4096], P(('fsdp', 'sub'))
- column_stat: float32 [20498], replicated
- clip_spread: float32 [8], replicated
Inputs may be any that keep to these rules, and one draw needn't show every extreme that they name: `scale_ids`: each row holds one whole item of 680 tokens and one item cut after fewer scales, in either order, then padding; scales count from 0 within each item, padding has scale 0. `segment_ids`: 0 for the first item of a row, 1 for the second and for padding. `real_mask`: padding only after both items. `loss_weight`: 0 exactly on padding.
All inputs are finite; a program needn't handle non-finite values.
Results may differ from a plain program's by a relative error of at most 0.0075.
The roundings to bfloat16 on the way count: a program that leaves them out, or rounds other values in their place, can miss the bound.
Values may be sent and summed in bfloat16 or wider, within the bound.
A program may use at most 512 MiB of HBM per device.

v0:
```python
from functools import partial

import jax
import jax.numpy as jnp
from jax import lax
from jax.sharding import PartitionSpec as P

D = 1024
HEADS = 16
HEAD_DIM = 64
CLASSES = 1000
CODES = 4096
CODE_DIM = 32
LEVELS = 10
STEP = 10


TINY_SQUARE = 1e-30
SCALE_FLOOR = 0.001
STEP_RATE = 1.0
CLIP_LIMIT = 1.0
NORM_EPSILON = 1e-06
MASK_VALUE = -1000000000.0


def precise(left_side, right_side):
    return jnp.dot(
        left_side, right_side, precision=lax.Precision.HIGHEST, preferred_element_type=jnp.float32
    )


def bfloat_product(left_side, right_side):
    return jnp.dot(left_side, right_side, preferred_element_type=jnp.float32)


def layer_norm(values):
    center = values - jnp.mean(values, axis=-1, keepdims=True)
    return center * lax.rsqrt(jnp.mean(center * center, axis=-1, keepdims=True) + NORM_EPSILON)


def head_norm(values, gain_vector):
    shaped = values.reshape(values.shape[0], HEADS, HEAD_DIM)
    normed = shaped * lax.rsqrt(jnp.mean(shaped * shaped, axis=-1, keepdims=True) + NORM_EPSILON)
    return normed * gain_vector.reshape(1, HEADS, HEAD_DIM)


def modulate(values, scale_part, shift_part):
    return layer_norm(values) * (1.0 + scale_part) + shift_part


def final_norm(values, gain_vector):
    return layer_norm(values) * gain_vector


def attention_mask(scale_row, segment_row, real_row):
    same_item = segment_row[:, None] == segment_row[None, :]
    earlier = scale_row[None, :] <= scale_row[:, None]
    places = jnp.arange(scale_row.shape[0])
    usable = (real_row[None, :] == 1) | (places[:, None] == places[None, :])
    return same_item & earlier & usable


def on_device(
    code_vectors,
    scale_ids,
    segment_ids,
    real_mask,
    labels,
    targets,
    loss_weight,
    tables,
    vectors,
    ada_weight,
    qkv_weight,
    out_weight,
    up_weight,
    down_weight,
    head_weight,
    tables_moment,
    ada_moment,
    qkv_moment,
    out_moment,
    up_moment,
    down_moment,
    head_moment,
    vector_moment,
    column_moment,
):
    devices = lax.axis_size(("fsdp", "sub"))
    masters = (
        tables,
        vectors,
        ada_weight,
        qkv_weight,
        out_weight,
        up_weight,
        down_weight,
        head_weight,
    )
    local_count = jnp.sum(loss_weight).astype(jnp.float32)
    local_squares = jnp.stack([jnp.sum(master * master) for master in masters])
    weight_total = lax.psum(local_count, ("fsdp", "sub"))
    tables_low = tables.astype(jnp.bfloat16)
    vectors_low = vectors.astype(jnp.bfloat16)
    ada_low = ada_weight.astype(jnp.bfloat16)
    qkv_low = qkv_weight.astype(jnp.bfloat16)
    out_low = out_weight.astype(jnp.bfloat16)
    up_low = up_weight.astype(jnp.bfloat16)
    down_low = down_weight.astype(jnp.bfloat16)
    head_low = head_weight.astype(jnp.bfloat16)
    first_full = (
        lax.all_gather(tables_low, ("fsdp", "sub"), axis=0, tiled=True),
        lax.all_gather(vectors_low, ("fsdp", "sub"), axis=0, tiled=True),
        lax.all_gather(ada_low, ("fsdp", "sub"), axis=0, tiled=True),
        lax.all_gather(qkv_low, ("fsdp", "sub"), axis=0, tiled=True),
        lax.all_gather(out_low, ("fsdp", "sub"), axis=0, tiled=True),
    )
    full_tables, full_vectors, full_ada, full_qkv, full_out = first_full
    gain_vector = full_vectors.astype(jnp.float32)
    level_hot = (scale_ids[:, None] == jnp.arange(LEVELS)[None, :]).astype(jnp.float32)
    label_hot = (labels[:, None] == jnp.arange(CLASSES)[None, :]).astype(jnp.bfloat16)
    segment_hot = (segment_ids[:, None] == jnp.arange(2)[None, :]).astype(jnp.float32)
    level_rows = full_tables[:, CLASSES + CODE_DIM :].astype(jnp.float32)
    embedded = bfloat_product(
        code_vectors, full_tables[:, CLASSES : CLASSES + CODE_DIM].T
    ) + precise(level_hot, level_rows.T)
    class_cond = bfloat_product(label_hot, full_tables[:, :CLASSES].T)
    activated = jax.nn.silu(class_cond).astype(jnp.bfloat16)
    modulation = bfloat_product(activated, full_ada) + gain_vector[:, :6].T.reshape(1, 6 * D)
    token_mod = precise(segment_hot, modulation)
    gamma_one, gamma_two, scale_one, scale_two, shift_one, shift_two = jnp.split(
        token_mod, 6, axis=1
    )
    normed = modulate(embedded, scale_one, shift_one).astype(jnp.bfloat16)
    projected = bfloat_product(normed, full_qkv)
    query_raw = projected[:, :D]
    key_raw = projected[:, D : 2 * D]
    queries = head_norm(query_raw, gain_vector[:, 6]).astype(jnp.bfloat16)
    keys_all = head_norm(key_raw, gain_vector[:, 7]).astype(jnp.bfloat16)
    values_all = projected[:, 2 * D :].reshape(-1, HEADS, HEAD_DIM).astype(jnp.bfloat16)
    allowed = attention_mask(scale_ids, segment_ids, real_mask)
    root_scale = HEAD_DIM ** (-0.5)

    def score_block():
        raw_scores = (
            jnp.einsum("qhd,khd->hqk", queries, keys_all, preferred_element_type=jnp.float32)
            * root_scale
        )
        return jnp.where(allowed[None], raw_scores, MASK_VALUE)

    scores = score_block()
    score_peak = jnp.max(scores, axis=-1, keepdims=True)
    score_total = score_peak + jnp.log(
        jnp.sum(jnp.exp(scores - score_peak), axis=-1, keepdims=True)
    )
    probabilities = jnp.exp(scores - score_total)
    mixed_heads = (
        jnp.einsum(
            "hqk,khd->qhd",
            probabilities.astype(jnp.bfloat16),
            values_all,
            preferred_element_type=jnp.float32,
        )
        .reshape(-1, D)
        .astype(jnp.bfloat16)
    )
    attended = bfloat_product(mixed_heads, full_out)
    residual_one = embedded + gamma_one * attended
    second_full = (
        lax.all_gather(up_low, ("fsdp", "sub"), axis=0, tiled=True),
        lax.all_gather(down_low, ("fsdp", "sub"), axis=0, tiled=True),
        lax.all_gather(head_low, ("fsdp", "sub"), axis=0, tiled=True),
    )
    full_up, full_down, full_head = second_full
    normed_two = modulate(residual_one, scale_two, shift_two).astype(jnp.bfloat16)
    hidden_pre = bfloat_product(normed_two, full_up)
    hidden_act = jax.nn.gelu(hidden_pre, approximate=True).astype(jnp.bfloat16)
    branch = bfloat_product(hidden_act, full_down)
    residual_two = residual_one + gamma_two * branch
    final_normed = final_norm(residual_two, gain_vector[:, 8]).astype(jnp.bfloat16)
    logits = bfloat_product(final_normed, full_head)
    logit_peak = jnp.max(logits, axis=-1, keepdims=True)
    log_total = logit_peak + jnp.log(jnp.sum(jnp.exp(logits - logit_peak), axis=-1, keepdims=True))
    target_hot = targets[:, None] == jnp.arange(CODES)[None, :]
    picked = jnp.sum(jnp.where(target_hot, logits, 0.0), axis=-1, keepdims=True)
    weight_column = loss_weight.astype(jnp.float32)[:, None]
    local_loss = jnp.sum(weight_column * (log_total - picked))
    loss_sum = lax.psum(local_loss, ("fsdp", "sub"))
    logit_grad = (
        (jnp.exp(logits - log_total) - target_hot.astype(jnp.float32))
        * (weight_column / weight_total)
    ).astype(jnp.bfloat16)
    head_grad = bfloat_product(final_normed.T, logit_grad)
    final_grad = bfloat_product(logit_grad, full_head.T)
    _, final_back = jax.vjp(final_norm, residual_two, gain_vector[:, 8])
    residual_grad, head_gain_grad = final_back(final_grad)
    branch_grad = (gamma_two * residual_grad).astype(jnp.bfloat16)
    gamma_two_grad = residual_grad * branch
    down_grad = bfloat_product(hidden_act.T, branch_grad)
    act_grad = bfloat_product(branch_grad, full_down.T)
    _, gelu_back = jax.vjp(partial(jax.nn.gelu, approximate=True), hidden_pre)
    pre_grad = gelu_back(act_grad)[0].astype(jnp.bfloat16)
    up_grad = bfloat_product(normed_two.T, pre_grad)
    normed_two_grad = bfloat_product(pre_grad, full_up.T)
    _, modulate_two_back = jax.vjp(modulate, residual_one, scale_two, shift_two)
    norm_grad, scale_two_grad, shift_two_grad = modulate_two_back(normed_two_grad)
    residual_grad = residual_grad + norm_grad
    second_grads = (
        lax.psum_scatter(up_grad, ("fsdp", "sub"), scatter_dimension=0, tiled=True),
        lax.psum_scatter(down_grad, ("fsdp", "sub"), scatter_dimension=0, tiled=True),
        lax.psum_scatter(head_grad, ("fsdp", "sub"), scatter_dimension=0, tiled=True),
    )
    attended_grad = (gamma_one * residual_grad).astype(jnp.bfloat16)
    gamma_one_grad = residual_grad * attended
    out_grad = bfloat_product(mixed_heads.T, attended_grad)
    mixed_grad = (
        bfloat_product(attended_grad, full_out.T).astype(jnp.bfloat16).reshape(-1, HEADS, HEAD_DIM)
    )
    probabilities = jnp.exp(score_block() - score_total)
    prob_grad = jnp.einsum(
        "qhd,khd->hqk", mixed_grad, values_all, preferred_element_type=jnp.float32
    )
    value_grad = jnp.einsum(
        "hqk,qhd->khd",
        probabilities.astype(jnp.bfloat16),
        mixed_grad,
        preferred_element_type=jnp.float32,
    ).reshape(-1, D)
    score_grad = (
        probabilities * (prob_grad - jnp.sum(probabilities * prob_grad, axis=-1, keepdims=True))
    ).astype(jnp.bfloat16)
    query_grad = (
        jnp.einsum("hqk,khd->qhd", score_grad, keys_all, preferred_element_type=jnp.float32)
        * root_scale
    )
    key_grad = (
        jnp.einsum("hqk,qhd->khd", score_grad, queries, preferred_element_type=jnp.float32)
        * root_scale
    )
    _, query_back = jax.vjp(head_norm, query_raw, gain_vector[:, 6])
    query_raw_grad, query_gain_grad = query_back(query_grad)
    _, key_back = jax.vjp(head_norm, key_raw, gain_vector[:, 7])
    key_raw_grad, key_gain_grad = key_back(key_grad)
    projected_grad = jnp.concatenate([query_raw_grad, key_raw_grad, value_grad], axis=1).astype(
        jnp.bfloat16
    )
    qkv_grad = bfloat_product(normed.T, projected_grad)
    normed_grad = bfloat_product(projected_grad, full_qkv.T)
    _, modulate_one_back = jax.vjp(modulate, embedded, scale_one, shift_one)
    norm_grad, scale_one_grad, shift_one_grad = modulate_one_back(normed_grad)
    embedded_grad = residual_grad + norm_grad
    token_mod_grad = jnp.concatenate(
        [
            gamma_one_grad,
            gamma_two_grad,
            scale_one_grad,
            scale_two_grad,
            shift_one_grad,
            shift_two_grad,
        ],
        axis=1,
    )
    modulation_grad = precise(segment_hot.T, token_mod_grad)
    bias_grad = jnp.sum(modulation_grad, axis=0).reshape(6, D).T
    modulation_low = modulation_grad.astype(jnp.bfloat16)
    ada_grad = bfloat_product(activated.T, modulation_low)
    activated_grad = bfloat_product(modulation_low, full_ada.T)
    _, silu_back = jax.vjp(jax.nn.silu, class_cond)
    cond_grad = silu_back(activated_grad)[0]
    class_grad = precise(cond_grad.T, label_hot.astype(jnp.float32))
    code_grad = precise(embedded_grad.T, code_vectors.astype(jnp.float32))
    level_grad = precise(embedded_grad.T, level_hot)
    tables_grad = jnp.concatenate([class_grad, code_grad, level_grad], axis=1)
    vectors_grad = jnp.concatenate(
        [bias_grad, query_gain_grad[:, None], key_gain_grad[:, None], head_gain_grad[:, None]],
        axis=1,
    )
    first_grads = (
        lax.psum_scatter(tables_grad, ("fsdp", "sub"), scatter_dimension=0, tiled=True),
        lax.psum_scatter(vectors_grad, ("fsdp", "sub"), scatter_dimension=0, tiled=True),
        lax.psum_scatter(ada_grad, ("fsdp", "sub"), scatter_dimension=0, tiled=True),
        lax.psum_scatter(qkv_grad, ("fsdp", "sub"), scatter_dimension=0, tiled=True),
        lax.psum_scatter(out_grad, ("fsdp", "sub"), scatter_dimension=0, tiled=True),
    )
    gradients = tuple(first_grads) + tuple(second_grads)
    second_decay = 1.0 - STEP ** (-0.8)
    factored_index = (0, 2, 3, 4, 5, 6, 7)
    factored_moments = (
        tables_moment,
        ada_moment,
        qkv_moment,
        out_moment,
        up_moment,
        down_moment,
        head_moment,
    )
    rows_list = []
    column_parts = []
    row_parts = []
    for position, moment in zip(factored_index, factored_moments):
        gradient = gradients[position]
        squared = gradient * gradient + TINY_SQUARE
        rows_new = second_decay * moment + (1.0 - second_decay) * jnp.mean(squared, axis=1)
        rows_list.append(rows_new)
        column_parts.append(jnp.sum(squared, axis=0))
        row_parts.append(jnp.sum(rows_new))
    column_local = jnp.concatenate(column_parts)
    row_local = jnp.stack(row_parts)
    column_total, row_total, weight_squares = lax.psum(
        (column_local, row_local, local_squares), ("fsdp", "sub")
    )
    updates = [None] * 8
    moments_new = [None] * 8
    column_new = []
    offset = 0
    for factor_slot, position in enumerate(factored_index):
        gradient = gradients[position]
        rows_all = gradient.shape[0] * devices
        column_count = gradient.shape[1]
        cols_new = second_decay * column_moment[offset : offset + column_count] + (
            1.0 - second_decay
        ) * (column_total[offset : offset + column_count] / rows_all)
        offset += column_count
        estimate = (
            rows_list[factor_slot][:, None]
            * cols_new[None, :]
            / (row_total[factor_slot] / rows_all)
        )
        updates[position] = gradient * lax.rsqrt(estimate)
        moments_new[position] = rows_list[factor_slot]
        column_new.append(cols_new)
    vector_new = second_decay * vector_moment + (1.0 - second_decay) * (
        gradients[1] * gradients[1] + TINY_SQUARE
    )
    updates[1] = gradients[1] * lax.rsqrt(vector_new)
    moments_new[1] = vector_new
    local_spread = jnp.stack([jnp.sum(update * update) for update in updates])
    spread_total = lax.psum(local_spread, ("fsdp", "sub"))
    next_weights = []
    spreads = []
    for position in range(8):
        count_all = gradients[position].size * devices
        spread = jnp.sqrt(spread_total[position] / count_all)
        step_scale = jnp.maximum(SCALE_FLOOR, jnp.sqrt(weight_squares[position] / count_all))
        next_weights.append(
            masters[position]
            - STEP_RATE * step_scale * (updates[position] / jnp.maximum(1.0, spread / CLIP_LIMIT))
        )
        spreads.append(spread)
    column_stat = jnp.concatenate(column_new)
    clip_spread = jnp.stack(spreads)
    return (
        loss_sum,
        weight_total,
        gradients[0],
        moments_new[0],
        next_weights[0],
        gradients[1],
        moments_new[1],
        next_weights[1],
        gradients[2],
        moments_new[2],
        next_weights[2],
        gradients[3],
        moments_new[3],
        next_weights[3],
        gradients[4],
        moments_new[4],
        next_weights[4],
        gradients[5],
        moments_new[5],
        next_weights[5],
        gradients[6],
        moments_new[6],
        next_weights[6],
        gradients[7],
        moments_new[7],
        next_weights[7],
        column_stat,
        clip_spread,
    )


def solution(mesh):
    in_specs = (
        P(("fsdp", "sub"), None),
        P(("fsdp", "sub")),
        P(("fsdp", "sub")),
        P(("fsdp", "sub")),
        P(("fsdp", "sub")),
        P(("fsdp", "sub")),
        P(("fsdp", "sub")),
        P(("fsdp", "sub"), None),
        P(("fsdp", "sub"), None),
        P(("fsdp", "sub"), None),
        P(("fsdp", "sub"), None),
        P(("fsdp", "sub"), None),
        P(("fsdp", "sub"), None),
        P(("fsdp", "sub"), None),
        P(("fsdp", "sub"), None),
        P(("fsdp", "sub")),
        P(("fsdp", "sub")),
        P(("fsdp", "sub")),
        P(("fsdp", "sub")),
        P(("fsdp", "sub")),
        P(("fsdp", "sub")),
        P(("fsdp", "sub")),
        P(("fsdp", "sub"), None),
        P(),
    )
    out_specs = (
        P(),
        P(),
        P(("fsdp", "sub"), None),
        P(("fsdp", "sub")),
        P(("fsdp", "sub"), None),
        P(("fsdp", "sub"), None),
        P(("fsdp", "sub"), None),
        P(("fsdp", "sub"), None),
        P(("fsdp", "sub"), None),
        P(("fsdp", "sub")),
        P(("fsdp", "sub"), None),
        P(("fsdp", "sub"), None),
        P(("fsdp", "sub")),
        P(("fsdp", "sub"), None),
        P(("fsdp", "sub"), None),
        P(("fsdp", "sub")),
        P(("fsdp", "sub"), None),
        P(("fsdp", "sub"), None),
        P(("fsdp", "sub")),
        P(("fsdp", "sub"), None),
        P(("fsdp", "sub"), None),
        P(("fsdp", "sub")),
        P(("fsdp", "sub"), None),
        P(("fsdp", "sub"), None),
        P(("fsdp", "sub")),
        P(("fsdp", "sub"), None),
        P(),
        P(),
    )
    return jax.shard_map(
        on_device, mesh=mesh, in_specs=in_specs, out_specs=out_specs, check_vma=False
    )
```

profile of v0, /device:TPU:0, one launch (start us, length us, event | category | flops | bytes accessed | tf_op | source)
XLA Modules:
  0.0 2468.5 jit_solution(11884644514001450593)
XLA Ops:
  24.9 43.9 %all-gather = bf16[32,32,9]{1,2,0:T(8,128)(2,1)S(1)} all-gather(bf16[1,32,9]{1,2,0:T(8,128)(2,1)S(1)} %get-tuple-element.221), channel_id=1, replica_groups=mesh['fsdp'=8,'sub'=4] {'fsdp','sub'}, dimensions={0}, use_global_device_ids=true | all-gather | bytes 19008 | tf_op jit(solution)/shard_map/all_gather | solution.py:113
  69.5 37.5 %psum.43 = f32[]{:T(128)} all-reduce(f32[]{:T(128)S(6)} %convert_element_type.124), channel_id=1, replica_groups=mesh['fsdp'=8,'sub'=4] {'fsdp','sub'}, use_global_device_ids=true, to_apply=%region_16.17 | all-reduce | flops 1 | bytes 8 | tf_op jit(solution)/shard_map/psum | solution.py:102
  116.5 54.5 %all-gather.11.cloned.1.call-done = bf16[1024,6144]{1,0:T(8,128)(2,1)} async-done(((bf16[32,6144]{1,0:T(8,128)(2,1)}), bf16[1024,6144]{1,0:T(8,128)(2,1)}) %all-gather.11.cloned.1.call-update) | async-done | bytes 12582928 | tf_op jit(solution)/shard_map/all_gather | solution.py:114
  170.9 6.3 convolution_add_fusion
  177.3 13.8 fusion.30
  191.1 5.1 fusion.12
  196.3 45.9 %all-gather.13.cloned.1.call-done = bf16[1024,3072]{1,0:T(8,128)(2,1)} async-done(((bf16[32,3072]{1,0:T(8,128)(2,1)}), bf16[1024,3072]{1,0:T(8,128)(2,1)}) %all-gather.13.cloned.1.call-update) | async-done | bytes 6291472 | tf_op jit(solution)/shard_map/all_gather | solution.py:115
  242.2 9.2 fusion.112
  253.1 4.1 fusion.105
  257.2 5.4 copy.113
  265.5 3.5 multiply_reduce_fusion.7
  269.0 5.4 copy.112
  277.9 26.5 %fusion = (f32[16,1024]{1,0:T(8,128)S(1)}, f32[16,1024,1024]{1,2,0:T(8,128)}) fusion(pred[1024,1024]{0,1:T(8,128)(4,1)S(1)} %fusion.18, f32[1024,16,64]{0,2,1:T(8,128)S(1)} %bitcast.137, f32[16,64]{1,0:T(8,128)S(1)} %mul.800, f32[1024,16]{0,1:T(8,128)S(1)} %get-tuple-element.265, f32[1024,16,64]{0,2,1:T(8,128)} %bitcast.138, f32[16,64]{1,0:T(8,128)S(1)} %mul.794, ...), kind=kOutput, calls=%fused_computation.5 | convolution fusion | flops 2204090368 | bytes 76750848 | tf_op jit(solution)/shard_map/qhd,khd->hqk/dot_general | solution.py:146
  304.4 21.9 exponential_reduce_fusion
  327.0 27.1 %convolution_convert_fusion.1 = bf16[16,64,1024]{2,1,0:T(8,128)(2,1)} fusion(bf16[1024,16,64]{0,2,1:T(8,128)(2,1)S(1)} %bitcast.141, f32[16,1024,1024]{1,2,0:T(8,128)} %get-tuple-element.249, f32[16,1024]{1,0:T(8,128)S(1)} %log_add_fusion, pred[1024,1024]{0,1:T(8,128)(4,1)S(1)} %fusion.18), kind=kOutput, calls=%fused_computation.81 | convolution fusion | flops 2215641088 | bytes 72417280 | tf_op jit(solution)/shard_map/hqk,khd->qhd/dot_general | solution.py:158
  354.1 9.7 fusion.104
  366.4 5.3 fusion.11
  371.8 8.2 all-gather.17.cloned.1.call-done
  380.0 14.7 fusion.113
  394.7 64.7 %all-gather.19.cloned.1.call-done = bf16[4096,1024]{1,0:T(8,128)(2,1)} async-done(((bf16[128,1024]{1,0:T(8,128)(2,1)}), bf16[4096,1024]{1,0:T(8,128)(2,1)}) %all-gather.19.cloned.1.call-update) | async-done | bytes 8388624 | tf_op jit(solution)/shard_map/all_gather | solution.py:171
  459.4 20.5 fusion.103
  482.4 56.5 %all-gather.21.cloned.1.call-done = bf16[1024,4096]{1,0:T(8,128)(2,1)} async-done(((bf16[32,4096]{1,0:T(8,128)(2,1)}), bf16[1024,4096]{1,0:T(8,128)(2,1)}) %all-gather.21.cloned.1.call-update) | async-done | bytes 8388624 | tf_op jit(solution)/shard_map/all_gather | solution.py:172
  538.9 13.8 fusion.110
  552.8 5.6 select_reduce_fusion
  559.6 7.8 multiply_convert_fusion.1
  567.5 15.4 multiply_reduce_fusion.1
  589.2 24.4 fusion.8
  613.7 16.2 multiply_reduce_fusion.3
  630.0 7.2 fusion.101
  637.3 5.7 multiply_dynamic-update-slice_fusion.3
  643.0 4.4 multiply_convert_fusion.3
  647.5 3.7 convolution_convert_fusion.2
  651.2 26.2 %convolution_convert_fusion = bf16[16,64,1024]{2,1,0:T(8,128)(2,1)} fusion(bf16[1024,16,64]{0,2,1:T(8,128)(2,1)} %bitcast.145, f32[16,1024,1024]{1,2,0:T(8,128)} %get-tuple-element.249, f32[16,1024]{1,0:T(8,128)S(1)} %copy-done.39, pred[1024,1024]{0,1:T(8,128)(4,1)S(1)} %copy-done.10), kind=kOutput, calls=%fused_computation.80 | convolution fusion | flops 2215641088 | bytes 72417280 | tf_op jit(solution)/shard_map/hqk,qhd->khd/dot_general | solution.py:223
  677.4 50.0 %multiply_reduce_fusion = (f32[16,1024]{1,0:T(8,128)S(1)}, f32[16,1024,1024]{1,2,0:T(8,128)}) fusion(f32[16,1024,1024]{1,2,0:T(8,128)} %get-tuple-element.249, f32[16,1024]{1,0:T(8,128)S(1)} %copy-done.39, pred[1024,1024]{0,1:T(8,128)(4,1)S(1)} %copy-done.10, bf16[1024,16,64]{0,2,1:T(8,128)(2,1)} %bitcast.146, bf16[1024,16,64]{0,2,1:T(8,128)(2,1)S(1)} %bitcast.142), kind=kOutput, calls=%fused_computation.1 | convolution fusion | flops 2231353344 | bytes 139591680 | tf_op jit(solution)/shard_map/qhd,khd->hqk/dot_general | solution.py:220
  727.4 53.3 %multiply_convert_fusion = bf16[16,1024,1024]{1,2,0:T(8,128)(2,1)} fusion(f32[16,1024,1024]{1,2,0:T(8,128)} %get-tuple-element.258, f32[16,1024,1024]{1,2,0:T(8,128)} %get-tuple-element.249, f32[16,1024]{1,0:T(8,128)S(1)} %get-tuple-element.257, f32[16,1024]{1,0:T(8,128)S(1)} %copy-done.39, pred[1024,1024]{0,1:T(8,128)(4,1)S(1)} %copy-done.10), kind=kLoop, calls=%fused_computation | loop fusion | flops 100663296 | bytes 168951808 | tf_op jit(solution)/shard_map/convert_element_type | solution.py:231
  780.8 19.7 fusion.13
  800.6 19.6 fusion.14
  820.2 7.0 multiply_dynamic-update-slice_fusion.2
  835.1 12.7 multiply_dynamic-update-slice_fusion.1
  847.8 5.3 fusion.100
  858.1 7.0 multiply_dynamic-update-slice_fusion
  871.1 15.0 fusion.111
  887.3 7.9 fusion.65
  899.6 5.7 copy.129
  906.9 5.9 fusion.114
  914.4 14.1 fusion.21
  930.1 18.7 fusion.91
  949.5 16.6 fusion.89
  967.6 14.4 fusion.115
  982.2 10.3 fusion.63
  994.4 5.3 stack.97
  999.6 20.4 reduce-scatter.27.cloned.1.call-done
  1022.1 107.8 %reduce-scatter.25.cloned.1.call-done = f32[32,1042]{1,0:T(8,128)} async-done(((f32[1024,1042]{1,0:T(8,128)}), f32[32,1042]{1,0:T(8,128)}) %reduce-scatter.25.cloned.1.call-update) | async-done | bytes 133392
  1131.9 140.8 %reduce-scatter.17.cloned.1.call-done = f32[32,1024]{1,0:T(8,128)} async-done(((f32[1024,1024]{1,0:T(8,128)}), f32[32,1024]{1,0:T(8,128)}) %reduce-scatter.17.cloned.1.call-update) | async-done | bytes 131088 | tf_op jit(solution)/shard_map/reduce_scatter | solution.py:283
  1274.4 156.3 %reduce-scatter.15.cloned.1.call-done = f32[32,3072]{1,0:T(8,128)} async-done(((f32[1024,3072]{1,0:T(8,128)}), f32[32,3072]{1,0:T(8,128)}) %reduce-scatter.15.cloned.1.call-update) | async-done | bytes 393232 | tf_op jit(solution)/shard_map/reduce_scatter | solution.py:282
  1432.6 183.1 %reduce-scatter.21.cloned.1.call-done = f32[128,1024]{1,0:T(8,128)} async-done(((f32[4096,1024]{1,0:T(8,128)}), f32[128,1024]{1,0:T(8,128)}) %reduce-scatter.21.cloned.1.call-update) | async-done | bytes 524304 | tf_op jit(solution)/shard_map/reduce_scatter | solution.py:210
  1616.8 186.2 %reduce-scatter.23.cloned.1.call-done = f32[32,4096]{1,0:T(8,128)} async-done(((f32[1024,4096]{1,0:T(8,128)}), f32[32,4096]{1,0:T(8,128)}) %reduce-scatter.23.cloned.1.call-update) | async-done | bytes 524304 | tf_op jit(solution)/shard_map/reduce_scatter | solution.py:211
  1804.4 185.8 %reduce-scatter.19.cloned.1.call-done = f32[32,4096]{1,0:T(8,128)} async-done(((f32[1024,4096]{1,0:T(8,128)}), f32[32,4096]{1,0:T(8,128)}) %reduce-scatter.19.cloned.1.call-update) | async-done | bytes 524304 | tf_op jit(solution)/shard_map/reduce_scatter | solution.py:209
  1993.3 252.1 %reduce-scatter.13.cloned.1.call-done = f32[32,6144]{1,0:T(8,128)} async-done(((f32[1024,6144]{1,0:T(8,128)}), f32[32,6144]{1,0:T(8,128)}) %reduce-scatter.13.cloned.1.call-update) | async-done | bytes 786448 | tf_op jit(solution)/shard_map/reduce_scatter | solution.py:281
  2248.2 4.6 stack.105
  2252.8 40.2 %psum.46 = f32[7]{0:T(128)S(1)} all-reduce(f32[7]{0:T(128)S(1)} %stack.105), channel_id=1, replica_groups=mesh['fsdp'=8,'sub'=4] {'fsdp','sub'}, use_global_device_ids=true, to_apply=%region_64.65 | all-reduce | flops 7 | bytes 56 | tf_op jit(solution)/shard_map/psum | solution.py:309
  2298.2 73.9 %all-reduce.3.cloned.1.call-done = f32[20498]{0:T(1024)} async-done(((f32[20498]{0:T(1024)}), f32[20498]{0:T(1024)}) %all-reduce.3.cloned.1.call-update) | async-done | bytes 82008 | tf_op jit(solution)/shard_map/psum | solution.py:309
  2384.0 5.2 stack.114
  2389.2 42.4 %all-reduce = (f32[]{:T(128)}, f32[8]{0:T(128)S(1)}, f32[8]{0:T(128)S(1)}) all-reduce(f32[]{:T(128)} %get-tuple-element.191, f32[8]{0:T(128)S(1)} %stack.114, f32[8]{0:T(128)S(1)} %stack.97), channel_id=1, replica_groups=mesh['fsdp'=8,'sub'=4] {'fsdp','sub'}, use_global_device_ids=true, to_apply=%region_14.15 | all-reduce | flops 17 | bytes 136 | tf_op jit(solution)/shard_map/psum | solution.py:188
  (386 shorter events, 129.1 us)
Async XLA Ops:
  7.2 105.3 %copy-start = (bf16[1024,32]{0,1:T(8,128)(2,1)S(1)}, bf16[1024,32]{0,1:T(8,128)(2,1)}, u32[]{:S(2)}) copy-start(bf16[1024,32]{0,1:T(8,128)(2,1)} %param.24) | copy-start | bytes 196612
  7.3 99.8 %copy-start.112 = (s32[1024]{0:T(1024)S(1)}, s32[1024]{0:T(1024)}, u32[]{:S(2)}) copy-start(s32[1024]{0:T(1024)} %param.27) | copy-start | bytes 12292
  7.3 101.2 %copy-start.52 = (s32[1024]{0:T(1024)S(1)}, s32[1024]{0:T(1024)}, u32[]{:S(2)}) copy-start(s32[1024]{0:T(1024)} %param.26) | copy-start | bytes 12292
  7.3 101.2 %copy-start.73 = (s32[1024]{0:T(1024)S(1)}, s32[1024]{0:T(1024)}, u32[]{:S(2)}) copy-start(s32[1024]{0:T(1024)} %param.25) | copy-start | bytes 12292
  7.3 103.0 %all-gather.9.cloned.1.call-start = ((), (), s32[]{:S(2)}) async-start(), calls=%async_computation.8 | async-start | bytes 2433024 | tf_op jit(solution)/shard_map/all_gather | solution.py:112
  9.7 161.3 %all-gather.11.cloned.1.call-start = ((), (), s32[]{:S(2)}) async-start(), calls=%async_computation.9 | async-start | bytes 12976128 | tf_op jit(solution)/shard_map/all_gather | solution.py:114
  12.6 229.6 %all-gather.13.cloned.1.call-start = ((), (), s32[]{:S(2)}) async-start(), calls=%async_computation.10 | async-start | bytes 6488064 | tf_op jit(solution)/shard_map/all_gather | solution.py:115
  15.1 339.0 %all-gather.15.cloned.1.call-start = ((), (), s32[]{:S(2)}) async-start(), calls=%async_computation.11 | async-start | bytes 2162688 | tf_op jit(solution)/shard_map/all_gather | solution.py:116
  17.4 362.6 %all-gather.17.cloned.1.call-start = ((), (), s32[]{:S(2)}) async-start(), calls=%async_computation.12 | async-start | bytes 8650752 | tf_op jit(solution)/shard_map/all_gather | solution.py:170
  20.0 439.3 %all-gather.19.cloned.1.call-start = ((), (), s32[]{:S(2)}) async-start(), calls=%async_computation.13 | async-start | bytes 8650752 | tf_op jit(solution)/shard_map/all_gather | solution.py:171
  21.5 517.4 %all-gather.21.cloned.1.call-start = ((), (), s32[]{:S(2)}) async-start(), calls=%async_computation.14 | async-start | bytes 8650752 | tf_op jit(solution)/shard_map/all_gather | solution.py:172
  23.0 997.1 %reduce-scatter.27.cloned.1.call-start = ((), (), s32[]{:S(2)}) async-start(), calls=%async_computation.23 | async-start | bytes 540672
  107.2 170.3 %copy-start.60 = (f32[16,64]{1,0:T(8,128)}, f32[16,64]{1,0:T(8,128)S(1)}, u32[]{:S(2)}) copy-start(f32[16,64]{1,0:T(8,128)S(1)} %mul.800) | copy-start | bytes 12292
  107.2 170.2 %copy-start.62 = (f32[16,64]{1,0:T(8,128)}, f32[16,64]{1,0:T(8,128)S(1)}, u32[]{:S(2)}) copy-start(f32[16,64]{1,0:T(8,128)S(1)} %mul.794) | copy-start | bytes 12292
  110.3 216.1 %copy-start.9 = (pred[1024,1024]{0,1:T(8,128)(4,1)}, pred[1024,1024]{0,1:T(8,128)(4,1)S(1)}, u32[]{:S(2)}) copy-start(pred[1024,1024]{0,1:T(8,128)(4,1)S(1)} %fusion.18) | copy-start | bytes 3145732
  113.3 77.8 %copy-start.83 = (f32[1024]{0:T(1024)}, f32[1024]{0:T(1024)S(1)}, u32[]{:S(2)}) copy-start(f32[1024]{0:T(1024)S(1)} %broadcast_multiply_fusion.4) | copy-start | bytes 12292
  115.8 75.3 %copy-start.85 = (f32[1024]{0:T(1024)}, f32[1024]{0:T(1024)S(1)}, u32[]{:S(2)}) copy-start(f32[1024]{0:T(1024)S(1)} %fusion.79) | copy-start | bytes 12292
  116.5 60.8 %copy-start.64 = (f32[2,1024]{1,0:T(2,128)}, f32[2,1024]{1,0:T(2,128)S(1)}, u32[]{:S(2)}) copy-start(f32[2,1024]{1,0:T(2,128)S(1)} %fusion.23) | copy-start | bytes 24580
  196.2 55.1 %copy-start.40 = (bf16[1024,1024]{0,1:T(8,128)(2,1)}, bf16[1024,1024]{0,1:T(8,128)(2,1)S(1)}, u32[]{:S(2)}) copy-start(bf16[1024,1024]{0,1:T(8,128)(2,1)S(1)} %fusion.12) | copy-start | bytes 6291460
  265.5 60.9 %copy-start.24 = (bf16[1024,1024]{0,1:T(8,128)(2,1)}, bf16[1024,1024]{0,1:T(8,128)(2,1)S(1)}, u32[]{:S(2)}) copy-start(bf16[1024,1024]{0,1:T(8,128)(2,1)S(1)} %copy.111) | copy-start | bytes 6291460
  277.4 27.0 %copy-start.57 = (f32[1024,16]{0,1:T(8,128)}, f32[1024,16]{0,1:T(8,128)S(1)}, u32[]{:S(2)}) copy-start(f32[1024,16]{0,1:T(8,128)S(1)} %multiply_reduce_fusion.8) | copy-start | bytes 196612
  277.4 27.0 %copy-start.32 = (f32[1024,16]{0,1:T(8,128)}, f32[1024,16]{0,1:T(8,128)S(1)}, u32[]{:S(2)}) copy-start(f32[1024,16]{0,1:T(8,128)S(1)} %get-tuple-element.265) | copy-start | bytes 196612
  277.5 27.0 %copy-start.34 = (f32[1024,16]{0,1:T(8,128)}, f32[1024,16]{0,1:T(8,128)S(1)}, u32[]{:S(2)}) copy-start(f32[1024,16]{0,1:T(8,128)S(1)} %get-tuple-element.264) | copy-start | bytes 196612
  363.8 266.2 %copy-start.67 = (f32[1024]{0:T(1024)}, f32[1024]{0:T(1024)S(1)}, u32[]{:S(2)}) copy-start(f32[1024]{0:T(1024)S(1)} %broadcast_multiply_fusion.3) | copy-start | bytes 12292
  479.9 59.0 %copy-start.97 = (f32[1024,1]{0,1:T(1,128)S(1)}, f32[1024,1]{0,1:T(1,128)}, u32[]{:S(2)}) copy-start(f32[1024,1]{0,1:T(1,128)} %get-tuple-element.219) | copy-start | bytes 12292
  479.9 103.0 %copy-start.87 = (f32[1024]{0:T(1024)}, f32[1024]{0:T(1024)S(1)}, u32[]{:S(2)}) copy-start(f32[1024]{0:T(1024)S(1)} %broadcast_multiply_fusion.2) | copy-start | bytes 12292
  482.4 100.5 %copy-start.95 = (f32[1024]{0:T(1024)}, f32[1024]{0:T(1024)S(1)}, u32[]{:S(2)}) copy-start(f32[1024]{0:T(1024)S(1)} %fusion.81) | copy-start | bytes 12292
  584.0 53.3 %copy-start.78 = (f32[1024]{0:T(1024)}, f32[1024]{0:T(1024)S(1)}, u32[]{:S(2)}) copy-start(f32[1024]{0:T(1024)S(1)} %negate_multiply_fusion.2) | copy-start | bytes 12292
  727.4 53.3 %copy-start.33 = (f32[1024,16]{0,1:T(8,128)S(1)}, f32[1024,16]{0,1:T(8,128)}, u32[]{:S(2)}) copy-start(f32[1024,16]{0,1:T(8,128)} %copy-done.32) | copy-start | bytes 196612
  727.4 53.3 %copy-start.35 = (f32[1024,16]{0,1:T(8,128)S(1)}, f32[1024,16]{0,1:T(8,128)}, u32[]{:S(2)}) copy-start(f32[1024,16]{0,1:T(8,128)} %copy-done.34) | copy-start | bytes 196612
  727.4 53.3 %copy-start.63 = (f32[16,64]{1,0:T(8,128)S(1)}, f32[16,64]{1,0:T(8,128)}, u32[]{:S(2)}) copy-start(f32[16,64]{1,0:T(8,128)} %copy-done.62) | copy-start | bytes 12292
  727.4 53.4 %copy-start.70 = (f32[16,64]{1,0:T(8,128)S(1)}, f32[16,64]{1,0:T(8,128)}, u32[]{:S(2)}) copy-start(f32[16,64]{1,0:T(8,128)} %broadcast_multiply_fusion) | copy-start | bytes 12292
  887.3 242.6 %reduce-scatter.25.cloned.1.call-start = ((), (), s32[]{:S(2)}) async-start(), calls=%async_computation.22 | async-start | bytes 4866048
  905.3 367.4 %reduce-scatter.17.cloned.1.call-start = ((), (), s32[]{:S(2)}) async-start(), calls=%async_computation.17 | async-start | bytes 4325376 | tf_op jit(solution)/shard_map/reduce_scatter | solution.py:283
  912.8 517.9 %reduce-scatter.15.cloned.1.call-start = ((), (), s32[]{:S(2)}) async-start(), calls=%async_computation.16 | async-start | bytes 12976128 | tf_op jit(solution)/shard_map/reduce_scatter | solution.py:282
  928.5 687.1 %reduce-scatter.21.cloned.1.call-start = ((), (), s32[]{:S(2)}) async-start(), calls=%async_computation.19 | async-start | bytes 17301504 | tf_op jit(solution)/shard_map/reduce_scatter | solution.py:210
  948.8 854.3 %reduce-scatter.23.cloned.1.call-start = ((), (), s32[]{:S(2)}) async-start(), calls=%async_computation.20 | async-start | bytes 17301504 | tf_op jit(solution)/shard_map/reduce_scatter | solution.py:211
  966.1 1024.1 %reduce-scatter.19.cloned.1.call-start = ((), (), s32[]{:S(2)}) async-start(), calls=%async_computation.18 | async-start | bytes 17301504 | tf_op jit(solution)/shard_map/reduce_scatter | solution.py:209
  982.1 1263.3 %reduce-scatter.13.cloned.1.call-start = ((), (), s32[]{:S(2)}) async-start(), calls=%async_computation.15 | async-start | bytes 25952256 | tf_op jit(solution)/shard_map/reduce_scatter | solution.py:281
  992.4 28.4 %copy-start.101 = (f32[32,9]{0,1:T(8,128)S(1)}, f32[32,9]{0,1:T(8,128)}, u32[]{:S(2)}) copy-start(f32[32,9]{0,1:T(8,128)} %param.46) | copy-start | bytes 3460
  992.4 138.8 %copy-start.115 = (f32[32]{0:T(128)S(1)}, f32[32]{0:T(128)}, u32[]{:S(2)}) copy-start(f32[32]{0:T(128)} %param.39) | copy-start | bytes 388
  992.4 281.4 %copy-start.116 = (f32[32]{0:T(128)S(1)}, f32[32]{0:T(128)}, u32[]{:S(2)}) copy-start(f32[32]{0:T(128)} %param.42) | copy-start | bytes 388
  992.4 439.5 %copy-start.117 = (f32[32]{0:T(128)S(1)}, f32[32]{0:T(128)}, u32[]{:S(2)}) copy-start(f32[32]{0:T(128)} %param.41) | copy-start | bytes 388
  992.5 999.1 %copy-start.118 = (f32[128]{0:T(128)S(1)}, f32[128]{0:T(128)}, u32[]{:S(2)}) copy-start(f32[128]{0:T(128)} %param.44) | copy-start | bytes 1540
  992.5 999.7 %copy-start.119 = (f32[32]{0:T(128)S(1)}, f32[32]{0:T(128)}, u32[]{:S(2)}) copy-start(f32[32]{0:T(128)} %param.45) | copy-start | bytes 388
  992.5 1000.3 %copy-start.120 = (f32[32]{0:T(128)S(1)}, f32[32]{0:T(128)}, u32[]{:S(2)}) copy-start(f32[32]{0:T(128)} %param.43) | copy-start | bytes 388
  992.5 1254.3 %copy-start.121 = (f32[32]{0:T(128)S(1)}, f32[32]{0:T(128)}, u32[]{:S(2)}) copy-start(f32[32]{0:T(128)} %param.40) | copy-start | bytes 388
  992.5 1379.6 %copy-start.69 = (f32[20498]{0:T(1024)S(1)}, f32[20498]{0:T(1024)}, u32[]{:S(2)}) copy-start(f32[20498]{0:T(1024)} %param.47) | copy-start | bytes 245980
  992.5 1379.5 %all-reduce.3.cloned.1.call-start = ((), (), s32[]{:S(2)}) async-start(), calls=%async_computation.21 | async-start | bytes 172032 | tf_op jit(solution)/shard_map/psum | solution.py:309
  1131.9 1313.1 %copy-start.102 = (f32[32]{0:T(128)}, f32[32]{0:T(128)S(1)}, u32[]{:S(2)}) copy-start(f32[32]{0:T(128)S(1)} %get-tuple-element.182) | copy-start | bytes 388
  1272.7 1104.2 %copy-start.54 = (f32[32,1024]{1,0:T(8,128)S(1)}, f32[32,1024]{1,0:T(8,128)}, u32[]{:S(2)}) copy-start(f32[32,1024]{1,0:T(8,128)} %reduce-scatter.17.cloned.1.call-done) | copy-start | bytes 393220
  1274.4 1170.5 %copy-start.103 = (f32[32]{0:T(128)}, f32[32]{0:T(128)S(1)}, u32[]{:S(2)}) copy-start(f32[32]{0:T(128)S(1)} %get-tuple-element.176) | copy-start | bytes 388
  1430.7 948.8 %copy-start.31 = (f32[32,3072]{1,0:T(8,128)S(1)}, f32[32,3072]{1,0:T(8,128)}, u32[]{:S(2)}) copy-start(f32[32,3072]{1,0:T(8,128)} %reduce-scatter.15.cloned.1.call-done) | copy-start | bytes 1179652
  1432.6 1012.4 %copy-start.104 = (f32[32]{0:T(128)}, f32[32]{0:T(128)S(1)}, u32[]{:S(2)}) copy-start(f32[32]{0:T(128)S(1)} %get-tuple-element.178) | copy-start | bytes 388
  1803.1 580.1 %copy-start.29 = (f32[32,4096]{1,0:T(8,128)S(1)}, f32[32,4096]{1,0:T(8,128)}, u32[]{:S(2)}) copy-start(f32[32,4096]{1,0:T(8,128)} %reduce-scatter.23.cloned.1.call-done) | copy-start | bytes 1572868
  1990.2 392.1 %copy-start.30 = (f32[32,4096]{1,0:T(8,128)S(1)}, f32[32,4096]{1,0:T(8,128)}, u32[]{:S(2)}) copy-start(f32[32,4096]{1,0:T(8,128)} %reduce-scatter.19.cloned.1.call-done) | copy-start | bytes 1572868
  1992.1 452.8 %copy-start.105 = (f32[128]{0:T(128)}, f32[128]{0:T(128)S(1)}, u32[]{:S(2)}) copy-start(f32[128]{0:T(128)S(1)} %get-tuple-element.172) | copy-start | bytes 1540
  1992.7 452.2 %copy-start.107 = (f32[32]{0:T(128)}, f32[32]{0:T(128)S(1)}, u32[]{:S(2)}) copy-start(f32[32]{0:T(128)S(1)} %get-tuple-element.170) | copy-start | bytes 388
  1993.3 451.6 %copy-start.108 = (f32[32]{0:T(128)}, f32[32]{0:T(128)S(1)}, u32[]{:S(2)}) copy-start(f32[32]{0:T(128)S(1)} %get-tuple-element.174) | copy-start | bytes 388
  2247.4 197.6 %copy-start.109 = (f32[32]{0:T(128)}, f32[32]{0:T(128)S(1)}, u32[]{:S(2)}) copy-start(f32[32]{0:T(128)S(1)} %get-tuple-element.180) | copy-start | bytes 388
  2372.8 72.2 %copy-start.66 = (f32[1042]{0:T(1024)}, f32[1042]{0:T(1024)S(1)}, u32[]{:S(2)}) copy-start(f32[1042]{0:T(1024)S(1)} %fusion.71) | copy-start | bytes 12508
  2374.4 70.6 %copy-start.80 = (f32[1024]{0:T(1024)}, f32[1024]{0:T(1024)S(1)}, u32[]{:S(2)}) copy-start(f32[1024]{0:T(1024)S(1)} %get-tuple-element.213) | copy-start | bytes 12292
  2374.4 70.6 %copy-start.82 = (f32[1024]{0:T(1024)}, f32[1024]{0:T(1024)S(1)}, u32[]{:S(2)}) copy-start(f32[1024]{0:T(1024)S(1)} %get-tuple-element.214) | copy-start | bytes 12292
  2382.3 76.0 %copy-start.28 = (f32[128,1024]{1,0:T(8,128)S(1)}, f32[128,1024]{1,0:T(8,128)}, u32[]{:S(2)}) copy-start(f32[128,1024]{1,0:T(8,128)} %reduce-scatter.21.cloned.1.call-done) | copy-start | bytes 1572868
  (75 other events, 592.1 us)
Sparse Core Ops, SparseCore 0:
  11.6 60.1 all-gather.8
  75.2 95.6 all-gather.10
  174.4 67.7 all-gather.12
  245.5 54.8 all-gather.14
  303.7 76.2 all-gather.16
  383.3 76.0 all-gather.18
  462.8 76.0 all-gather.20
  887.4 132.5 reduce-scatter.26
  1027.0 102.8 reduce-scatter.24
  1132.6 140.0 reduce-scatter.16
  1279.3 151.3 reduce-scatter.14
  1433.5 182.0 reduce-scatter.20
  1618.6 184.4 reduce-scatter.22
  1805.9 184.2 reduce-scatter.18
  1998.2 247.2 reduce-scatter.12
  2252.9 119.1 all-reduce.2
where the time goes:
time: 2480 us; the launch traced here: 2470 us
  waiting for transfers between devices  1540 us (62%)
  matrix products  443 us (18%)
  other arithmetic  213 us (9%)
  blocking collectives  164 us (7%)
  local copies, waits for them, and re-layouts  79 us (3%)
  between operations  31.6 us (1%)
    reduce_scatter x1, waiting for transfers between devices, on_device(): lax.psum_scatter(ada_grad, ('fsdp', 'sub'), scatter_dimension=0, tiled=True)  252 us
    dot_general x20, matrix products, bfloat_product(): return jnp.dot(left_side, right_side, preferred_element_type=jnp.float32)  236 us
    reduce_scatter x1, waiting for transfers between devices, on_device(): lax.psum_scatter(head_grad, ('fsdp', 'sub'), scatter_dimension=0, tiled=T...  186 us
    reduce_scatter x1, waiting for transfers between devices, on_device(): lax.psum_scatter(up_grad, ('fsdp', 'sub'), scatter_dimension=0, tiled=True)  186 us
    reduce_scatter x1, waiting for transfers between devices, on_device(): lax.psum_scatter(down_grad, ('fsdp', 'sub'), scatter_dimension=0, tiled=T...  183 us
    reduce_scatter x1, waiting for transfers between devices, on_device(): lax.psum_scatter(qkv_grad, ('fsdp', 'sub'), scatter_dimension=0, tiled=True)  156 us
    reduce_scatter x1, waiting for transfers between devices, on_device(): lax.psum_scatter(out_grad, ('fsdp', 'sub'), scatter_dimension=0, tiled=True)  141 us
    unnamed x18, waiting for transfers between devices  128 us
  transfers between devices with their start and end apart: 16, of which 14 were waited for; matrix products, arithmetic and copies ran while one was open for 13% of the time, Pallas kernels for 0%

commit v1 on v0

v1 whole, which is shorter than its diff:
```python
import math
from functools import partial

import jax
import jax.numpy as jnp
from jax import lax
from jax.experimental import pallas as pl
from jax.experimental.pallas import tpu as pltpu
from jax.sharding import PartitionSpec as P

D = 1024
HEADS = 16
HEAD_DIM = 64
CLASSES = 1000
CODES = 4096
CODE_DIM = 32
LEVELS = 10
STEP = 10


TINY_SQUARE = 1e-30
SCALE_FLOOR = 0.001
STEP_RATE = 1.0
CLIP_LIMIT = 1.0
NORM_EPSILON = 1e-06
MASK_VALUE = -1000000000.0

AXES = ("fsdp", "sub")
MESH = pl.DeviceIdType.MESH
ANY = pl.BlockSpec(memory_space=pl.ANY)
WHOLE = pl.BlockSpec(memory_space=pltpu.VMEM)
FIVE = (2, 2, 2, 2, 2)
DIMS = ("w", "u", "y", "x", "c")
SCATTER_ORDERS = (("c", "x", "y", "w", "u"), ("c", "y", "x", "w", "u"))
GATHER_ORDERS = (("u", "w", "y", "x", "c"), ("u", "w", "x", "y", "c"))
SCORE_SCALE = HEAD_DIM ** (-0.5)
EXP_SCALE = SCORE_SCALE * math.log2(math.e)
VMEM_GRANT = 58 * 1024 * 1024


def bfloat_product(left_side, right_side):
    return jnp.dot(left_side, right_side, preferred_element_type=jnp.float32)


class Place:
    def __init__(self):
        fsdp, sub = lax.axis_index("fsdp"), lax.axis_index("sub")
        self.bit = {
            "c": lax.rem(sub, 2),
            "x": lax.div(sub, 2),
            "y": lax.rem(fsdp, 2),
            "u": lax.rem(lax.div(fsdp, 2), 2),
            "w": lax.div(fsdp, 4),
        }
        bit = self.bit
        self.partner = {
            "c": (fsdp, sub + 1 - 2 * bit["c"]),
            "x": (fsdp, sub + 2 - 4 * bit["x"]),
            "y": (fsdp + 1 - 2 * bit["y"], sub),
            "u": (fsdp + 2 - 4 * bit["u"], sub),
            "w": (fsdp + 4 - 8 * bit["w"], sub),
        }

    def meet(self):
        barrier = pltpu.get_barrier_semaphore()
        for dim in DIMS:
            pl.semaphore_signal(
                barrier, inc=1, device_id=self.partner[dim], device_id_type=MESH
            )
        pl.semaphore_wait(barrier, 5)

    def send(self, src, dst, send_sem, recv_sem, dim):
        return pltpu.make_async_remote_copy(
            src_ref=src,
            dst_ref=dst,
            send_sem=send_sem,
            recv_sem=recv_sem,
            device_id=self.partner[dim],
            device_id_type=MESH,
        )


def when_in(index, low, high, body):
    if isinstance(index, int):
        if low <= index < high:
            body()
    else:
        pl.when((index >= low) & (index < high))(body)


class Gather:
    def __init__(self, place, groups, sends, recvs, local_sems):
        self.place, self.groups = place, groups
        self.sends, self.recvs, self.local_sems = sends, recvs, local_sems

    @staticmethod
    def scratch():
        dma = pltpu.SemaphoreType.DMA
        return [dma((5, 2, 2)), dma((5, 2, 2)), dma((2, 2))]

    def region(self, stage, parity):
        done = GATHER_ORDERS[parity][:stage]
        return tuple(slice(None) if d in done else self.place.bit[d] for d in DIMS)

    def copy(self, group, j, stage, parity, slot):
        _, _, own, full = group
        ref = full(j, parity, self.region(stage, parity))
        return self.place.send(
            own(j, parity) if stage == 0 else ref,
            ref,
            self.sends.at[stage, parity, slot],
            self.recvs.at[stage, parity, slot],
            GATHER_ORDERS[parity][stage],
        )

    def local(self, group, j, parity, slot):
        _, _, own, full = group
        return pltpu.make_async_copy(
            own(j, parity), full(j, parity, self.region(0, parity)), self.local_sems.at[parity, slot]
        )

    def step(self, t):
        for stage in reversed(range(6)):
            j = t - stage
            for group in self.groups:

                def body(group=group, stage=stage, j=j):
                    slot = lax.rem(j, 2)
                    for parity in range(2):
                        if stage == 0:
                            self.local(group, j, parity, slot).start()
                        if stage == 1:
                            self.local(group, j, parity, slot).wait()
                        if stage >= 1:
                            self.copy(group, j, stage - 1, parity, slot).wait()
                        if stage < 5:
                            self.copy(group, j, stage, parity, slot).start()

                when_in(j, group[0], group[1], body)


class Scatter:
    def __init__(self, place, groups, store, scratch):
        self.place, self.groups, self.store = place, groups, store
        self.keep = scratch[0]
        self.land = scratch[1:6]
        self.sums = (None,) + tuple(scratch[6:10])
        self.sends, self.recvs, self.keep_sems = scratch[10:13]
        self.first, self.end = groups[0][0], groups[-1][1]

    @staticmethod
    def scratch(piece, kind):
        dma = pltpu.SemaphoreType.DMA
        return (
            [pltpu.VMEM((2,) + (2,) * 4 + piece, kind)]
            + [pltpu.VMEM((2, 2) + (2,) * (4 - k) + piece, kind) for k in range(5)]
            + [pltpu.VMEM((2,) + (2,) * (5 - k) + piece, kind) for k in range(1, 5)]
            + [dma((5, 2, 2)), dma((5, 2, 2)), dma((2,))]
        )

    def half(self, stage, parity, other):
        order = SCATTER_ORDERS[parity]
        left = [d for d in DIMS if d not in order[:stage]]
        bit = self.place.bit[order[stage]]
        value = 1 - bit if other else bit
        return (parity,) + tuple(value if d == order[stage] else slice(None) for d in left)

    def copy(self, stage, parity, slot, source=None):
        if source is None:
            if stage == 0:
                source = self.keep.at[parity]
            else:
                source = self.sums[stage].at[self.half(stage, parity, True)]
        return self.place.send(
            source,
            self.land[stage].at[slot, parity],
            self.sends.at[stage, parity, slot],
            self.recvs.at[stage, parity, slot],
            SCATTER_ORDERS[parity][stage],
        )

    def step(self, t):
        for stage in reversed(range(6)):
            j = t - stage

            def body(stage=stage, j=j):
                slot = lax.rem(j, 2)
                for parity in range(2):
                    if stage >= 1:
                        before = stage - 1
                        if before == 0:
                            pltpu.make_async_copy(
                                self.keep.at[parity], self.keep.at[parity], self.keep_sems.at[parity]
                            ).wait()
                        self.copy(before, parity, slot).wait()
                        if before == 0:
                            mine = self.keep[parity]
                        else:
                            mine = self.sums[before][self.half(before, parity, False)]
                        total = mine.astype(jnp.float32) + self.land[before][slot, parity].astype(
                            jnp.float32
                        )
                        if stage < 5:
                            self.sums[stage][parity] = total.astype(self.keep.dtype)
                        else:
                            self.store(j, parity, total)
                    if 1 <= stage < 5:
                        self.copy(stage, parity, slot).start()

            if stage == 0:
                for low, high, source in self.groups:

                    def begin(source=source, j=j):
                        slot = lax.rem(j, 2)
                        core = self.place.bit["c"]
                        for parity in range(2):
                            self.copy(0, parity, slot, source(j, parity, 1 - core)).start()
                            pltpu.make_async_copy(
                                source(j, parity, core), self.keep.at[parity], self.keep_sems.at[parity]
                            ).start()

                    when_in(j, low, high, begin)
            else:
                when_in(j, self.first, self.end, body)


def params(collective_id, **more):
    return pltpu.CompilerParams(
        collective_id=collective_id, has_side_effects=True, vmem_limit_bytes=VMEM_GRANT, **more
    )


def columns(start, size):
    return pl.ds(pl.multiple_of(start, 128), size)


def small_gather_kernel(rows_ref, tags_ref, rows_full, tags_full, *sems):
    place = Place()
    place.meet()
    gather = Gather(
        place,
        [(0, 1, lambda j, p: (rows_ref, tags_ref)[p], lambda j, p, r: (rows_full, tags_full)[p].at[r])],
        *sems,
    )
    for t in range(6):
        gather.step(t)


def small_gather(rows, tags):
    return pl.pallas_call(
        small_gather_kernel,
        out_shape=(
            jax.ShapeDtypeStruct(FIVE + rows.shape, rows.dtype),
            jax.ShapeDtypeStruct(FIVE + tags.shape, tags.dtype),
        ),
        in_specs=[WHOLE, WHOLE],
        out_specs=(WHOLE, WHOLE),
        scratch_shapes=Gather.scratch(),
        compiler_params=params(0),
        name="small_gather",
    )(rows, tags)


def first_kernel(part_ref, own_ref, mod_ref, full_ref, *scratch):
    place = Place()
    place.meet()
    rows = part_ref.shape[5] // 2
    width = 256

    def store(j, parity, total):
        mod_ref[pl.ds(parity * rows, rows)] = total

    scatter = Scatter(
        place,
        [(0, 1, lambda j, p, core: part_ref.at[:, :, :, :, core, pl.ds(p * rows, rows)])],
        store,
        scratch[:13],
    )
    pairs = own_ref.shape[1] // (2 * width)
    gather = Gather(
        place,
        [
            (
                0,
                pairs,
                lambda j, p: own_ref.at[:, columns((2 * j + p) * width, width)],
                lambda j, p, r: full_ref.at[r + (slice(None), columns((2 * j + p) * width, width))],
            )
        ],
        *scratch[13:],
    )
    for t in range(pairs + 5):
        scatter.step(t)
        gather.step(t)


def first_exchange(part, own):
    return pl.pallas_call(
        first_kernel,
        out_shape=(
            jax.ShapeDtypeStruct(part.shape[5:], jnp.float32),
            jax.ShapeDtypeStruct(FIVE + own.shape, own.dtype),
        ),
        in_specs=[ANY, ANY],
        out_specs=(WHOLE, ANY),
        scratch_shapes=Scatter.scratch((part.shape[5] // 2, 128), jnp.float32) + Gather.scratch(),
        compiler_params=params(1),
        name="modulation_scatter_qkv_gather",
    )(part, own)


def head_mean(values):
    low_lane = lax.broadcasted_iota(jnp.int32, values.shape, 1) < HEAD_DIM
    low_sum = jnp.sum(jnp.where(low_lane, values, 0.0), axis=1, keepdims=True)
    high_sum = jnp.sum(jnp.where(low_lane, 0.0, values), axis=1, keepdims=True)
    return jnp.where(low_lane, low_sum, high_sum) * (1.0 / HEAD_DIM)


def of_head(values, head):
    low_lane = lax.broadcasted_iota(jnp.int32, values.shape, 1) < HEAD_DIM
    zero = jnp.zeros_like(values)
    return jnp.where(low_lane, values, zero) if head == 0 else jnp.where(low_lane, zero, values)


def dot_last(left, right):
    return lax.dot_general(left, right, (((1,), (1,)), ((), ())), preferred_element_type=jnp.float32)


def dot_first(left, right):
    return lax.dot_general(left, right, (((0,), (0,)), ((), ())), preferred_element_type=jnp.float32)


def dot_plain(left, right):
    return lax.dot_general(left, right, (((1,), (0,)), ((), ())), preferred_element_type=jnp.float32)


UNITS = 4


def normed_head(raw, gain):
    return (raw * lax.rsqrt(head_mean(raw * raw) + NORM_EPSILON) * gain).astype(jnp.bfloat16)


def attend_kernel(linked, q_ref, k_ref, v_ref, gain_ref, bias_ref, *refs):
    if linked:
        out_own, down_own, mixed_ref, out_full, down_full, qn, kn, vn = refs[:8]
        sems = refs[8:]
        place = Place()
        width = 128
        split = out_own.shape[1] // (2 * width)
        depth = out_own.shape[0]
        parts = down_own.shape[0] // depth

        def spread(j):
            return lax.div(j - split, split), lax.rem(j - split, split)

        def down_source(j, p):
            part, column = spread(j)
            return down_own.at[
                pl.ds(pl.multiple_of(part * depth, depth), depth), columns((2 * column + p) * width, width)
            ]

        def down_target(j, p, r):
            part, column = spread(j)
            return down_full.at[r + (part, slice(None), columns((2 * column + p) * width, width))]

        gather = Gather(
            place,
            [
                (
                    0,
                    split,
                    lambda j, p: out_own.at[:, columns((2 * j + p) * width, width)],
                    lambda j, p, r: out_full.at[r + (slice(None), columns((2 * j + p) * width, width))],
                ),
                (split, split + split * parts, down_source, down_target),
            ],
            *sems,
        )
        assert split + split * parts + 5 <= UNITS * (HEADS // 2)
        pl.when(pl.program_id(0) == 0)(place.meet)
    else:
        mixed_ref, qn, kn, vn = refs
    qn[...] = normed_head(q_ref[...], gain_ref[0:1])
    kn[...] = normed_head(k_ref[...], gain_ref[1:2])
    vn[...] = v_ref[...].astype(jnp.bfloat16)
    size = q_ref.shape[0] // UNITS

    @pl.loop(0, UNITS)
    def unit(u):
        if linked:
            gather.step(pl.program_id(0) * UNITS + u)
        rows = pl.ds(pl.multiple_of(u * size, size), size)
        both = []
        for head in range(2):
            scores = dot_last(of_head(qn[rows], head), kn[...]) * EXP_SCALE + bias_ref[rows]
            raised = jnp.exp2(scores)
            share = 1.0 / jnp.sum(raised, axis=1, keepdims=True)
            both.append(dot_plain((raised * share).astype(jnp.bfloat16), vn[...]))
        low_lane = lax.broadcasted_iota(jnp.int32, both[0].shape, 1) < HEAD_DIM
        mixed_ref[rows] = jnp.where(low_lane, both[0], both[1]).astype(jnp.bfloat16)


def attend(projected, gains, bias, out_own=None, down_own=None):
    tokens = projected.shape[0]
    pair = pl.BlockSpec((tokens, 128), lambda i: (0, i))
    specs = [
        pair,
        pl.BlockSpec((tokens, 128), lambda i: (0, i + 8)),
        pl.BlockSpec((tokens, 128), lambda i: (0, i + 16)),
        pl.BlockSpec((8, 128), lambda i: (0, i)),
        pl.BlockSpec((tokens, tokens), lambda i: (0, 0), pipeline_mode=pl.Buffered(1)),
    ]
    outs = [jax.ShapeDtypeStruct((tokens, D), jnp.bfloat16)]
    out_specs = [pair]
    scratch = [pltpu.VMEM((tokens, 128), jnp.bfloat16)] * 3
    operands = [projected, projected, projected, gains, bias]
    linked = out_own is not None
    if linked:
        depth = out_own.shape[0]
        specs += [ANY, ANY]
        operands += [out_own, down_own]
        outs += [
            jax.ShapeDtypeStruct(FIVE + out_own.shape, jnp.bfloat16),
            jax.ShapeDtypeStruct(FIVE + (down_own.shape[0] // depth, depth, D), jnp.bfloat16),
        ]
        out_specs += [ANY, ANY]
        scratch = scratch + Gather.scratch()
    return pl.pallas_call(
        partial(attend_kernel, linked),
        grid=(HEADS // 2,),
        out_shape=tuple(outs),
        in_specs=specs,
        out_specs=tuple(out_specs),
        scratch_shapes=scratch,
        compiler_params=params(2) if linked else pltpu.CompilerParams(vmem_limit_bytes=VMEM_GRANT),
        name="attention_forward",
    )(*operands)


def attend_back_kernel(linked, q_ref, k_ref, v_ref, m_ref, gain_ref, bias_ref, *refs):
    if linked:
        head_ref, up_ref, down_ref, grad_ref, gain_grad_ref, done_ref = refs[:6]
        qn, kn, vn, dq, dk, dv = refs[6:12]
        place = Place()
        width = 256
        wide = up_ref.shape[6] // (2 * width)
        narrow = down_ref.shape[7] // (2 * width)
        parts = down_ref.shape[5]

        def columns_of(ref, first):
            return lambda j, p, core: ref.at[
                :, :, :, :, core, :, columns((2 * (j - first) + p) * width, width)
            ]

        def down_source(j, p, core):
            spread = j - 2 * wide
            part, column = lax.div(spread, narrow), lax.rem(spread, narrow)
            return down_ref.at[:, :, :, :, core, part, :, columns((2 * column + p) * width, width)]

        def store(j, parity, total):
            done_ref[j, :, parity * width : (parity + 1) * width] = total

        pairs = 2 * wide + parts * narrow
        scatter = Scatter(
            place,
            [
                (0, wide, columns_of(head_ref, 0)),
                (wide, 2 * wide, columns_of(up_ref, wide)),
                (2 * wide, pairs, down_source),
            ],
            store,
            refs[12:],
        )
        assert pairs + 5 <= UNITS * (HEADS // 2)
        pl.when(pl.program_id(0) == 0)(place.meet)
    else:
        grad_ref, gain_grad_ref = refs[:2]
        qn, kn, vn, dq, dk, dv = refs[2:]
    qn[...] = normed_head(q_ref[...], gain_ref[0:1])
    kn[...] = normed_head(k_ref[...], gain_ref[1:2])
    vn[...] = v_ref[...].astype(jnp.bfloat16)
    dk[...] = jnp.zeros_like(dk)
    dv[...] = jnp.zeros_like(dv)
    size = q_ref.shape[0] // UNITS

    @pl.loop(0, UNITS)
    def unit(u):
        if linked:
            scatter.step(pl.program_id(0) * UNITS + u)
        rows = pl.ds(pl.multiple_of(u * size, size), size)
        query_sum = None
        for head in range(2):
            query = of_head(qn[rows], head)
            mixed = of_head(m_ref[rows], head)
            raised = jnp.exp2(dot_last(kn[...], query) * EXP_SCALE + bias_ref[:, rows])
            probs = raised * (1.0 / jnp.sum(raised, axis=0, keepdims=True))
            prob_grad = dot_last(vn[...], mixed)
            center = jnp.sum(probs * prob_grad, axis=0, keepdims=True)
            score_grad = (probs * (prob_grad - center)).astype(jnp.bfloat16)
            dk[...] += dot_plain(score_grad, query)
            dv[...] += dot_plain(probs.astype(jnp.bfloat16), mixed)
            part = dot_first(score_grad, of_head(kn[...], head))
            query_sum = part if query_sum is None else query_sum + part
        dq[rows] = query_sum

    gain_rows = []
    for place_at, raw_ref, grad in ((0, q_ref, dq), (1, k_ref, dk)):
        raw = raw_ref[...]
        normed_grad = grad[...] * SCORE_SCALE
        rate = lax.rsqrt(head_mean(raw * raw) + NORM_EPSILON)
        scaled = gain_ref[place_at : place_at + 1] * normed_grad
        back = rate * scaled - raw * (rate * rate * rate) * head_mean(raw * scaled)
        grad_ref[place_at] = back.astype(jnp.bfloat16)
        gain_rows.append(jnp.sum(normed_grad * raw * rate, axis=0, keepdims=True))
    grad_ref[2] = dv[...].astype(jnp.bfloat16)
    gain_grad_ref[...] = jnp.concatenate(gain_rows + [jnp.zeros((6, 128), jnp.float32)], axis=0)


def attend_back(projected, mixed_grad, gains, bias, head_grad=None, up_grad=None, down_grad=None):
    tokens = projected.shape[0]
    pair = pl.BlockSpec((tokens, 128), lambda i: (0, i))
    specs = [
        pair,
        pl.BlockSpec((tokens, 128), lambda i: (0, i + 8)),
        pl.BlockSpec((tokens, 128), lambda i: (0, i + 16)),
        pair,
        pl.BlockSpec((8, 128), lambda i: (0, i)),
        pl.BlockSpec((tokens, tokens), lambda i: (0, 0), pipeline_mode=pl.Buffered(1)),
    ]
    outs = [
        jax.ShapeDtypeStruct((3, tokens, D), jnp.bfloat16),
        jax.ShapeDtypeStruct((8, D), jnp.float32),
    ]
    out_specs = [
        pl.BlockSpec((3, tokens, 128), lambda i: (0, 0, i)),
        pl.BlockSpec((8, 128), lambda i: (0, i)),
    ]
    scratch = [pltpu.VMEM((tokens, 128), jnp.bfloat16)] * 3 + [
        pltpu.VMEM((tokens, 128), jnp.float32)
    ] * 3
    operands = [projected, projected, projected, mixed_grad, gains, bias]
    linked = head_grad is not None
    if linked:
        depth = head_grad.shape[5]
        specs += [ANY, ANY, ANY]
        operands += [head_grad, up_grad, down_grad]
        pairs = (head_grad.shape[6] + up_grad.shape[6] + down_grad.shape[5] * down_grad.shape[7]) // 512
        outs += [jax.ShapeDtypeStruct((pairs, depth, 512), jnp.float32)]
        out_specs += [WHOLE]
        scratch = scratch + Scatter.scratch((depth, 256), jnp.bfloat16)
    return pl.pallas_call(
        partial(attend_back_kernel, linked),
        grid=(HEADS // 2,),
        out_shape=tuple(outs),
        in_specs=specs,
        out_specs=tuple(out_specs),
        scratch_shapes=scratch,
        compiler_params=params(3) if linked else pltpu.CompilerParams(vmem_limit_bytes=VMEM_GRANT),
        name="attention_backward",
    )(*operands)


def last_kernel(qkv_ref, out_ref, small_ref, mod_ref, done_ref, small_done, mod_full, *scratch):
    place = Place()
    place.meet()
    width = 256
    wide = qkv_ref.shape[6] // (2 * width)
    narrow = out_ref.shape[6] // (2 * width)

    def columns_of(ref, first):
        return lambda j, p, core: ref.at[
            :, :, :, :, core, :, columns((2 * (j - first) + p) * width, width)
        ]

    def store(j, parity, total):
        done_ref[j, :, parity * width : (parity + 1) * width] = total

    pairs = wide + narrow
    scatter = Scatter(
        place,
        [(0, wide, columns_of(qkv_ref, 0)), (wide, pairs, columns_of(out_ref, wide))],
        store,
        scratch[:13],
    )
    half = small_ref.shape[5] // 2

    def small_store(j, parity, total):
        small_done[pl.ds(parity * half, half)] = total

    small = Scatter(
        place,
        [(0, 1, lambda j, p, core: small_ref.at[:, :, :, :, core, pl.ds(p * half, half)])],
        small_store,
        scratch[13:26],
    )
    rows = mod_ref.shape[0] // 2
    gather = Gather(
        place,
        [
            (
                0,
                1,
                lambda j, p: mod_ref.at[pl.ds(p * rows, rows)],
                lambda j, p, r: mod_full.at[r + (pl.ds(p * rows, rows),)],
            )
        ],
        *scratch[26:],
    )
    for t in range(6):
        gather.step(t)
        small.step(t)
        scatter.step(t)

    @pl.loop(6, pairs + 5)
    def later(t):
        scatter.step(t)


def last_exchange(qkv_grad, out_grad, small, modulation):
    depth = qkv_grad.shape[5]
    pairs = (qkv_grad.shape[6] + out_grad.shape[6]) // 512
    return pl.pallas_call(
        last_kernel,
        out_shape=(
            jax.ShapeDtypeStruct((pairs, depth, 512), jnp.float32),
            jax.ShapeDtypeStruct(small.shape[5:], jnp.float32),
            jax.ShapeDtypeStruct(FIVE + modulation.shape, modulation.dtype),
        ),
        in_specs=[ANY, ANY, ANY, ANY],
        out_specs=(WHOLE, WHOLE, ANY),
        scratch_shapes=Scatter.scratch((depth, 256), jnp.bfloat16)
        + Scatter.scratch((small.shape[5] // 2, 128), jnp.float32)
        + Gather.scratch(),
        compiler_params=params(4),
        name="last_scatter",
    )(qkv_grad, out_grad, small, modulation)


def total_kernel(in_ref, out_ref, sums, land, sends, recvs):
    place = Place()
    place.meet()
    sums[0] = in_ref[...]
    for stage, dim in enumerate(DIMS):
        copy = place.send(
            sums.at[stage], land.at[stage], sends.at[stage], recvs.at[stage], dim
        )
        copy.start()
        copy.wait()
        sums[stage + 1] = sums[stage] + land[stage]
    out_ref[...] = sums[5]


def total(values, collective_id):
    if not linked_mesh():
        return lax.psum(values, AXES)
    size = values.shape[0]
    rows = -(-size // 1024) * 8
    flat = jnp.pad(values, (0, rows * 128 - size)).reshape(rows, 128)
    summed = pl.pallas_call(
        total_kernel,
        out_shape=jax.ShapeDtypeStruct(flat.shape, jnp.float32),
        in_specs=[WHOLE],
        out_specs=WHOLE,
        scratch_shapes=[
            pltpu.VMEM((6, rows, 128), jnp.float32),
            pltpu.VMEM((5, rows, 128), jnp.float32),
            pltpu.SemaphoreType.DMA((5,)),
            pltpu.SemaphoreType.DMA((5,)),
        ],
        compiler_params=params(collective_id),
        name="total",
    )(flat)
    return summed.reshape(-1)[:size]


def linked_mesh():
    return lax.axis_size("fsdp") == 8 and lax.axis_size("sub") == 4


def gathered(values):
    return lax.all_gather(values, AXES, axis=0, tiled=True)


def scattered(values):
    return lax.psum_scatter(values, AXES, scatter_dimension=0, tiled=True)


def layer_norm(values):
    center = values - jnp.mean(values, axis=-1, keepdims=True)
    return center * lax.rsqrt(jnp.mean(center * center, axis=-1, keepdims=True) + NORM_EPSILON)


def modulate(values, scale_part, shift_part):
    return layer_norm(values) * (1.0 + scale_part) + shift_part


def final_norm(values, gain_vector):
    return layer_norm(values) * gain_vector


def attention_bias(scale_query, segment_query, scale_key, segment_key, real_key, same):
    usable = (segment_query == segment_key) & (scale_key <= scale_query) & ((real_key == 1) | same)
    return jnp.where(usable, 0.0, MASK_VALUE)


def split_product(left_side, right_low):
    high = left_side.astype(jnp.bfloat16)
    rest = (left_side - high.astype(jnp.float32)).astype(jnp.bfloat16)
    return bfloat_product(high, right_low) + bfloat_product(rest, right_low)


def on_device(
    code_vectors,
    scale_ids,
    segment_ids,
    real_mask,
    labels,
    targets,
    loss_weight,
    tables,
    vectors,
    ada_weight,
    qkv_weight,
    out_weight,
    up_weight,
    down_weight,
    head_weight,
    tables_moment,
    ada_moment,
    qkv_moment,
    out_moment,
    up_moment,
    down_moment,
    head_moment,
    vector_moment,
    column_moment,
):
    devices = lax.axis_size(AXES)
    linked = linked_mesh()
    depth = tables.shape[0]
    tokens = code_vectors.shape[0]
    masters = (
        tables,
        vectors,
        ada_weight,
        qkv_weight,
        out_weight,
        up_weight,
        down_weight,
        head_weight,
    )
    local_count = jnp.sum(loss_weight).astype(jnp.float32)
    local_squares = jnp.stack([jnp.sum(master * master) for master in masters])
    low = jnp.bfloat16
    part_kind = low if linked else jnp.float32
    tables_low = tables.astype(low)
    ada_low = ada_weight.astype(low)
    qkv_low = qkv_weight.astype(low)
    out_low = out_weight.astype(low)
    down_low = down_weight.astype(low)

    small_rows = jnp.concatenate(
        [
            tables_low[:, CLASSES:],
            vectors.astype(low),
            jnp.zeros((depth, 128 - CODE_DIM - LEVELS - 9), low),
        ],
        axis=1,
    )
    tags = jnp.zeros((8, 128), jnp.float32)
    tags = tags.at[0, :2].set(labels.astype(jnp.float32)).at[0, 2].set(local_count)
    if linked:
        small_full, tags_full = small_gather(small_rows, tags)
    else:
        small_full, tags_full = gathered(small_rows), gathered(tags)
    full_up = gathered(up_weight.astype(low))
    full_head = gathered(head_weight.astype(low))
    small_full = small_full.reshape(D, 128)
    tags_full = tags_full.reshape(devices, 8, 128)[:, 0]
    labels_all = tags_full[:, :2].reshape(2 * devices)
    weight_total = jnp.sum(tags_full[:, 2])
    code_tables = small_full[:, : CODE_DIM + LEVELS]
    gain_vector = small_full[:, CODE_DIM + LEVELS : CODE_DIM + LEVELS + 9].astype(jnp.float32)

    label_hot = (labels_all[:, None] == jnp.arange(CLASSES, dtype=jnp.float32)[None, :]).astype(low)
    class_cond = bfloat_product(label_hot, tables_low[:, :CLASSES].T)
    activated = jax.nn.silu(class_cond).astype(low)
    modulation_part = bfloat_product(activated, ada_low)
    if linked:
        own_modulation, full_qkv = first_exchange(
            modulation_part.reshape(FIVE + (12 * D // 128, 128)), qkv_low
        )
        own_modulation = own_modulation.reshape(2, 6 * D)
        full_qkv = full_qkv.reshape(D, 3 * D)
    else:
        own_modulation, full_qkv = scattered(modulation_part), gathered(qkv_low)
    modulation = own_modulation + gain_vector[:, :6].T.reshape(1, 6 * D)
    second = (segment_ids == 1)[:, None]

    def of_token(block):
        piece = modulation[:, block * D : (block + 1) * D]
        return jnp.where(second, piece[1:2], piece[0:1])

    gamma_one, gamma_two, scale_one, scale_two, shift_one, shift_two = (
        of_token(block) for block in range(6)
    )

    level_hot = (scale_ids[:, None] == jnp.arange(LEVELS)[None, :]).astype(low)
    code_levels = jnp.concatenate([code_vectors, level_hot], axis=1)
    embedded = bfloat_product(code_levels, code_tables.T)
    normed = modulate(embedded, scale_one, shift_one).astype(low)
    projected = bfloat_product(normed, full_qkv)
    gains = jnp.pad(gain_vector[:, 6:8].T, ((0, 6), (0, 0)))
    places = jnp.arange(tokens)
    same = places[:, None] == places[None, :]
    bias = attention_bias(
        scale_ids[:, None], segment_ids[:, None], scale_ids[None, :], segment_ids[None, :], real_mask[None, :], same
    )
    if linked:
        mixed_heads, full_out, full_down = attend(projected, gains, bias, out_low, down_low)
        full_out = full_out.reshape(D, D)
        full_down = full_down.reshape(-1, D)
    else:
        (mixed_heads,) = attend(projected, gains, bias)
        full_out, full_down = gathered(out_low), gathered(down_low)
    attended = bfloat_product(mixed_heads, full_out)
    residual_one = embedded + gamma_one * attended
    normed_two = modulate(residual_one, scale_two, shift_two).astype(low)
    hidden_pre = bfloat_product(normed_two, full_up)
    hidden_act = jax.nn.gelu(hidden_pre, approximate=True).astype(low)
    branch = bfloat_product(hidden_act, full_down)
    residual_two = residual_one + gamma_two * branch
    final_normed = final_norm(residual_two, gain_vector[:, 8]).astype(low)
    logits = bfloat_product(final_normed, full_head)
    logit_peak = jnp.max(logits, axis=-1, keepdims=True)
    log_total = logit_peak + jnp.log(jnp.sum(jnp.exp(logits - logit_peak), axis=-1, keepdims=True))
    target_hot = targets[:, None] == jnp.arange(CODES)[None, :]
    picked = jnp.sum(jnp.where(target_hot, logits, 0.0), axis=-1, keepdims=True)
    weight_column = loss_weight.astype(jnp.float32)[:, None]
    local_loss = jnp.sum(weight_column * (log_total - picked))
    logit_grad = (
        (jnp.exp(logits - log_total) - target_hot.astype(jnp.float32))
        * (weight_column / weight_total)
    ).astype(low)

    head_part = bfloat_product(final_normed.T, logit_grad).astype(part_kind)
    final_grad = bfloat_product(logit_grad, full_head.T)
    _, final_back = jax.vjp(final_norm, residual_two, gain_vector[:, 8])
    residual_grad, head_gain_grad = final_back(final_grad)
    branch_grad = (gamma_two * residual_grad).astype(low)

    def slot_sums(token_grad):
        other = jnp.sum(jnp.where(second, token_grad, 0.0), axis=0)
        first = jnp.sum(jnp.where(second, 0.0, token_grad), axis=0)
        return jnp.stack([first, other])

    gamma_two_grad = slot_sums(residual_grad * branch)
    down_part = bfloat_product(hidden_act.T, branch_grad).astype(part_kind)
    act_grad = bfloat_product(branch_grad, full_down.T)
    _, gelu_back = jax.vjp(partial(jax.nn.gelu, approximate=True), hidden_pre)
    pre_grad = gelu_back(act_grad)[0].astype(low)
    up_part = bfloat_product(normed_two.T, pre_grad).astype(part_kind)
    normed_two_grad = bfloat_product(pre_grad, full_up.T)
    _, modulate_two_back = jax.vjp(modulate, residual_one, scale_two, shift_two)
    norm_grad, scale_two_grad, shift_two_grad = modulate_two_back(normed_two_grad)
    scale_two_grad, shift_two_grad = slot_sums(scale_two_grad), slot_sums(shift_two_grad)
    residual_grad = residual_grad + norm_grad
    attended_grad = (gamma_one * residual_grad).astype(low)
    gamma_one_grad = slot_sums(residual_grad * attended)
    out_part = bfloat_product(mixed_heads.T, attended_grad).astype(part_kind)
    mixed_grad = bfloat_product(attended_grad, full_out.T).astype(low)
    turned_bias = attention_bias(
        scale_ids[None, :], segment_ids[None, :], scale_ids[:, None], segment_ids[:, None], real_mask[:, None], same
    )
    if linked:
        heads_grad, gain_grads, done = attend_back(
            projected,
            mixed_grad,
            gains,
            turned_bias,
            head_part.reshape(FIVE + (depth, CODES)),
            up_part.reshape(FIVE + (depth, up_part.shape[1])),
            down_part.reshape(FIVE + (down_part.shape[0] // D, depth, D)),
        )
        wide = CODES // 512
        wide_up = wide + up_part.shape[1] // 512
        head_grad = done[:wide].transpose(1, 0, 2).reshape(depth, CODES)
        up_grad = done[wide:wide_up].transpose(1, 0, 2).reshape(depth, -1)
        down_grad = done[wide_up:].reshape(-1, 2, depth, 512).transpose(0, 2, 1, 3).reshape(-1, D)
    else:
        heads_grad, gain_grads = attend_back(projected, mixed_grad, gains, turned_bias)
        head_grad, up_grad, down_grad = scattered(head_part), scattered(up_part), scattered(down_part)
    qkv_part = jnp.concatenate(
        [bfloat_product(normed.T, heads_grad[part]).astype(part_kind) for part in range(3)], axis=1
    )
    normed_grad = sum(
        bfloat_product(heads_grad[part], full_qkv[:, part * D : (part + 1) * D].T) for part in range(3)
    )
    _, modulate_one_back = jax.vjp(modulate, embedded, scale_one, shift_one)
    norm_grad, scale_one_grad, shift_one_grad = modulate_one_back(normed_grad)
    scale_one_grad, shift_one_grad = slot_sums(scale_one_grad), slot_sums(shift_one_grad)
    embedded_grad = residual_grad + norm_grad
    modulation_grad = jnp.concatenate(
        [
            gamma_one_grad,
            gamma_two_grad,
            scale_one_grad,
            scale_two_grad,
            shift_one_grad,
            shift_two_grad,
        ],
        axis=1,
    )
    bias_grad = jnp.sum(modulation_grad, axis=0).reshape(6, D)
    code_grad = split_product(embedded_grad.T, code_levels)
    small_part = jnp.concatenate(
        [
            code_grad,
            bias_grad.T,
            gain_grads[:2].T,
            head_gain_grad[:, None],
            jnp.zeros((D, 128 - CODE_DIM - LEVELS - 9), jnp.float32),
        ],
        axis=1,
    )
    modulation_low = modulation_grad.astype(low)
    if linked:
        done, small_grad, modulation_all = last_exchange(
            qkv_part.reshape(FIVE + (depth, 3 * D)),
            out_part.reshape(FIVE + (depth, D)),
            small_part.reshape(FIVE + (depth, 128)),
            modulation_low.reshape(12 * D // 128, 128),
        )
        modulation_all = modulation_all.reshape(2 * devices, 6 * D)
        wide = 3 * D // 512
        qkv_grad = done[:wide].transpose(1, 0, 2).reshape(depth, 3 * D)
        out_grad = done[wide:].transpose(1, 0, 2).reshape(depth, D)
    else:
        modulation_all = gathered(modulation_low)
        small_grad, qkv_grad, out_grad = scattered(small_part), scattered(qkv_part), scattered(out_part)
    ada_grad = bfloat_product(activated.T, modulation_all)
    activated_grad = bfloat_product(modulation_all, ada_low.T)
    _, silu_back = jax.vjp(jax.nn.silu, class_cond)
    cond_grad = silu_back(activated_grad)[0]
    class_grad = jnp.dot(
        cond_grad.T,
        label_hot.astype(jnp.float32),
        precision=lax.Precision.HIGHEST,
        preferred_element_type=jnp.float32,
    )
    tables_grad = jnp.concatenate([class_grad, small_grad[:, : CODE_DIM + LEVELS]], axis=1)
    vectors_grad = small_grad[:, CODE_DIM + LEVELS : CODE_DIM + LEVELS + 9]
    gradients = (
        tables_grad,
        vectors_grad,
        ada_grad,
        qkv_grad,
        out_grad,
        up_grad,
        down_grad,
        head_grad,
    )
    second_decay = 1.0 - STEP ** (-0.8)
    factored_index = (0, 2, 3, 4, 5, 6, 7)
    factored_moments = (
        tables_moment,
        ada_moment,
        qkv_moment,
        out_moment,
        up_moment,
        down_moment,
        head_moment,
    )
    rows_list = []
    column_parts = []
    row_parts = []
    for position, moment in zip(factored_index, factored_moments):
        gradient = gradients[position]
        squared = gradient * gradient + TINY_SQUARE
        rows_new = second_decay * moment + (1.0 - second_decay) * jnp.mean(squared, axis=1)
        rows_list.append(rows_new)
        column_parts.append(jnp.sum(squared, axis=0))
        row_parts.append(jnp.sum(rows_new))
    column_count = column_moment.shape[0]
    sums = total(
        jnp.concatenate(column_parts + [jnp.stack(row_parts), local_squares, local_loss[None]]), 5
    )
    column_total = sums[:column_count]
    row_total = sums[column_count : column_count + 7]
    weight_squares = sums[column_count + 7 : column_count + 15]
    loss_sum = sums[column_count + 15]
    updates = [None] * 8
    moments_new = [None] * 8
    column_new = []
    offset = 0
    for factor_slot, position in enumerate(factored_index):
        gradient = gradients[position]
        rows_all = gradient.shape[0] * devices
        column_count = gradient.shape[1]
        cols_new = second_decay * column_moment[offset : offset + column_count] + (
            1.0 - second_decay
        ) * (column_total[offset : offset + column_count] / rows_all)
        offset += column_count
        estimate = (
            rows_list[factor_slot][:, None]
            * cols_new[None, :]
            / (row_total[factor_slot] / rows_all)
        )
        updates[position] = gradient * lax.rsqrt(estimate)
        moments_new[position] = rows_list[factor_slot]
        column_new.append(cols_new)
    vector_new = second_decay * vector_moment + (1.0 - second_decay) * (
        gradients[1] * gradients[1] + TINY_SQUARE
    )
    updates[1] = gradients[1] * lax.rsqrt(vector_new)
    moments_new[1] = vector_new
    local_spread = jnp.stack([jnp.sum(update * update) for update in updates])
    spread_total = total(local_spread, 6)
    next_weights = []
    spreads = []
    for position in range(8):
        count_all = gradients[position].size * devices
        spread = jnp.sqrt(spread_total[position] / count_all)
        step_scale = jnp.maximum(SCALE_FLOOR, jnp.sqrt(weight_squares[position] / count_all))
        next_weights.append(
            masters[position]
            - STEP_RATE * step_scale * (updates[position] / jnp.maximum(1.0, spread / CLIP_LIMIT))
        )
        spreads.append(spread)
    column_stat = jnp.concatenate(column_new)
    clip_spread = jnp.stack(spreads)
    results = [loss_sum, weight_total]
    for position in range(8):
        results += [gradients[position], moments_new[position], next_weights[position]]
    return tuple(results + [column_stat, clip_spread])


def solution(mesh):
    in_specs = (
        P(("fsdp", "sub"), None),
        P(("fsdp", "sub")),
        P(("fsdp", "sub")),
        P(("fsdp", "sub")),
        P(("fsdp", "sub")),
        P(("fsdp", "sub")),
        P(("fsdp", "sub")),
        P(("fsdp", "sub"), None),
        P(("fsdp", "sub"), None),
        P(("fsdp", "sub"), None),
        P(("fsdp", "sub"), None),
        P(("fsdp", "sub"), None),
        P(("fsdp", "sub"), None),
        P(("fsdp", "sub"), None),
        P(("fsdp", "sub"), None),
        P(("fsdp", "sub")),
        P(("fsdp", "sub")),
        P(("fsdp", "sub")),
        P(("fsdp", "sub")),
        P(("fsdp", "sub")),
        P(("fsdp", "sub")),
        P(("fsdp", "sub")),
        P(("fsdp", "sub"), None),
        P(),
    )
    out_specs = (
        P(),
        P(),
        P(("fsdp", "sub"), None),
        P(("fsdp", "sub")),
        P(("fsdp", "sub"), None),
        P(("fsdp", "sub"), None),
        P(("fsdp", "sub"), None),
        P(("fsdp", "sub"), None),
        P(("fsdp", "sub"), None),
        P(("fsdp", "sub")),
        P(("fsdp", "sub"), None),
        P(("fsdp", "sub"), None),
        P(("fsdp", "sub")),
        P(("fsdp", "sub"), None),
        P(("fsdp", "sub"), None),
        P(("fsdp", "sub")),
        P(("fsdp", "sub"), None),
        P(("fsdp", "sub"), None),
        P(("fsdp", "sub")),
        P(("fsdp", "sub"), None),
        P(("fsdp", "sub"), None),
        P(("fsdp", "sub")),
        P(("fsdp", "sub"), None),
        P(("fsdp", "sub"), None),
        P(("fsdp", "sub")),
        P(("fsdp", "sub"), None),
        P(),
        P(),
    )
    return jax.shard_map(
        on_device, mesh=mesh, in_specs=in_specs, out_specs=out_specs, check_vma=False
    )
```

time: 2480 us -> 990 us (0.40)
  waiting for transfers between devices: 1540 us -> 0.07 us
  Pallas kernels: 0 us -> 486 us
  matrix products: 443 us -> 218 us
  blocking collectives: 164 us -> 0 us
  other arithmetic: 213 us -> 146 us
    reduce_scatter x6 -> x0, waiting for transfers between devices: 1100 us -> none  [the longest x1 252 us: on_device(): lax.psum_scatter(ada_grad, ('fsdp', 'sub'), scatter_dimension=0, tiled=True)]
    pallas_call x0 -> x7, Pallas kernels: none -> 486 us  [the longest x1 175 us: attend_back(): pl.pallas_call(partial(attend_back_kernel, linked), grid=(HEADS // 2,), o...]
    all_gather x7 -> x2, waiting for transfers between devices: 230 us -> 0.04 us  [gathered(): return lax.all_gather(values, AXES, axis=0, tiled=True)]
    dot_general x12 -> x1, matrix products: 207 us -> 0.94 us  [on_device(): jnp.dot(cond_grad.T, label_hot.astype(jnp.float32), precision=lax.Precisi...]
    unnamed x18 -> x2, waiting for transfers between devices: 128 us -> 0.03 us
    psum x3 -> x0, blocking collectives: 120 us -> none  [the longest x1 42.4 us: on_device(): loss_sum = lax.psum(local_loss, ('fsdp', 'sub'))]
    psum x1 -> x0, waiting for transfers between devices: 73.9 us -> none  [on_device(): lax.psum((column_local, row_local, local_squares), ('fsdp', 'sub'))]
    convert_element_type x6 -> x4, other arithmetic: 71.5 us -> 5.69 us  [the longest x1 4.92 us: on_device(): normed = modulate(embedded, scale_one, shift_one).astype(low)]
  transfers between devices with their start and end apart: 16 -> 2, of which waited for: 14 -> 0; matrix products, arithmetic and copies ran while one was open for 13% -> 11% of each run, Pallas kernels for 0% -> 22%
where the time goes in v1:
time: 990 us; the launch traced here: 979 us
  Pallas kernels  486 us (49%)
  matrix products  218 us (22%)
  other arithmetic  146 us (15%)
  local copies, waits for them, and re-layouts  96.9 us (10%)
  between operations  32 us (3%)
    dot_general x26, matrix products, bfloat_product(): return jnp.dot(left_side, right_side, preferred_element_type=jnp.float32)  217 us
    pallas_call x1, Pallas kernels, attend_back(): pl.pallas_call(partial(attend_back_kernel, linked), grid=(HEADS // 2,), o...  175 us
    pallas_call x1, Pallas kernels, attend(): pl.pallas_call(partial(attend_kernel, linked), grid=(HEADS // 2,), out_sh...  127 us
    pallas_call x1, Pallas kernels, last_exchange(): pl.pallas_call(last_kernel, out_shape=(jax.ShapeDtypeStruct((pairs, depth...  64.9 us
    pallas_call x1, Pallas kernels, first_exchange(): pl.pallas_call(first_kernel, out_shape=(jax.ShapeDtypeStruct(part.shape[5...  64.9 us
    pallas_call x2, Pallas kernels, total(): pl.pallas_call(total_kernel, out_shape=jax.ShapeDtypeStruct(flat.shape, j...  34 us
    pallas_call x1, Pallas kernels, small_gather(): pl.pallas_call(small_gather_kernel, out_shape=(jax.ShapeDtypeStruct(FIVE...  20.6 us
  transfers between devices with their start and end apart: 2, of which 0 were waited for; matrix products, arithmetic and copies ran while one was open for 11% of the time, Pallas kernels for 22%

profile of v1, /device:TPU:0, one launch (start us, length us, event | category | flops | bytes accessed | tf_op | source)
XLA Modules:
  0.0 978.8 jit_solution(1550792190970734587)
XLA Ops:
  7.2 2.6 multiply_reduce_fusion.12
  10.0 2.6 multiply_reduce_fusion.10
  20.3 2.5 fusion.158
  22.9 2.1 scatter.9.tags_ref
  25.6 20.6 %small_gather.1 = (bf16[2,2,2,2,2,32,128]{6,5,4,3,2,1,0:T(8,128)(2,1)}, f32[2,2,2,2,2,8,128]{6,5,4,3,2,1,0:T(8,128)}) custom-call(bf16[32,128]{1,0:T(8,128)(2,1)} %maximum_maximum_fusion.rows_ref, f32[8,128]{1,0:T(8,128)} %copy-done.88), custom_call_target="tpu_custom_call" | custom-call | tf_op jit(solution)/shard_map/small_gather/pallas_call | solution.py:250
  49.6 3.6 fusion.159
  53.2 5.5 copy.137
  61.6 3.0 reshape.525.part_ref
  65.9 64.9 %modulation_scatter_qkv_gather.1 = (f32[96,128]{1,0:T(8,128)}, bf16[2,2,2,2,2,32,3072]{6,5,4,3,2,1,0:T(8,128)(2,1)}) custom-call(f32[2,2,2,2,2,96,128]{6,5,4,3,2,1,0:T(8,128)} %reshape.525.part_ref, bf16[32,3072]{1,0:T(8,128)(2,1)} %get-tuple-element.242.own_ref), custom_call_target="tpu_custom_call" | custom-call | tf_op jit(solution)/shard_map/modulation_scatter_qkv_gather/pallas_call | solution.py:298
  133.0 3.1 multiply_reduce_fusion.6
  139.7 4.9 add_convert_fusion.1
  144.6 4.9 fusion.31
  149.6 9.0 fusion.161.q_ref.k_ref.v_ref
  158.6 126.6 %attention_forward.1 = (bf16[1024,1024]{1,0:T(8,128)(2,1)}, bf16[2,2,2,2,2,32,1024]{6,5,4,3,2,1,0:T(8,128)(2,1)}, bf16[2,2,2,2,2,4,32,1024]{7,6,5,4,3,2,1,0:T(8,128)(2,1)}) custom-call(f32[1024,3072]{1,0:T(8,128)} %fusion.161.q_ref.k_ref.v_ref, f32[1024,3072]{1,0:T(8,128)} %fusion.161.q_ref.k_ref.v_ref, f32[1024,3072]{1,0:T(8,128)} %fusion.161.q_ref.k_ref.v_ref, ...), custom_call_target="tpu_custom_call" | custom-call | tf_op jit(solution)/shard_map/attention_forward/pallas_call | solution.py:429
  286.6 7.2 fusion.151
  293.8 2.0 copy-done
  296.4 16.8 %fusion.139 = f32[1024,4096]{1,0:T(8,128)} fusion(bf16[1024,4096]{1,0:T(8,128)(2,1)} %all-gather.3.cloned.1.call-done, f32[1024,1024]{0,1:T(8,128)} %copy-done, f32[1024]{0:T(1024)S(1)} %bitcast.375, f32[1024]{0:T(1024)S(1)} %bitcast.377, f32[1024]{0:T(1024)S(1)} %bitcast.311, f32[1024]{0:T(1024)S(1)} %bitcast.317, f32[1024]{0:T(1024)S(1)} %fusion.123, ...), kind=kOutput, calls=%fused_computation.277 | convolution fusion | flops 8598323200 | bytes 29385728 | tf_op jit(solution)/shard_map/dot_general | solution.py:42
  313.3 21.9 %fusion.149 = (f32[1024]{0:T(1024)S(1)}, f32[1024,1024]{0,1:T(8,128)S(1)}, f32[1024,1024]{0,1:T(8,128)}) fusion(f32[1024,1024]{0,1:T(8,128)S(1)} %copy-done.1, f32[1024]{0:T(1024)S(1)} %bitcast.358, f32[1024]{0:T(1024)S(1)} %bitcast.354, pred[1024]{0:T(1024)(128)(4,1)S(1)} %broadcast_compare_fusion.1, bf16[4096,1024]{1,0:T(8,128)(2,1)} %bitcast.380, ...), kind=kOutput, calls=%fused_computation.287 | convolution fusion | flops 8631876608 | bytes 37762048 | tf_op jit(solution)/shard_map/dot_general | solution.py:42
  335.2 1.9 copy-done.12
  337.7 13.6 %fusion.160 = (f32[1024]{0:T(1024)S(1)}, f32[1024,4096]{1,0:T(8,128)S(1)}) fusion(bf16[1024,4096]{1,0:T(8,128)(2,1)} %all-gather.5.cloned.1.call-done, f32[1024,1024]{0,1:T(8,128)} %copy-done.12, f32[1024]{0:T(1024)S(1)} %bitcast.343, f32[1024]{0:T(1024)S(1)} %fusion.124, f32[1024]{0:T(1024)S(1)} %broadcast_multiply_fusion), kind=kOutput, calls=%fused_computation.296 | convolution fusion | flops 8598322176 | bytes 29376512 | tf_op jit(solution)/shard_map/dot_general | solution.py:42
  351.3 5.6 select_reduce_fusion
  358.2 8.1 multiply_convert_fusion
  366.3 14.8 %convolution_convert_fusion.2 = bf16[1024,4096]{1,0:T(8,128)(2,1)} fusion(bf16[1024,4096]{1,0:T(8,128)(2,1)} %multiply_convert_fusion, f32[1024,1024]{0,1:T(8,128)S(1)} %copy-done.13, f32[1024]{0:T(1024)S(1)} %bitcast.344, f32[1024]{0:T(1024)S(1)} %fusion.124, f32[1024]{0:T(1024)S(1)} %broadcast_multiply_fusion), kind=kOutput, calls=%fused_computation.16 | convolution fusion | flops 8598323200 | bytes 20983808 | tf_op jit(solution)/shard_map/dot_general | solution.py:42
  381.2 12.6 %multiply_reduce_fusion = (f32[1024]{0:T(1024)}, f32[1024]{0:T(1024)S(1)}, f32[1024,1024]{0,1:T(8,128)S(1)}) fusion(f32[1024,1024]{0,1:T(8,128)S(1)} %copy-done.13, f32[1024]{0:T(1024)S(1)} %fusion.124, f32[1024]{0:T(1024)S(1)} %broadcast_multiply_fusion, f32[1024]{0:T(1024)S(1)} %bitcast.345, bf16[1024,4096]{1,0:T(8,128)(2,1)S(1)} %copy-done.18, ...), kind=kOutput, calls=%fused_computation.50 | convolution fusion | flops 8597272576 | bytes 25186304 | tf_op jit(solution)/shard_map/dot_general | solution.py:42
  393.8 3.3 fusion.148
  397.1 26.8 %fusion.6 = bf16[1024,4096]{1,0:T(8,128)(2,1)} fusion(f32[1024,4096]{1,0:T(8,128)} %fusion.139, bf16[4096,1024]{1,0:T(8,128)(2,1)} %bitcast.381, f32[1024,1024]{0,1:T(8,128)} %get-tuple-element.227, f32[1024]{0:T(1024)S(1)} %negate_multiply_fusion.2, f32[1024]{0:T(1024)S(1)} %bitcast.359, f32[1024]{0:T(1024)S(1)} %bitcast.355, ...), kind=kOutput, calls=%fused_computation.8 | convolution fusion | flops 8678014976 | bytes 37762048 | tf_op jit(solution)/shard_map/dot_general | solution.py:42
  423.9 19.3 %convolution_convert_fusion = bf16[4096,1024]{1,0:T(8,128)(2,1)} fusion(f32[1024,1024]{0,1:T(8,128)} %get-tuple-element.227, f32[1024]{0:T(1024)S(1)} %negate_multiply_fusion.2, f32[1024]{0:T(1024)S(1)} %bitcast.360, f32[1024]{0:T(1024)S(1)} %bitcast.356, pred[1024]{0:T(1024)(128)(4,1)S(1)} %broadcast_compare_fusion.1, f32[1024,4096]{1,0:T(8,128)} %fusion.139), kind=kOutput, calls=%fused_computation.14 | convolution fusion | flops 8636071936 | bytes 29373440 | tf_op jit(solution)/shard_map/dot_general | solution.py:42
  443.3 15.5 %convolution_convert_fusion.1 = bf16[1024,4096]{1,0:T(8,128)(2,1)} fusion(bf16[1024,4096]{1,0:T(8,128)(2,1)} %fusion.6, f32[1024,1024]{0,1:T(8,128)S(1)} %copy-done.2, f32[1024]{0:T(1024)S(1)} %bitcast.376, f32[1024]{0:T(1024)S(1)} %bitcast.378, f32[1024]{0:T(1024)S(1)} %bitcast.312, f32[1024]{0:T(1024)S(1)} %bitcast.318, f32[1024]{0:T(1024)S(1)} %copy-done.65, ...), kind=kOutput, calls=%fused_computation.15 | convolution fusion | flops 8602517504 | bytes 20997120 | tf_op jit(solution)/shard_map/dot_general | solution.py:42
  458.7 12.8 %fusion.162 = f32[1024,1024]{1,0:T(8,128)} fusion(bf16[1024,4096]{1,0:T(8,128)(2,1)S(1)} %copy-done.104, bf16[1024,4096]{1,0:T(8,128)(2,1)} %all-gather.3.cloned.1.call-done), kind=kOutput, calls=%fused_computation.298 | convolution fusion | flops 8589934592 | bytes 20971520 | tf_op jit(solution)/shard_map/dot_general | solution.py:42
  471.5 5.3 copy.147
  476.8 4.9 multiply_reduce_fusion.2
  482.8 7.3 select_reduce_fusion.6
  490.1 3.8 select_reduce_fusion.12
  493.9 4.1 convolution_convert_fusion.4.m_ref
  498.0 175.1 %attention_backward.1 = (bf16[3,1024,1024]{2,1,0:T(8,128)(2,1)}, f32[8,1024]{1,0:T(8,128)}, f32[24,32,512]{2,1,0:T(8,128)}) custom-call(f32[1024,3072]{1,0:T(8,128)} %fusion.161.q_ref.k_ref.v_ref, f32[1024,3072]{1,0:T(8,128)} %fusion.161.q_ref.k_ref.v_ref, f32[1024,3072]{1,0:T(8,128)} %fusion.161.q_ref.k_ref.v_ref, ...), custom_call_target="tpu_custom_call" | custom-call | tf_op jit(solution)/shard_map/attention_backward/pallas_call | solution.py:552
  673.1 4.8 fusion.54
  677.9 2.4 fusion.51
  680.3 2.4 fusion.48
  682.8 4.1 convolution_convert_fusion.3
  686.9 4.3 fusion.33
  691.2 4.6 fusion.35
  695.8 13.1 %pad_maximum_fusion = bf16[1024,3072]{0,1:T(8,128)(2,1)} fusion(bf16[1024,1024]{0,1:T(8,128)(2,1)S(1)} %fusion.54, bf16[1024,1024]{0,1:T(8,128)(2,1)S(1)} %fusion.51, bf16[1024,1024]{0,1:T(8,128)(2,1)S(1)} %fusion.48), kind=kLoop, calls=%fused_computation.17 | loop fusion | flops 18874368 | bytes 12582912 | tf_op jit(solution)/shard_map/concatenate | solution.py:894
  708.9 8.6 copy.148
  717.5 10.8 %multiply_reduce_fusion.1 = (f32[1024]{0:T(1024)S(1)}, f32[1024,1024]{1,0:T(8,128)}) fusion(f32[1024,1024]{1,0:T(8,128)} %copy.137, f32[1024]{0:T(1024)S(1)} %bitcast.324, f32[1024]{0:T(1024)S(1)} %bitcast.328, f32[1024]{0:T(1024)S(1)} %copy-done.51, pred[1024]{0:T(1024)(128)(4,1)S(1)} %broadcast_compare_fusion.1, f32[1024,1024]{1,0:T(8,128)} %fusion.33, ...), kind=kOutput, calls=%fused_computation.64 | convolution fusion | flops 2155871232 | bytes 20988928 | tf_op jit(solution)/shard_map/dot_general | solution.py:42
  728.4 5.4 copy.151
  733.9 7.5 select_reduce_fusion.2
  742.1 14.9 %fusion.13 = f32[1024,1024]{1,0:T(8,128)S(1)} fusion(f32[1024,1024]{0,1:T(8,128)} %copy.151, f32[1024,1024]{0,1:T(8,128)S(1)} %copy-done.5, f32[1024,1024]{0,1:T(8,128)} %get-tuple-element.301, f32[1024,1024]{0,1:T(8,128)S(1)} %copy-done.7, f32[1024,1024]{0,1:T(8,128)S(1)} %copy-done.11, f32[1024,1024]{0,1:T(8,128)} %copy-done.14, ...), kind=kLoop, calls=%fused_computation.34 | loop fusion | flops 34603008 | bytes 29447168 | tf_op jit(solution)/shard_map/add | solution.py:903
  762.9 64.9 %last_scatter.1 = (f32[8,32,512]{2,1,0:T(8,128)}, f32[32,128]{1,0:T(8,128)}, bf16[2,2,2,2,2,96,128]{6,5,4,3,2,1,0:T(8,128)(2,1)}) custom-call(bf16[2,2,2,2,2,32,3072]{6,5,4,3,2,1,0:T(8,128)(2,1)} %bitcast.275, bf16[2,2,2,2,2,32,1024]{6,5,4,3,2,1,0:T(8,128)(2,1)} %bitcast.282, f32[2,2,2,2,2,32,128]{6,5,4,3,2,1,0:T(8,128)} %concatenate.45.small_ref, ...), custom_call_target="tpu_custom_call" | custom-call | tf_op jit(solution)/shard_map/last_scatter/pallas_call | solution.py:623
  827.8 1.8 reshape.536
  830.0 1.9 fusion.71
  831.9 1.8 fusion.88
  843.5 1.8 fusion.142
  845.3 1.8 fusion.146
  847.1 1.8 fusion.144
  849.0 1.9 fusion.141
  850.9 11.6 %concatenate.47 = f32[20514]{0:T(1024)} concatenate(f32[1042]{0:T(1024)} %get-tuple-element.198, f32[6144]{0:T(1024)} %get-tuple-element.190, f32[3072]{0:T(1024)} %reduce_sum.706, f32[1024]{0:T(1024)} %bitcast.369, f32[4096]{0:T(1024)} %bitcast.333, f32[1024]{0:T(1024)} %bitcast.370, f32[4096]{0:T(1024)} %bitcast.334, f32[1]{0:T(128)} %bitcast.63, f32[1]{0:T(128)} %bitcast.64, ...), dimensions={0} | concatenate | bytes 164112 | tf_op jit(solution)/shard_map/concatenate | solution.py:987
  863.9 19.4 %total.2 = f32[168,128]{1,0:T(8,128)} custom-call(f32[168,128]{1,0:T(8,128)} %pad_bitcast_fusion.in_ref), custom_call_target="tpu_custom_call" | custom-call | tf_op jit(solution)/shard_map/total/pallas_call | solution.py:660
  883.3 1.9 fusion.153
  895.0 2.1 multiply_reduce_fusion.17
  912.4 2.0 multiply_reduce_fusion.7
  918.9 1.7 fusion.75
  920.6 5.2 stack.178
  926.4 14.7 %total.3 = f32[8,128]{1,0:T(8,128)} custom-call(f32[8,128]{1,0:T(8,128)} %pad_bitcast_fusion.1.in_ref), custom_call_target="tpu_custom_call" | custom-call | tf_op jit(solution)/shard_map/total/pallas_call | solution.py:660
  966.8 1.7 multiply_subtract_fusion.6
  (347 shorter events, 87.5 us)
Async XLA Ops:
  7.2 289.2 %all-gather.3.cloned.1.call-start = ((), (), s32[]{:S(2)}) async-start(), calls=%async_computation | async-start | bytes 8650752 | tf_op jit(solution)/shard_map/all_gather | solution.py:682
  9.9 327.7 %all-gather.5.cloned.1.call-start = ((), (), s32[]{:S(2)}) async-start(), calls=%async_computation.1 | async-start | bytes 8650752 | tf_op jit(solution)/shard_map/all_gather | solution.py:682
  47.5 346.3 %copy-start.78 = (f32[1024,1]{0,1:T(1,128)}, f32[1024,1]{0,1:T(1,128)S(1)}, u32[]{:S(2)}) copy-start(f32[1024,1]{0,1:T(1,128)S(1)} %slice.417) | copy-start | bytes 12292
  58.7 73.6 %copy-start.89 = (f32[32,9]{0,1:T(8,128)S(1)}, f32[32,9]{0,1:T(8,128)}, u32[]{:S(2)}) copy-start(f32[32,9]{0,1:T(8,128)} %param.50) | copy-start | bytes 3460
  59.6 73.3 %copy-start.71 = (s32[1024]{0:T(1024)S(1)}, s32[1024]{0:T(1024)}, u32[]{:S(2)}) copy-start(s32[1024]{0:T(1024)} %param.30) | copy-start | bytes 12292
  59.7 73.3 %copy-start.100 = (s32[1024]{0:T(1024)S(1)}, s32[1024]{0:T(1024)}, u32[]{:S(2)}) copy-start(s32[1024]{0:T(1024)} %param.31) | copy-start | bytes 12292
  59.8 71.9 %copy-start.101 = (f32[64]{0:T(128)}, f32[64]{0:T(128)S(1)}, u32[]{:S(2)}) copy-start(f32[64]{0:T(128)S(1)} %eq.101) | copy-start | bytes 772
  64.6 72.3 %copy-start.39 = (f32[32,1024]{1,0:T(8,128)S(1)}, f32[32,1024]{1,0:T(8,128)}, u32[]{:S(2)}) copy-start(f32[32,1024]{1,0:T(8,128)} %param.39) | copy-start | bytes 393220
  64.6 73.7 %copy-start.24 = (f32[128,1024]{1,0:T(8,128)S(1)}, f32[128,1024]{1,0:T(8,128)}, u32[]{:S(2)}) copy-start(f32[128,1024]{1,0:T(8,128)} %param.41) | copy-start | bytes 1572868
  133.0 11.6 %copy-start.50 = (f32[1024]{0:T(1024)}, f32[1024]{0:T(1024)S(1)}, u32[]{:S(2)}) copy-start(f32[1024]{0:T(1024)S(1)} %broadcast_multiply_fusion.2) | copy-start | bytes 12292
  136.8 12.8 %copy-start.60 = (f32[1024]{0:T(1024)}, f32[1024]{0:T(1024)S(1)}, u32[]{:S(2)}) copy-start(f32[1024]{0:T(1024)S(1)} %fusion.122) | copy-start | bytes 12292
  136.9 12.7 %copy-start.56 = (f32[1,1024]{1,0:T(1,128)}, f32[1,1024]{1,0:T(1,128)S(1)}, u32[]{:S(2)}) copy-start(f32[1,1024]{1,0:T(1,128)S(1)} %get-tuple-element.279) | copy-start | bytes 12292
  136.9 12.7 %copy-start.58 = (f32[1,1024]{1,0:T(1,128)}, f32[1,1024]{1,0:T(1,128)S(1)}, u32[]{:S(2)}) copy-start(f32[1,1024]{1,0:T(1,128)S(1)} %get-tuple-element.280) | copy-start | bytes 12292
  136.9 149.8 %copy-start.72 = (f32[1,1024]{1,0:T(1,128)}, f32[1,1024]{1,0:T(1,128)S(1)}, u32[]{:S(2)}) copy-start(f32[1,1024]{1,0:T(1,128)S(1)} %get-tuple-element.275) | copy-start | bytes 12292
  136.9 149.8 %copy-start.74 = (f32[1,1024]{1,0:T(1,128)}, f32[1,1024]{1,0:T(1,128)S(1)}, u32[]{:S(2)}) copy-start(f32[1,1024]{1,0:T(1,128)S(1)} %get-tuple-element.276) | copy-start | bytes 12292
  136.9 159.5 %copy-start.52 = (f32[1,1024]{1,0:T(1,128)}, f32[1,1024]{1,0:T(1,128)S(1)}, u32[]{:S(2)}) copy-start(f32[1,1024]{1,0:T(1,128)S(1)} %get-tuple-element.272) | copy-start | bytes 12292
  136.9 159.5 %copy-start.54 = (f32[1,1024]{1,0:T(1,128)}, f32[1,1024]{1,0:T(1,128)S(1)}, u32[]{:S(2)}) copy-start(f32[1,1024]{1,0:T(1,128)S(1)} %get-tuple-element.273) | copy-start | bytes 12292
  136.9 159.5 %copy-start.96 = (f32[1,1024]{1,0:T(1,128)}, f32[1,1024]{1,0:T(1,128)S(1)}, u32[]{:S(2)}) copy-start(f32[1,1024]{1,0:T(1,128)S(1)} %get-tuple-element.270) | copy-start | bytes 12292
  136.9 159.5 %copy-start.98 = (f32[1,1024]{1,0:T(1,128)}, f32[1,1024]{1,0:T(1,128)S(1)}, u32[]{:S(2)}) copy-start(f32[1,1024]{1,0:T(1,128)S(1)} %get-tuple-element.271) | copy-start | bytes 12292
  139.7 9.9 %slice-start = ((s8[6291456]{0:T(1024)(128)(4,1)}), s8[4194304]{0:T(1024)(128)(4,1)S(1)}, s32[]{:S(2)}) async-start(s8[6291456]{0:T(1024)(128)(4,1)} %bitcast.383), calls=%async_computation.2 | async-start | bytes 8388608
  158.6 128.1 %copy-start.6 = (f32[1024,1024]{0,1:T(8,128)S(1)}, f32[1024,1024]{0,1:T(8,128)}, u32[]{:S(2)}) copy-start(f32[1024,1024]{0,1:T(8,128)} %get-tuple-element.299) | copy-start | bytes 12582916
  293.8 19.4 %copy-start.47 = (f32[1024]{0:T(1024)}, f32[1024]{0:T(1024)S(1)}, u32[]{:S(2)}) copy-start(f32[1024]{0:T(1024)S(1)} %broadcast_multiply_fusion.1) | copy-start | bytes 12292
  296.3 17.0 %copy-start.84 = (f32[1024]{0:T(1024)}, f32[1024]{0:T(1024)S(1)}, u32[]{:S(2)}) copy-start(f32[1024]{0:T(1024)S(1)} %multiply_reduce_fusion.5) | copy-start | bytes 12292
  296.3 16.9 %copy-start.64 = (f32[1024]{0:T(1024)}, f32[1024]{0:T(1024)S(1)}, u32[]{:S(2)}) copy-start(f32[1024]{0:T(1024)S(1)} %fusion.123) | copy-start | bytes 12292
  296.4 16.9 %copy-start.1 = (f32[1024,1024]{0,1:T(8,128)S(1)}, f32[1024,1024]{0,1:T(8,128)}, u32[]{:S(2)}) copy-start(f32[1024,1024]{0,1:T(8,128)} %copy-done) | copy-start | bytes 12582916
  335.2 58.6 %copy-start.68 = (f32[1024]{0:T(1024)}, f32[1024]{0:T(1024)S(1)}, u32[]{:S(2)}) copy-start(f32[1024]{0:T(1024)S(1)} %broadcast_multiply_fusion) | copy-start | bytes 12292
  337.6 56.2 %copy-start.80 = (f32[1024]{0:T(1024)}, f32[1024]{0:T(1024)S(1)}, u32[]{:S(2)}) copy-start(f32[1024]{0:T(1024)S(1)} %fusion.124) | copy-start | bytes 12292
  337.7 13.7 %copy-start.86 = (s32[1024]{0:T(1024)S(1)}, s32[1024]{0:T(1024)}, u32[]{:S(2)}) copy-start(s32[1024]{0:T(1024)} %param.33) | copy-start | bytes 12292
  366.3 14.8 %copy-start.18 = (bf16[1024,4096]{1,0:T(8,128)(2,1)S(1)}, bf16[1024,4096]{1,0:T(8,128)(2,1)}, u32[]{:S(2)}) copy-start(bf16[1024,4096]{1,0:T(8,128)(2,1)} %multiply_convert_fusion) | copy-start | bytes 25165828
  423.9 19.3 %copy-start.2 = (f32[1024,1024]{0,1:T(8,128)S(1)}, f32[1024,1024]{0,1:T(8,128)}, u32[]{:S(2)}) copy-start(f32[1024,1024]{0,1:T(8,128)} %copy-done) | copy-start | bytes 12582916
  423.9 19.3 %copy-start.48 = (f32[1024]{0:T(1024)S(1)}, f32[1024]{0:T(1024)}, u32[]{:S(2)}) copy-start(f32[1024]{0:T(1024)} %copy-done.47) | copy-start | bytes 12292
  423.9 19.3 %copy-start.53 = (f32[1,1024]{1,0:T(1,128)S(1)}, f32[1,1024]{1,0:T(1,128)}, u32[]{:S(2)}) copy-start(f32[1,1024]{1,0:T(1,128)} %copy-done.52) | copy-start | bytes 12292
  423.9 19.3 %copy-start.55 = (f32[1,1024]{1,0:T(1,128)S(1)}, f32[1,1024]{1,0:T(1,128)}, u32[]{:S(2)}) copy-start(f32[1,1024]{1,0:T(1,128)} %copy-done.54) | copy-start | bytes 12292
  423.9 19.3 %copy-start.65 = (f32[1024]{0:T(1024)S(1)}, f32[1024]{0:T(1024)}, u32[]{:S(2)}) copy-start(f32[1024]{0:T(1024)} %copy-done.64) | copy-start | bytes 12292
  423.9 19.3 %copy-start.97 = (f32[1,1024]{1,0:T(1,128)S(1)}, f32[1,1024]{1,0:T(1,128)}, u32[]{:S(2)}) copy-start(f32[1,1024]{1,0:T(1,128)} %copy-done.96) | copy-start | bytes 12292
  423.9 19.3 %copy-start.99 = (f32[1,1024]{1,0:T(1,128)S(1)}, f32[1,1024]{1,0:T(1,128)}, u32[]{:S(2)}) copy-start(f32[1,1024]{1,0:T(1,128)} %copy-done.98) | copy-start | bytes 12292
  443.3 15.5 %copy-start.104 = (bf16[1024,4096]{1,0:T(8,128)(2,1)S(1)}, bf16[1024,4096]{1,0:T(8,128)(2,1)}, u32[]{:S(2)}) copy-start(bf16[1024,4096]{1,0:T(8,128)(2,1)} %fusion.6) | copy-start | bytes 25165828
  742.1 15.0 %copy-start.37 = (bf16[1024,32]{0,1:T(8,128)(2,1)S(1)}, bf16[1024,32]{0,1:T(8,128)(2,1)}, u32[]{:S(2)}) copy-start(bf16[1024,32]{0,1:T(8,128)(2,1)} %param.28) | copy-start | bytes 196612
  742.1 15.0 %copy-start.42 = (bf16[1024,10]{0,1:T(8,128)(2,1)S(1)}, bf16[1024,10]{0,1:T(8,128)(2,1)}, u32[]{:S(2)}) copy-start(bf16[1024,10]{0,1:T(8,128)(2,1)} %copy-done.41) | copy-start | bytes 61444
  762.9 66.7 %copy-start.16 = (f32[32,6144]{1,0:T(8,128)S(1)}, f32[32,6144]{1,0:T(8,128)}, u32[]{:S(2)}) copy-start(f32[32,6144]{1,0:T(8,128)} %param.37) | copy-start | bytes 2359300
  762.9 67.1 %copy-start.63 = (f32[64,32]{0,1:T(8,128)S(1)}, f32[64,32]{0,1:T(8,128)}, u32[]{:S(2)}) copy-start(f32[64,32]{0,1:T(8,128)} %copy-done.62) | copy-start | bytes 24580
  831.9 60.5 %copy-start.20 = (f32[8,32,512]{2,1,0:T(8,128)S(1)}, f32[8,32,512]{2,1,0:T(8,128)}, u32[]{:S(2)}) copy-start(f32[8,32,512]{2,1,0:T(8,128)} %get-tuple-element.76) | copy-start | bytes 1572868
  843.5 75.4 %copy-start.35 = (f32[32,1042]{1,0:T(8,128)}, f32[32,1042]{1,0:T(8,128)S(1)}, u32[]{:S(2)}) copy-start(f32[32,1042]{1,0:T(8,128)S(1)} %get-tuple-element.224) | copy-start | bytes 400132
  918.9 45.2 %copy-start.19 = (f32[32,6144]{1,0:T(8,128)S(1)}, f32[32,6144]{1,0:T(8,128)}, u32[]{:S(2)}) copy-start(f32[32,6144]{1,0:T(8,128)} %get-tuple-element.307) | copy-start | bytes 2359300
  918.9 46.3 %copy-start.34 = (f32[32,3072]{1,0:T(8,128)S(1)}, f32[32,3072]{1,0:T(8,128)}, u32[]{:S(2)}) copy-start(f32[32,3072]{1,0:T(8,128)} %param.38) | copy-start | bytes 1179652
  918.9 46.3 %copy-start.46 = (f32[3072]{0:T(1024)S(1)}, f32[3072]{0:T(1024)}, u32[]{:S(2)}) copy-start(f32[3072]{0:T(1024)} %fusion.117) | copy-start | bytes 36868
  952.2 14.6 %copy-start.67 = (f32[1024]{0:T(1024)S(1)}, f32[1024]{0:T(1024)}, u32[]{:S(2)}) copy-start(f32[1024]{0:T(1024)} %get-tuple-element.244) | copy-start | bytes 12292
  953.5 9.7 copy-start.36
  953.6 9.7 copy-start.38
  953.6 9.7 copy-start.49
  953.6 9.7 copy-start.92
  953.6 10.5 %copy-start.43 = (f32[6144]{0:T(1024)S(1)}, f32[6144]{0:T(1024)}, u32[]{:S(2)}) copy-start(f32[6144]{0:T(1024)} %fusion.109) | copy-start | bytes 73732
  953.6 10.5 %copy-start.94 = (f32[32]{0:T(128)S(1)}, f32[32]{0:T(128)}, u32[]{:S(2)}) copy-start(f32[32]{0:T(128)} %get-tuple-element.221) | copy-start | bytes 388
  954.3 14.2 %copy-start.23 = (f32[32,4096]{1,0:T(8,128)S(1)}, f32[32,4096]{1,0:T(8,128)}, u32[]{:S(2)}) copy-start(f32[32,4096]{1,0:T(8,128)} %param.40) | copy-start | bytes 1572868
  954.3 14.1 %copy-start.45 = (f32[4096]{0:T(1024)S(1)}, f32[4096]{0:T(1024)}, u32[]{:S(2)}) copy-start(f32[4096]{0:T(1024)} %get-tuple-element.245) | copy-start | bytes 49156
  954.3 14.1 %copy-start.91 = (f32[32]{0:T(128)S(1)}, f32[32]{0:T(128)}, u32[]{:S(2)}) copy-start(f32[32]{0:T(128)} %get-tuple-element.309) | copy-start | bytes 388
  955.4 14.0 %copy-start.32 = (f32[6,4,8,512]{3,2,0,1:T(8,128)}, f32[6,4,8,512]{3,2,0,1:T(8,128)S(1)}, u32[]{:S(2)}) copy-start(f32[6,4,8,512]{3,2,0,1:T(8,128)S(1)} %copy.256) | copy-start | bytes 1179652
  956.9 12.5 %copy-start.40 = (f32[2,4,8,512]{3,2,0,1:T(8,128)}, f32[2,4,8,512]{3,2,0,1:T(8,128)S(1)}, u32[]{:S(2)}) copy-start(f32[2,4,8,512]{3,2,0,1:T(8,128)S(1)} %copy.257) | copy-start | bytes 393220
  958.7 11.8 %copy-start.27 = (f32[8,4,8,512]{3,2,0,1:T(8,128)}, f32[8,4,8,512]{3,2,0,1:T(8,128)S(1)}, u32[]{:S(2)}) copy-start(f32[8,4,8,512]{3,2,0,1:T(8,128)S(1)} %copy.258) | copy-start | bytes 1572868
  958.7 10.7 %copy-start.25 = (f32[128,1024]{1,0:T(8,128)S(1)}, f32[128,1024]{1,0:T(8,128)}, u32[]{:S(2)}) copy-start(f32[128,1024]{1,0:T(8,128)} %param.41) | copy-start | bytes 1572868
  958.7 10.7 %copy-start.66 = (f32[1024]{0:T(1024)S(1)}, f32[1024]{0:T(1024)}, u32[]{:S(2)}) copy-start(f32[1024]{0:T(1024)} %get-tuple-element.243) | copy-start | bytes 12292
  958.8 10.7 %copy-start.93 = (f32[128]{0:T(128)S(1)}, f32[128]{0:T(128)}, u32[]{:S(2)}) copy-start(f32[128]{0:T(128)} %get-tuple-element.213) | copy-start | bytes 1540
  960.7 9.8 %copy-start.28 = (f32[16,8,2,512]{3,1,2,0:T(8,128)}, f32[16,8,2,512]{3,1,2,0:T(8,128)S(1)}, u32[]{:S(2)}) copy-start(f32[16,8,2,512]{3,1,2,0:T(8,128)S(1)} %copy.264) | copy-start | bytes 1572868
  961.3 9.1 copy-start.26
  (47 other events, 270.8 us)
Sparse Core Ops, SparseCore 0:
  11.5 92.7 all-gather.2
  107.7 80.6 all-gather.4

commit v2 on v1

--- a/solution.py
+++ b/solution.py
@@ -36,6 +36,10 @@
 SCORE_SCALE = HEAD_DIM ** (-0.5)
 EXP_SCALE = SCORE_SCALE * math.log2(math.e)
 VMEM_GRANT = 58 * 1024 * 1024
+FIRST_WIDTH, FIRST_LAG = 256, 1
+ATTEND_WIDTH, ATTEND_LAG = 128, 2
+BACK_WIDTH, BACK_LAG = 256, 2
+LAST_WIDTH, LAST_LAG = 256, 2
 
 
 def bfloat_product(left_side, right_side):
@@ -89,14 +93,15 @@
 
 
 class Gather:
-    def __init__(self, place, groups, sends, recvs, local_sems):
-        self.place, self.groups = place, groups
+    def __init__(self, place, groups, sends, recvs, local_sems, lag=1):
+        self.place, self.groups, self.lag = place, groups, lag
         self.sends, self.recvs, self.local_sems = sends, recvs, local_sems
+        self.steps = groups[-1][1] + 5 * lag
 
     @staticmethod
-    def scratch():
+    def scratch(lag=1):
         dma = pltpu.SemaphoreType.DMA
-        return [dma((5, 2, 2)), dma((5, 2, 2)), dma((2, 2))]
+        return [dma((5, 2, 2 * lag)), dma((5, 2, 2 * lag)), dma((2, 2 * lag))]
 
     def region(self, stage, parity):
         done = GATHER_ORDERS[parity][:stage]
@@ -121,11 +126,11 @@
 
     def step(self, t):
         for stage in reversed(range(6)):
-            j = t - stage
+            j = t - stage * self.lag
             for group in self.groups:
 
                 def body(group=group, stage=stage, j=j):
-                    slot = lax.rem(j, 2)
+                    slot = lax.rem(j, 2 * self.lag)
                     for parity in range(2):
                         if stage == 0:
                             self.local(group, j, parity, slot).start()
@@ -140,22 +145,23 @@
 
 
 class Scatter:
-    def __init__(self, place, groups, store, scratch):
-        self.place, self.groups, self.store = place, groups, store
+    def __init__(self, place, groups, store, scratch, lag=1):
+        self.place, self.groups, self.store, self.lag = place, groups, store, lag
         self.keep = scratch[0]
         self.land = scratch[1:6]
         self.sums = (None,) + tuple(scratch[6:10])
         self.sends, self.recvs, self.keep_sems = scratch[10:13]
         self.first, self.end = groups[0][0], groups[-1][1]
+        self.steps = self.end + 5 * lag
 
     @staticmethod
-    def scratch(piece, kind):
+    def scratch(piece, kind, lag=1):
         dma = pltpu.SemaphoreType.DMA
         return (
-            [pltpu.VMEM((2,) + (2,) * 4 + piece, kind)]
-            + [pltpu.VMEM((2, 2) + (2,) * (4 - k) + piece, kind) for k in range(5)]
-            + [pltpu.VMEM((2,) + (2,) * (5 - k) + piece, kind) for k in range(1, 5)]
-            + [dma((5, 2, 2)), dma((5, 2, 2)), dma((2,))]
+            [pltpu.VMEM((lag, 2) + (2,) * 4 + piece, kind)]
+            + [pltpu.VMEM((2 * lag, 2) + (2,) * (4 - k) + piece, kind) for k in range(5)]
+            + [pltpu.VMEM((lag, 2) + (2,) * (5 - k) + piece, kind) for k in range(1, 5)]
+            + [dma((5, 2, 2 * lag)), dma((5, 2, 2 * lag)), dma((2, lag))]
         )
 
     def half(self, stage, parity, other):
@@ -165,12 +171,13 @@
         value = 1 - bit if other else bit
         return (parity,) + tuple(value if d == order[stage] else slice(None) for d in left)
 
-    def copy(self, stage, parity, slot, source=None):
+    def copy(self, stage, parity, j, source=None):
+        slot = lax.rem(j, 2 * self.lag)
         if source is None:
             if stage == 0:
-                source = self.keep.at[parity]
+                source = self.keep.at[lax.rem(j, self.lag), parity]
             else:
-                source = self.sums[stage].at[self.half(stage, parity, True)]
+                source = self.sums[stage].at[(lax.rem(j, self.lag),) + self.half(stage, parity, True)]
         return self.place.send(
             source,
             self.land[stage].at[slot, parity],
@@ -181,47 +188,58 @@
 
     def step(self, t):
         for stage in reversed(range(6)):
-            j = t - stage
+            j = t - stage * self.lag
 
             def body(stage=stage, j=j):
-                slot = lax.rem(j, 2)
+                slot, near = lax.rem(j, 2 * self.lag), lax.rem(j, self.lag)
                 for parity in range(2):
-                    if stage >= 1:
-                        before = stage - 1
-                        if before == 0:
-                            pltpu.make_async_copy(
-                                self.keep.at[parity], self.keep.at[parity], self.keep_sems.at[parity]
-                            ).wait()
-                        self.copy(before, parity, slot).wait()
-                        if before == 0:
-                            mine = self.keep[parity]
-                        else:
-                            mine = self.sums[before][self.half(before, parity, False)]
-                        total = mine.astype(jnp.float32) + self.land[before][slot, parity].astype(
-                            jnp.float32
-                        )
-                        if stage < 5:
-                            self.sums[stage][parity] = total.astype(self.keep.dtype)
-                        else:
-                            self.store(j, parity, total)
-                    if 1 <= stage < 5:
-                        self.copy(stage, parity, slot).start()
+                    before = stage - 1
+                    if before == 0:
+                        pltpu.make_async_copy(
+                            self.keep.at[near, parity],
+                            self.keep.at[near, parity],
+                            self.keep_sems.at[parity, near],
+                        ).wait()
+                    self.copy(before, parity, j).wait()
+                    if before == 0:
+                        mine = self.keep[near, parity]
+                    else:
+                        mine = self.sums[before][(near,) + self.half(before, parity, False)]
+                    total = mine.astype(jnp.float32) + self.land[before][slot, parity].astype(
+                        jnp.float32
+                    )
+                    if stage < 5:
+                        self.sums[stage][near, parity] = total.astype(self.keep.dtype)
+                        self.copy(stage, parity, j).start()
+                    else:
+                        self.store(j, parity, total)
 
             if stage == 0:
                 for low, high, source in self.groups:
 
                     def begin(source=source, j=j):
-                        slot = lax.rem(j, 2)
+                        near = lax.rem(j, self.lag)
                         core = self.place.bit["c"]
                         for parity in range(2):
-                            self.copy(0, parity, slot, source(j, parity, 1 - core)).start()
+                            self.copy(0, parity, j, source(j, parity, 1 - core)).start()
                             pltpu.make_async_copy(
-                                source(j, parity, core), self.keep.at[parity], self.keep_sems.at[parity]
+                                source(j, parity, core),
+                                self.keep.at[near, parity],
+                                self.keep_sems.at[parity, near],
                             ).start()
 
                     when_in(j, low, high, begin)
             else:
                 when_in(j, self.first, self.end, body)
+
+
+def finish(engine):
+    done = UNITS * (HEADS // 2)
+
+    @pl.when(pl.program_id(0) == HEADS // 2 - 1)
+    def rest():
+        for t in range(done, engine.steps):
+            engine.step(t)
 
 
 def params(collective_id, **more):
@@ -265,7 +283,7 @@
     place = Place()
     place.meet()
     rows = part_ref.shape[5] // 2
-    width = 256
+    width = FIRST_WIDTH
 
     def store(j, parity, total):
         mod_ref[pl.ds(parity * rows, rows)] = total
@@ -288,9 +306,12 @@
             )
         ],
         *scratch[13:],
-    )
-    for t in range(pairs + 5):
+        lag=FIRST_LAG,
+    )
+    for t in range(6):
         scatter.step(t)
+        gather.step(t)
+    for t in range(6, gather.steps):
         gather.step(t)
 
 
@@ -303,7 +324,7 @@
         ),
         in_specs=[ANY, ANY],
         out_specs=(WHOLE, ANY),
-        scratch_shapes=Scatter.scratch((part.shape[5] // 2, 128), jnp.float32) + Gather.scratch(),
+        scratch_shapes=Scatter.scratch((part.shape[5] // 2, 128), jnp.float32) + Gather.scratch(FIRST_LAG),
         compiler_params=params(1),
         name="modulation_scatter_qkv_gather",
     )(part, own)
@@ -346,7 +367,7 @@
         out_own, down_own, mixed_ref, out_full, down_full, qn, kn, vn = refs[:8]
         sems = refs[8:]
         place = Place()
-        width = 128
+        width = ATTEND_WIDTH
         split = out_own.shape[1] // (2 * width)
         depth = out_own.shape[0]
         parts = down_own.shape[0] // depth
@@ -376,8 +397,8 @@
                 (split, split + split * parts, down_source, down_target),
             ],
             *sems,
+            lag=ATTEND_LAG,
         )
-        assert split + split * parts + 5 <= UNITS * (HEADS // 2)
         pl.when(pl.program_id(0) == 0)(place.meet)
     else:
         mixed_ref, qn, kn, vn = refs
@@ -399,6 +420,9 @@
             both.append(dot_plain((raised * share).astype(jnp.bfloat16), vn[...]))
         low_lane = lax.broadcasted_iota(jnp.int32, both[0].shape, 1) < HEAD_DIM
         mixed_ref[rows] = jnp.where(low_lane, both[0], both[1]).astype(jnp.bfloat16)
+
+    if linked:
+        finish(gather)
 
 
 def attend(projected, gains, bias, out_own=None, down_own=None):
@@ -425,7 +449,7 @@
             jax.ShapeDtypeStruct(FIVE + (down_own.shape[0] // depth, depth, D), jnp.bfloat16),
         ]
         out_specs += [ANY, ANY]
-        scratch = scratch + Gather.scratch()
+        scratch = scratch + Gather.scratch(ATTEND_LAG)
     return pl.pallas_call(
         partial(attend_kernel, linked),
         grid=(HEADS // 2,),
@@ -443,7 +467,7 @@
         head_ref, up_ref, down_ref, grad_ref, gain_grad_ref, done_ref = refs[:6]
         qn, kn, vn, dq, dk, dv = refs[6:12]
         place = Place()
-        width = 256
+        width = BACK_WIDTH
         wide = up_ref.shape[6] // (2 * width)
         narrow = down_ref.shape[7] // (2 * width)
         parts = down_ref.shape[5]
@@ -471,8 +495,8 @@
             ],
             store,
             refs[12:],
+            lag=BACK_LAG,
         )
-        assert pairs + 5 <= UNITS * (HEADS // 2)
         pl.when(pl.program_id(0) == 0)(place.meet)
     else:
         grad_ref, gain_grad_ref = refs[:2]
@@ -515,6 +539,8 @@
         gain_rows.append(jnp.sum(normed_grad * raw * rate, axis=0, keepdims=True))
     grad_ref[2] = dv[...].astype(jnp.bfloat16)
     gain_grad_ref[...] = jnp.concatenate(gain_rows + [jnp.zeros((6, 128), jnp.float32)], axis=0)
+    if linked:
+        finish(scatter)
 
 
 def attend_back(projected, mixed_grad, gains, bias, head_grad=None, up_grad=None, down_grad=None):
@@ -545,10 +571,10 @@
         depth = head_grad.shape[5]
         specs += [ANY, ANY, ANY]
         operands += [head_grad, up_grad, down_grad]
-        pairs = (head_grad.shape[6] + up_grad.shape[6] + down_grad.shape[5] * down_grad.shape[7]) // 512
-        outs += [jax.ShapeDtypeStruct((pairs, depth, 512), jnp.float32)]
+        pairs = (head_grad.shape[6] + up_grad.shape[6] + down_grad.shape[5] * down_grad.shape[7]) // (2 * BACK_WIDTH)
+        outs += [jax.ShapeDtypeStruct((pairs, depth, 2 * BACK_WIDTH), jnp.float32)]
         out_specs += [WHOLE]
-        scratch = scratch + Scatter.scratch((depth, 256), jnp.bfloat16)
+        scratch = scratch + Scatter.scratch((depth, BACK_WIDTH), jnp.bfloat16, BACK_LAG)
     return pl.pallas_call(
         partial(attend_back_kernel, linked),
         grid=(HEADS // 2,),
@@ -561,12 +587,128 @@
     )(*operands)
 
 
-def last_kernel(qkv_ref, out_ref, small_ref, mod_ref, done_ref, small_done, mod_full, *scratch):
+WEIGHT_COLUMNS = (CLASSES + CODE_DIM + LEVELS, 9, 6 * D, 3 * D, D, 4 * D, D, CODES)
+SUM_STARTS = (0, None, 1152, 1152 + 6144, 1152 + 9216, 1152 + 10240, 1152 + 14336, 1152 + 15360)
+SCALARS = 1152 + 19456
+SUM_LANES = SCALARS + 128
+SMALL_LANES = CODE_DIM + LEVELS + 9
+DECAY = 1.0 - STEP ** (-0.8)
+
+
+def three_terms(values):
+    high = values.astype(jnp.bfloat16)
+    rest = values - high.astype(jnp.float32)
+    middle = rest.astype(jnp.bfloat16)
+    return high, middle, (rest - middle.astype(jnp.float32)).astype(jnp.bfloat16)
+
+
+def lane_row(scalars):
+    lanes = lax.broadcasted_iota(jnp.int32, (1, 128), 1)
+    row = jnp.zeros((1, 128), jnp.float32)
+    for lane, value in scalars:
+        row = jnp.where(lanes == lane, value, row)
+    return row
+
+
+def whole_sum(values):
+    return jnp.sum(jnp.sum(values, axis=0, keepdims=True), axis=1, keepdims=True)
+
+
+def weight_tiles(tables_grad, ada_grad, done_attention, done_last, depth):
+    def blocks(ref, first, count, width):
+        return [(lambda at=first + i: ref[at], i * width, width) for i in range(count)]
+
+    near, far = 2 * LAST_WIDTH, 2 * BACK_WIDTH
+    tables_columns = WEIGHT_COLUMNS[0]
+    wide = CODES // far
+    return {
+        0: [(0, [(lambda: tables_grad[:, :tables_columns], 0, tables_columns)])],
+        2: [(1, [(lambda: ada_grad[...], 0, 6 * D)])],
+        3: [(2, blocks(done_last, D // near, 3 * D // near, near))],
+        4: [(3, blocks(done_last, 0, D // near, near))],
+        5: [(4, blocks(done_attention, wide, wide, far))],
+        6: [(6 + part, blocks(done_attention, 2 * wide + part * (D // far), D // far, far)) for part in range(4)],
+        7: [(5, blocks(done_attention, 0, wide, far))],
+    }
+
+
+class Total:
+    def __init__(self, place, sums, land, sends, recvs):
+        self.place, self.sums, self.land = place, sums, land
+        self.sends, self.recvs = sends, recvs
+
+    @staticmethod
+    def scratch(lanes):
+        dma = pltpu.SemaphoreType.DMA
+        return [
+            pltpu.VMEM((6, 1, lanes), jnp.float32),
+            pltpu.VMEM((5, 1, lanes), jnp.float32),
+            dma((5,)),
+            dma((5,)),
+        ]
+
+    def run(self):
+        for stage, dim in enumerate(DIMS):
+            copy = self.place.send(
+                self.sums.at[stage], self.land.at[stage], self.sends.at[stage], self.recvs.at[stage], dim
+            )
+            copy.start()
+            copy.wait()
+            self.sums[stage + 1] = self.sums[stage] + self.land[stage]
+
+
+def last_kernel(
+    out_ref,
+    qkv_low,
+    embedded_ref,
+    grad_ref,
+    heads_grad,
+    normed_ref,
+    codes_ref,
+    second_ref,
+    scale_ref,
+    known_ref,
+    gains_ref,
+    act_ref,
+    cond_ref,
+    hot_ref,
+    loss_ref,
+    attention_ref,
+    tables_ref,
+    vectors_ref,
+    ada_ref,
+    qkv_master,
+    out_master,
+    up_master,
+    down_master,
+    head_master,
+    moments_ref,
+    vector_moment_ref,
+    column_moment_ref,
+    done_ref,
+    small_done,
+    tables_grad,
+    ada_grad,
+    rows_ref,
+    columns_ref,
+    facts_ref,
+    *scratch,
+):
     place = Place()
     place.meet()
-    width = 256
-    wide = qkv_ref.shape[6] // (2 * width)
-    narrow = out_ref.shape[6] // (2 * width)
+    devices = lax.axis_size(AXES)
+    depth = tables_ref.shape[0]
+    width = LAST_WIDTH
+    narrow = D // (2 * width)
+    part_grads, qkv_full, embedded, grad, code_sums, mod_ref, small_ref, load_sems = scratch[40:48]
+    loads = [
+        pltpu.make_async_copy(source, target, load_sems.at[i])
+        for i, (source, target) in enumerate(
+            ((qkv_low, qkv_full), (embedded_ref, embedded), (grad_ref, grad))
+        )
+    ]
+    for load in loads:
+        load.start()
 
     def columns_of(ref, first):
         return lambda j, p, core: ref.at[
@@ -576,14 +718,19 @@
     def store(j, parity, total):
         done_ref[j, :, parity * width : (parity + 1) * width] = total
 
-    pairs = wide + narrow
+    pairs = 4 * narrow
     scatter = Scatter(
         place,
-        [(0, wide, columns_of(qkv_ref, 0)), (wide, pairs, columns_of(out_ref, wide))],
+        [(0, narrow, columns_of(out_ref, 0))]
+        + [
+            ((1 + part) * narrow, (2 + part) * narrow, columns_of(part_grads.at[part], (1 + part) * narrow))
+            for part in range(3)
+        ],
         store,
         scratch[:13],
-    )
-    half = small_ref.shape[5] // 2
+        lag=LAST_LAG,
+    )
+    half = depth // 2
 
     def small_store(j, parity, total):
         small_done[pl.ds(parity * half, half)] = total
@@ -594,84 +741,335 @@
         small_store,
         scratch[13:26],
     )
-    rows = mod_ref.shape[0] // 2
-    gather = Gather(
-        place,
-        [
-            (
-                0,
-                1,
-                lambda j, p: mod_ref.at[pl.ds(p * rows, rows)],
-                lambda j, p, r: mod_full.at[r + (pl.ds(p * rows, rows),)],
+    mod_sums, mod_land, mod_all, mod_sends, mod_recvs = scratch[26:31]
+    bit = place.bit
+
+    def mod_copy(stage):
+        dim = ("c", "x", "y", "u", "w")[stage]
+        if stage < 3:
+            source, target = (mod_ref, mod_sums.at[0], mod_sums.at[1])[stage], mod_land.at[stage]
+        elif stage == 3:
+            source = target = mod_all.at[bit["w"], bit["u"]]
+        else:
+            source = target = mod_all.at[bit["w"]]
+        return place.send(source, target, mod_sends.at[stage], mod_recvs.at[stage], dim)
+
+    def mod_step(stage):
+        if stage:
+            mod_copy(stage - 1).wait()
+        if stage == 1:
+            mod_sums[0] = mod_ref[...] + mod_land[0]
+        elif stage == 2:
+            mod_sums[1] = mod_sums[0] + mod_land[1]
+        elif stage == 3:
+            mod_all[bit["w"], bit["u"]] = mod_sums[1] + mod_land[2]
+        if stage < 5:
+            mod_copy(stage).start()
+
+    first_total = Total(place, *scratch[31:35])
+    second_total = Total(place, *scratch[35:39])
+    sums, facts = first_total.sums, scratch[39]
+    tiles = weight_tiles(tables_grad, ada_grad, attention_ref, done_ref, depth)
+    masters = (
+        tables_ref,
+        vectors_ref,
+        ada_ref,
+        qkv_master,
+        out_master,
+        up_master,
+        down_master,
+        head_master,
+    )
+
+    def ada_part():
+        slots = mod_all[...].reshape(2 * devices, 6 * D)
+        ada_grad[...] = dot_first(act_ref[...], slots)
+        activated_grad = dot_last(slots, ada_ref[...].astype(jnp.bfloat16))
+        cond = cond_ref[...]
+        gate = 1.0 / (1.0 + jnp.exp(-cond))
+        cond_grad = activated_grad * (gate * (1.0 + cond * (1.0 - gate)))
+        shape = (128, hot_ref.shape[1])
+        source = lax.broadcasted_iota(jnp.int32, shape, 0)
+        target = lax.broadcasted_iota(jnp.int32, shape, 1)
+        moved = (target == source + (CLASSES - 9)) & (source >= 9) & (source < SMALL_LANES)
+        shift = jnp.where(moved, 1.0, 0.0).astype(jnp.bfloat16)
+        total = jnp.zeros((depth, hot_ref.shape[1]), jnp.float32)
+        for term in three_terms(cond_grad)[::-1]:
+            total = total + dot_first(term, hot_ref[...])
+        for term in three_terms(small_done[...])[::-1]:
+            total = total + dot_plain(term, shift)
+        tables_grad[...] = total
+
+    def stats(position):
+        row_total = jnp.zeros((1, 1), jnp.float32)
+        for index, group in tiles[position]:
+            row_sum = jnp.zeros((depth, 1), jnp.float32)
+            for load, first, size in group:
+                gradient = load()
+                squared = gradient * gradient + TINY_SQUARE
+                row_sum = row_sum + jnp.sum(squared, axis=1, keepdims=True)
+                at = SUM_STARTS[position] + first
+                sums[0, :, at : at + size] += jnp.sum(squared, axis=0, keepdims=True)
+            rows_new = DECAY * moments_ref[index] + (1.0 - DECAY) * (
+                row_sum * (1.0 / WEIGHT_COLUMNS[position])
             )
-        ],
-        *scratch[26:],
-    )
+            rows_ref[index] = rows_new
+            row_total = row_total + jnp.sum(rows_new, axis=0, keepdims=True)
+        facts[...] += lane_row([(position, row_total)])
+
+    def squares(first, end):
+        for position in range(first, end):
+            master = masters[position][...]
+            facts[...] += lane_row([(8 + position, whole_sum(master * master))])
+
+    def part_grad(part):
+        @pl.loop(0, D // 256)
+        def tile(i):
+            at = columns(i * 256, 256)
+            product = dot_first(normed_ref[...], heads_grad[part, :, at])
+            part_grads[part, :, :, :, :, :, :, at] = product.astype(jnp.bfloat16).reshape(
+                FIVE + (depth, 256)
+            )
+
+    tokens = normed_ref.shape[0]
+    block = tokens // 4
+    slot_rows = [jnp.zeros((1, D), jnp.float32)] * 4
+
+    def norm_back(index):
+        rows = slice(index * block, (index + 1) * block)
+        back = jnp.zeros((block, D), jnp.float32)
+        for part in range(3):
+            back = back + dot_last(heads_grad[part, rows], qkv_full[:, part * D : (part + 1) * D])
+        values = embedded[rows]
+        center = values - jnp.sum(values, axis=1, keepdims=True) * (1.0 / D)
+        rate = lax.rsqrt(jnp.sum(center * center, axis=1, keepdims=True) * (1.0 / D) + NORM_EPSILON)
+        unit = center * rate
+        other = second_ref[rows] > 0.5
+        scale_back = back * unit
+        for at, value in enumerate((scale_back, back)):
+            everything = jnp.sum(value, axis=0, keepdims=True)
+            second = jnp.sum(jnp.where(other, value, 0.0), axis=0, keepdims=True)
+            slot_rows[2 * at] = slot_rows[2 * at] + (everything - second)
+            slot_rows[2 * at + 1] = slot_rows[2 * at + 1] + second
+        unit_back = back * (1.0 + jnp.where(other, scale_ref[1:2], scale_ref[0:1]))
+        mean_back = jnp.sum(unit_back, axis=1, keepdims=True) * (1.0 / D)
+        mean_along = jnp.sum(unit_back * unit, axis=1, keepdims=True) * (1.0 / D)
+        total = grad[rows] + rate * (unit_back - mean_back - unit * mean_along)
+        high = total.astype(jnp.bfloat16)
+        rest = (total - high.astype(jnp.float32)).astype(jnp.bfloat16)
+        product = dot_first(codes_ref[rows], high) + dot_first(codes_ref[rows], rest)
+        code_sums[...] = product if index == 0 else code_sums[...] + product
+
+    def gather_rows():
+        spot = 2 * (4 * bit["y"] + 2 * bit["x"] + bit["c"])
+        row_ids = lax.broadcasted_iota(jnp.int32, (16, D), 0)
+        for kind in range(6):
+            if kind in (2, 4):
+                first, other = slot_rows[kind - 2 : kind]
+            else:
+                at = slice(kind * D, (kind + 1) * D)
+                first, other = known_ref[0:1, at], known_ref[1:2, at]
+            placed = jnp.where(row_ids == spot, first, jnp.where(row_ids == spot + 1, other, 0.0))
+            mod_ref[:, kind * D : (kind + 1) * D] = placed.astype(jnp.bfloat16)
+            code_sums[kind : kind + 1] = first + other
+        code_sums[6:9] = gains_ref[0:3]
+        small_ref[...] = code_sums[...].T.reshape(FIVE + (depth, 128))
+
+    sums[0] = jnp.zeros_like(sums[0])
+    facts[...] = lane_row([(16, loss_ref[...])])
+    steps = iter(range(scatter.steps))
+    for _ in range(narrow):
+        scatter.step(next(steps))
+    for part in range(3):
+        part_grad(part)
+        for _ in range(narrow):
+            scatter.step(next(steps))
+    for load in loads:
+        load.wait()
+    for index in range(4):
+        norm_back(index)
+        scatter.step(next(steps))
+    gather_rows()
+    beside = [
+        partial(stats, 5),
+        partial(stats, 6),
+        partial(stats, 7),
+        partial(squares, 0, 5),
+        partial(squares, 5, 8),
+    ]
     for t in range(6):
-        gather.step(t)
+        mod_step(t)
         small.step(t)
-        scatter.step(t)
-
-    @pl.loop(6, pairs + 5)
-    def later(t):
-        scatter.step(t)
-
-
-def last_exchange(qkv_grad, out_grad, small, modulation):
-    depth = qkv_grad.shape[5]
-    pairs = (qkv_grad.shape[6] + out_grad.shape[6]) // 512
+        if t < len(beside):
+            beside[t]()
+        for step in steps:
+            scatter.step(step)
+            break
+    for step in steps:
+        scatter.step(step)
+    ada_part()
+    stats(0)
+    stats(2)
+    stats(3)
+    stats(4)
+    sums[0, :, SCALARS:] = facts[...]
+    first_total.run()
+    columns_ref[...] = DECAY * column_moment_ref[...] + (1.0 - DECAY) * sums[5] * (1.0 / D)
+    start, end = SUM_STARTS[6], SUM_STARTS[6] + D
+    columns_ref[:, start:end] = DECAY * column_moment_ref[:, start:end] + (1.0 - DECAY) * sums[
+        5, :, start:end
+    ] * (1.0 / (4 * D))
+
+    def rows_all(position):
+        return 4.0 * D if position == 6 else 1.0 * D
+
+    scalars = []
+    for position, groups in tiles.items():
+        at = SCALARS + position
+        row_mean = sums[5, :, at : at + 1] * (1.0 / rows_all(position))
+        spread = jnp.zeros((1, 1), jnp.float32)
+        for index, group in groups:
+            for load, first, size in group:
+                lane = SUM_STARTS[position] + first
+                estimate = rows_ref[index] * columns_ref[:, lane : lane + size] / row_mean
+                update = load() * lax.rsqrt(estimate)
+                spread = spread + whole_sum(update * update)
+        scalars.append((position, spread))
+    gradient = small_done[:, :9]
+    moment = DECAY * vector_moment_ref[...] + (1.0 - DECAY) * (gradient * gradient + TINY_SQUARE)
+    update = gradient * lax.rsqrt(moment)
+    scalars.append((1, whole_sum(update * update)))
+    second_total.sums[0] = lane_row(scalars)
+    second_total.run()
+    spread_row, factor_row = [], []
+    for position in range(8):
+        count = rows_all(position) * WEIGHT_COLUMNS[position]
+        spread = jnp.sqrt(second_total.sums[5, :, position : position + 1] * (1.0 / count))
+        at = SCALARS + 8 + position
+        scale = jnp.maximum(SCALE_FLOOR, jnp.sqrt(sums[5, :, at : at + 1] * (1.0 / count)))
+        spread_row.append((position, spread))
+        factor_row.append((position, STEP_RATE * scale / jnp.maximum(1.0, spread / CLIP_LIMIT)))
+    facts_ref[0] = lane_row(spread_row)
+    facts_ref[1] = lane_row(factor_row)
+    facts_ref[2] = sums[5, :, SCALARS:]
+
+
+def last_exchange(far, near, attention_done, masters, moments):
+    depth = far[0].shape[5]
+    pairs = 4 * D // (2 * LAST_WIDTH)
+    dma = pltpu.SemaphoreType.DMA
+    f32, low = jnp.float32, jnp.bfloat16
+    tokens = far[2].shape[0]
+    operands = list(far) + list(near) + [attention_done] + list(masters) + list(moments)
     return pl.pallas_call(
         last_kernel,
         out_shape=(
-            jax.ShapeDtypeStruct((pairs, depth, 512), jnp.float32),
-            jax.ShapeDtypeStruct(small.shape[5:], jnp.float32),
-            jax.ShapeDtypeStruct(FIVE + modulation.shape, modulation.dtype),
+            jax.ShapeDtypeStruct((pairs, depth, 2 * LAST_WIDTH), f32),
+            jax.ShapeDtypeStruct((depth, 128), f32),
+            jax.ShapeDtypeStruct((depth, 1152), f32),
+            jax.ShapeDtypeStruct((depth, 6 * D), f32),
+            jax.ShapeDtypeStruct((10, depth, 1), f32),
+            jax.ShapeDtypeStruct((1, SUM_LANES), f32),
+            jax.ShapeDtypeStruct((3, 1, 128), f32),
         ),
-        in_specs=[ANY, ANY, ANY, ANY],
-        out_specs=(WHOLE, WHOLE, ANY),
-        scratch_shapes=Scatter.scratch((depth, 256), jnp.bfloat16)
-        + Scatter.scratch((small.shape[5] // 2, 128), jnp.float32)
-        + Gather.scratch(),
+        in_specs=[ANY] * 4 + [WHOLE] * (len(operands) - 4),
+        out_specs=(WHOLE,) * 7,
+        scratch_shapes=Scatter.scratch((depth, LAST_WIDTH), low, LAST_LAG)
+        + Scatter.scratch((depth // 2, 128), f32)
+        + [
+            pltpu.VMEM((2, 16, 6 * D), low),
+            pltpu.VMEM((3, 16, 6 * D), low),
+            pltpu.VMEM((2, 2, 16, 6 * D), low),
+            dma((5,)),
+            dma((5,)),
+        ]
+        + Total.scratch(SUM_LANES)
+        + Total.scratch(128)
+        + [pltpu.VMEM((1, 128), f32)]
+        + [
+            pltpu.VMEM((3,) + FIVE + (depth, D), low),
+            pltpu.VMEM((D, 3 * D), low),
+            pltpu.VMEM((tokens, D), f32),
+            pltpu.VMEM((tokens, D), f32),
+            pltpu.VMEM((128, D), f32),
+            pltpu.VMEM((16, 6 * D), low),
+            pltpu.VMEM(FIVE + (depth, 128), f32),
+            dma((3,)),
+        ],
         compiler_params=params(4),
         name="last_scatter",
-    )(qkv_grad, out_grad, small, modulation)
-
-
-def total_kernel(in_ref, out_ref, sums, land, sends, recvs):
-    place = Place()
-    place.meet()
-    sums[0] = in_ref[...]
-    for stage, dim in enumerate(DIMS):
-        copy = place.send(
-            sums.at[stage], land.at[stage], sends.at[stage], recvs.at[stage], dim
-        )
-        copy.start()
-        copy.wait()
-        sums[stage + 1] = sums[stage] + land[stage]
-    out_ref[...] = sums[5]
-
-
-def total(values, collective_id):
-    if not linked_mesh():
-        return lax.psum(values, AXES)
-    size = values.shape[0]
-    rows = -(-size // 1024) * 8
-    flat = jnp.pad(values, (0, rows * 128 - size)).reshape(rows, 128)
-    summed = pl.pallas_call(
-        total_kernel,
-        out_shape=jax.ShapeDtypeStruct(flat.shape, jnp.float32),
-        in_specs=[WHOLE],
-        out_specs=WHOLE,
-        scratch_shapes=[
-            pltpu.VMEM((6, rows, 128), jnp.float32),
-            pltpu.VMEM((5, rows, 128), jnp.float32),
-            pltpu.SemaphoreType.DMA((5,)),
-            pltpu.SemaphoreType.DMA((5,)),
-        ],
-        compiler_params=params(collective_id),
-        name="total",
-    )(flat)
-    return summed.reshape(-1)[:size]
+    )(*operands)
+
+
+def step_kernel(
+    done_ref,
+    small_ref,
+    tables_grad,
+    ada_grad,
+    rows_ref,
+    columns_ref,
+    facts_ref,
+    attention_ref,
+    vector_moment_ref,
+    tables_ref,
+    vectors_ref,
+    ada_ref,
+    qkv_master,
+    out_master,
+    up_master,
+    down_master,
+    head_master,
+    *outs,
+):
+    depth = tables_ref.shape[0]
+    masters = (
+        tables_ref,
+        vectors_ref,
+        ada_ref,
+        qkv_master,
+        out_master,
+        up_master,
+        down_master,
+        head_master,
+    )
+    vector_stat = outs[16]
+    tiles = weight_tiles(tables_grad, ada_grad, attention_ref, done_ref, depth)
+    for position, groups in tiles.items():
+        grad_ref, next_ref, master = outs[2 * position], outs[2 * position + 1], masters[position]
+        factor = facts_ref[1, :, position : position + 1]
+        mean_scale = 1.0 / (4 * D) if position == 6 else 1.0 / D
+        row_mean = facts_ref[2, :, position : position + 1] * mean_scale
+        for order, (index, group) in enumerate(groups):
+            at = slice(order * depth, (order + 1) * depth)
+            for load, first, size in group:
+                gradient = load()
+                lane = SUM_STARTS[position] + first
+                estimate = rows_ref[index] * columns_ref[:, lane : lane + size] / row_mean
+                grad_ref[at, first : first + size] = gradient
+                next_ref[at, first : first + size] = master[at, first : first + size] - factor * (
+                    gradient * lax.rsqrt(estimate)
+                )
+    gradient = small_ref[:, :9]
+    moment = DECAY * vector_moment_ref[...] + (1.0 - DECAY) * (gradient * gradient + TINY_SQUARE)
+    vector_stat[...] = moment
+    outs[2][...] = gradient
+    outs[3][...] = vectors_ref[...] - facts_ref[1, :, 1:2] * (gradient * lax.rsqrt(moment))
+
+
+def take_step(last, attention_done, vector_moment, masters):
+    operands = list(last) + [attention_done, vector_moment] + list(masters)
+    shapes = []
+    for master in masters:
+        shapes += [jax.ShapeDtypeStruct(master.shape, jnp.float32)] * 2
+    shapes.append(jax.ShapeDtypeStruct(vector_moment.shape, jnp.float32))
+    return pl.pallas_call(
+        step_kernel,
+        out_shape=tuple(shapes),
+        in_specs=[WHOLE] * len(operands),
+        out_specs=(WHOLE,) * len(shapes),
+        compiler_params=pltpu.CompilerParams(vmem_limit_bytes=VMEM_GRANT),
+        name="weight_step",
+    )(*operands)
 
 
 def linked_mesh():
@@ -751,7 +1149,6 @@
         head_weight,
     )
     local_count = jnp.sum(loss_weight).astype(jnp.float32)
-    local_squares = jnp.stack([jnp.sum(master * master) for master in masters])
     low = jnp.bfloat16
     part_kind = low if linked else jnp.float32
     tables_low = tables.astype(low)
@@ -783,8 +1180,8 @@
     code_tables = small_full[:, : CODE_DIM + LEVELS]
     gain_vector = small_full[:, CODE_DIM + LEVELS : CODE_DIM + LEVELS + 9].astype(jnp.float32)
 
-    label_hot = (labels_all[:, None] == jnp.arange(CLASSES, dtype=jnp.float32)[None, :]).astype(low)
-    class_cond = bfloat_product(label_hot, tables_low[:, :CLASSES].T)
+    label_hot = (labels_all[:, None] == jnp.arange(1152, dtype=jnp.float32)[None, :]).astype(low)
+    class_cond = bfloat_product(label_hot[:, :CLASSES], tables_low[:, :CLASSES].T)
     activated = jax.nn.silu(class_cond).astype(low)
     modulation_part = bfloat_product(activated, ada_low)
     if linked:
@@ -874,7 +1271,7 @@
         scale_ids[None, :], segment_ids[None, :], scale_ids[:, None], segment_ids[:, None], real_mask[:, None], same
     )
     if linked:
-        heads_grad, gain_grads, done = attend_back(
+        heads_grad, gain_grads, attention_done = attend_back(
             projected,
             mixed_grad,
             gains,
@@ -883,14 +1280,51 @@
             up_part.reshape(FIVE + (depth, up_part.shape[1])),
             down_part.reshape(FIVE + (down_part.shape[0] // D, depth, D)),
         )
-        wide = CODES // 512
-        wide_up = wide + up_part.shape[1] // 512
-        head_grad = done[:wide].transpose(1, 0, 2).reshape(depth, CODES)
-        up_grad = done[wide:wide_up].transpose(1, 0, 2).reshape(depth, -1)
-        down_grad = done[wide_up:].reshape(-1, 2, depth, 512).transpose(0, 2, 1, 3).reshape(-1, D)
     else:
         heads_grad, gain_grads = attend_back(projected, mixed_grad, gains, turned_bias)
         head_grad, up_grad, down_grad = scattered(head_part), scattered(up_part), scattered(down_part)
+    if linked:
+        unknown = jnp.zeros((2, D), jnp.float32)
+        factored_rows = [tables_moment, ada_moment, qkv_moment, out_moment, up_moment, head_moment]
+        row_moments = jnp.concatenate(factored_rows + [down_moment]).reshape(10, depth, 1)
+        padding = jnp.zeros((110,), jnp.float32)
+        column_moments = jnp.concatenate(
+            [column_moment[:1042], padding, column_moment[1042:], jnp.zeros((128,), jnp.float32)]
+        )[None]
+        known = jnp.concatenate(
+            [gamma_one_grad, gamma_two_grad, unknown, scale_two_grad, unknown, shift_two_grad], axis=1
+        )
+        gain_rows = jnp.concatenate([gain_grads[:2], head_gain_grad[None], jnp.zeros((5, D), jnp.float32)])
+        codes = jnp.pad(code_levels, ((0, 0), (9, 128 - SMALL_LANES)))
+        last = last_exchange(
+            (out_part.reshape(FIVE + (depth, D)), full_qkv, embedded, residual_grad),
+            (
+                heads_grad,
+                normed,
+                codes,
+                second.astype(jnp.float32),
+                modulation[:, 2 * D : 3 * D],
+                known,
+                gain_rows,
+                activated,
+                class_cond,
+                label_hot,
+                local_loss[None, None],
+            ),
+            attention_done,
+            masters,
+            (row_moments, vector_moment, column_moments),
+        )
+        stepped = take_step(last, attention_done, vector_moment, masters)
+        rows_new, cols_new, facts = last[4].reshape(10 * depth), last[5][0], last[6][:, 0]
+        stats = [rows_new[i * depth : (i + 1) * depth] for i in range(6)] + [rows_new[6 * depth :]]
+        moment_of = (stats[0], stepped[16], stats[1], stats[2], stats[3], stats[4], stats[6], stats[5])
+        results = [facts[2, 16], weight_total]
+        for position in range(8):
+            results += [stepped[2 * position], moment_of[position], stepped[2 * position + 1]]
+        column_stat = jnp.concatenate([cols_new[:1042], cols_new[1152:SCALARS]])
+        return tuple(results + [column_stat, facts[0, :8]])
+
     qkv_part = jnp.concatenate(
         [bfloat_product(normed.T, heads_grad[part]).astype(part_kind) for part in range(3)], axis=1
     )
@@ -916,41 +1350,29 @@
     code_grad = split_product(embedded_grad.T, code_levels)
     small_part = jnp.concatenate(
         [
-            code_grad,
             bias_grad.T,
             gain_grads[:2].T,
             head_gain_grad[:, None],
+            code_grad,
             jnp.zeros((D, 128 - CODE_DIM - LEVELS - 9), jnp.float32),
         ],
         axis=1,
     )
     modulation_low = modulation_grad.astype(low)
-    if linked:
-        done, small_grad, modulation_all = last_exchange(
-            qkv_part.reshape(FIVE + (depth, 3 * D)),
-            out_part.reshape(FIVE + (depth, D)),
-            small_part.reshape(FIVE + (depth, 128)),
-            modulation_low.reshape(12 * D // 128, 128),
-        )
-        modulation_all = modulation_all.reshape(2 * devices, 6 * D)
-        wide = 3 * D // 512
-        qkv_grad = done[:wide].transpose(1, 0, 2).reshape(depth, 3 * D)
-        out_grad = done[wide:].transpose(1, 0, 2).reshape(depth, D)
-    else:
-        modulation_all = gathered(modulation_low)
-        small_grad, qkv_grad, out_grad = scattered(small_part), scattered(qkv_part), scattered(out_part)
+    modulation_all = gathered(modulation_low)
+    small_grad, qkv_grad, out_grad = scattered(small_part), scattered(qkv_part), scattered(out_part)
     ada_grad = bfloat_product(activated.T, modulation_all)
     activated_grad = bfloat_product(modulation_all, ada_low.T)
     _, silu_back = jax.vjp(jax.nn.silu, class_cond)
     cond_grad = silu_back(activated_grad)[0]
     class_grad = jnp.dot(
         cond_grad.T,
-        label_hot.astype(jnp.float32),
+        label_hot[:, :CLASSES].astype(jnp.float32),
         precision=lax.Precision.HIGHEST,
         preferred_element_type=jnp.float32,
     )
-    tables_grad = jnp.concatenate([class_grad, small_grad[:, : CODE_DIM + LEVELS]], axis=1)
-    vectors_grad = small_grad[:, CODE_DIM + LEVELS : CODE_DIM + LEVELS + 9]
+    tables_grad = jnp.concatenate([class_grad, small_grad[:, 9:SMALL_LANES]], axis=1)
+    vectors_grad = small_grad[:, :9]
     gradients = (
         tables_grad,
         vectors_grad,
@@ -961,7 +1383,7 @@
         down_grad,
         head_grad,
     )
-    second_decay = 1.0 - STEP ** (-0.8)
+    second_decay = DECAY
     factored_index = (0, 2, 3, 4, 5, 6, 7)
     factored_moments = (
         tables_moment,
@@ -972,6 +1394,7 @@
         down_moment,
         head_moment,
     )
+    local_squares = jnp.stack([jnp.sum(master * master) for master in masters])
     rows_list = []
     column_parts = []
     row_parts = []
@@ -983,8 +1406,8 @@
         column_parts.append(jnp.sum(squared, axis=0))
         row_parts.append(jnp.sum(rows_new))
     column_count = column_moment.shape[0]
-    sums = total(
-        jnp.concatenate(column_parts + [jnp.stack(row_parts), local_squares, local_loss[None]]), 5
+    sums = lax.psum(
+        jnp.concatenate(column_parts + [jnp.stack(row_parts), local_squares, local_loss[None]]), AXES
     )
     column_total = sums[:column_count]
     row_total = sums[column_count : column_count + 7]
@@ -1016,7 +1439,7 @@
     updates[1] = gradients[1] * lax.rsqrt(vector_new)
     moments_new[1] = vector_new
     local_spread = jnp.stack([jnp.sum(update * update) for update in updates])
-    spread_total = total(local_spread, 6)
+    spread_total = lax.psum(local_spread, AXES)
     next_weights = []
     spreads = []
     for position in range(8):

time: 990 us -> 724 us (0.73)
  other arithmetic: 146 us -> 54.8 us
  Pallas kernels: 486 us -> 416 us
  local copies, waits for them, and re-layouts: 96.9 us -> 40.7 us
  matrix products: 218 us -> 187 us
  between operations: 32 us -> 15.9 us
    pallas_call x1, Pallas kernels: 127 us -> 77 us  [attend(): pl.pallas_call(partial(attend_kernel, linked), grid=(HEADS // 2,), out_sh...]
    pallas_call x1, Pallas kernels: 64.9 us -> 112 us  [last_exchange(): pl.pallas_call(last_kernel, out_shape=(jax.ShapeDtypeStruct((pairs, depth...]
    pallas_call x1, Pallas kernels: 175 us -> 130 us  [attend_back(): pl.pallas_call(partial(attend_back_kernel, linked), grid=(HEADS // 2,), o...]
    reduce_sum x25 -> x0, other arithmetic: 43 us -> none  [the longest x8 13.1 us: on_device(): local_squares = jnp.stack([jnp.sum(master * master) for master in masters])]
    dot_general x26 -> x16, matrix products: 217 us -> 187 us  [bfloat_product(): return jnp.dot(left_side, right_side, preferred_element_type=jnp.float32)]
    pallas_call x2 -> x1, Pallas kernels: 34 us -> 6.04 us  [take_step(): pl.pallas_call(step_kernel, out_shape=tuple(shapes), in_specs=[WHOLE] * l...]
    concatenate x5 -> x4, local copies, waits for them, and re-layouts: 23.6 us -> 0.93 us  [the longest x1 0.59 us: on_device(): jnp.concatenate([gain_grads[:2], head_gain_grad[None], jnp.zeros((5, D),...]
    add x6 -> x0, other arithmetic: 22 us -> none  [the longest x1 14.9 us: on_device(): embedded_grad = residual_grad + norm_grad]
  transfers between devices with their start and end apart: 2 -> 2, of which waited for: 0 -> 0; matrix products, arithmetic and copies ran while one was open for 11% -> 15% of each run, Pallas kernels for 22% -> 23%
where the time goes in v2:
time: 724 us; the launch traced here: 714 us
  Pallas kernels  416 us (57%)
  matrix products  187 us (26%)
  other arithmetic  54.8 us (8%)
  local copies, waits for them, and re-layouts  40.7 us (6%)
  between operations  15.9 us (2%)
    dot_general x16, matrix products, bfloat_product(): return jnp.dot(left_side, right_side, preferred_element_type=jnp.float32)  187 us
    pallas_call x1, Pallas kernels, attend_back(): pl.pallas_call(partial(attend_back_kernel, linked), grid=(HEADS // 2,), o...  130 us
    pallas_call x1, Pallas kernels, last_exchange(): pl.pallas_call(last_kernel, out_shape=(jax.ShapeDtypeStruct((pairs, depth...  112 us
    pallas_call x1, Pallas kernels, attend(): pl.pallas_call(partial(attend_kernel, linked), grid=(HEADS // 2,), out_sh...  77 us
    pallas_call x1, Pallas kernels, first_exchange(): pl.pallas_call(first_kernel, out_shape=(jax.ShapeDtypeStruct(part.shape[5...  69.7 us
    pallas_call x1, Pallas kernels, small_gather(): pl.pallas_call(small_gather_kernel, out_shape=(jax.ShapeDtypeStruct(FIVE...  20.1 us
  transfers between devices with their start and end apart: 2, of which 0 were waited for; matrix products, arithmetic and copies ran while one was open for 15% of the time, Pallas kernels for 23%

profile of v2, /device:TPU:0, one launch (start us, length us, event | category | flops | bytes accessed | tf_op | source)
XLA Modules:
  0.0 713.9 jit_solution(9628915496482008765)
XLA Ops:
  7.2 1.8 convert_element_type.109
  9.1 1.8 convert_element_type.112
  10.9 0.7 convert_element_type.98
  11.7 0.9 convert_element_type.97
  12.7 1.3 reduce_sum.210
  16.0 1.3 and_reduce_fusion
  17.3 2.5 fusion.48
  19.8 2.1 scatter.9.tags_ref
  22.6 20.1 %small_gather.1 = (bf16[2,2,2,2,2,32,128]{6,5,4,3,2,1,0:T(8,128)(2,1)}, f32[2,2,2,2,2,8,128]{6,5,4,3,2,1,0:T(8,128)}) custom-call(bf16[32,128]{1,0:T(8,128)(2,1)} %maximum_maximum_fusion.1.rows_ref, f32[8,128]{1,0:T(8,128)} %copy-done.30), custom_call_target="tpu_custom_call" | custom-call | tf_op jit(solution)/shard_map/small_gather/pallas_call | solution.py:268
  42.7 1.1 slice.253
  44.6 1.4 copy.128.vectors_ref
  46.0 1.0 slice.226
  47.7 3.6 fusion.49
  51.3 5.5 copy.114.embedded_ref
  56.8 1.0 slice.249
  57.9 0.8 fusion.26
  58.7 0.8 multiply_convert_fusion.3
  60.6 1.4 reshape.271.part_ref
  62.7 69.7 %modulation_scatter_qkv_gather.1 = (f32[96,128]{1,0:T(8,128)}, bf16[2,2,2,2,2,32,3072]{6,5,4,3,2,1,0:T(8,128)(2,1)}) custom-call(f32[2,2,2,2,2,96,128]{6,5,4,3,2,1,0:T(8,128)} %reshape.271.part_ref, bf16[32,3072]{1,0:T(8,128)(2,1)} %convert_element_type.103.own_ref), custom_call_target="tpu_custom_call" | custom-call | tf_op jit(solution)/shard_map/modulation_scatter_qkv_gather/pallas_call | solution.py:319
  132.4 0.8 reshape.272
  133.2 0.8 slice_bitcast_fusion
  134.0 0.8 slice_bitcast_fusion.1
  136.0 0.7 convert_element_type.107.refs_1_
  137.0 0.8 pad.18.codes_ref
  137.8 1.0 copy.126.second_ref
  139.6 0.9 reshape.283.moments_ref
  142.5 2.8 multiply_reduce_fusion.5
  145.4 4.9 add_convert_fusion.1.normed_ref
  150.4 4.8 fusion.17
  155.2 9.0 %fusion.51.q_ref.k_ref.v_ref = f32[1024,3072]{1,0:T(8,128)} fusion(bf16[1024,1024]{1,0:T(8,128)(2,1)S(1)} %add_convert_fusion.1.normed_ref, bf16[1024,3072]{1,0:T(8,128)(2,1)S(1)} %bitcast.77), kind=kOutput, calls=%fused_computation.129 | convolution fusion | flops 6442450944 | bytes 20971520 | tf_op jit(solution)/shard_map/dot_general | solution.py:46
  164.2 77.0 %attention_forward.1 = (bf16[1024,1024]{1,0:T(8,128)(2,1)}, bf16[2,2,2,2,2,32,1024]{6,5,4,3,2,1,0:T(8,128)(2,1)}, bf16[2,2,2,2,2,4,32,1024]{7,6,5,4,3,2,1,0:T(8,128)(2,1)}) custom-call(f32[1024,3072]{1,0:T(8,128)} %fusion.51.q_ref.k_ref.v_ref, f32[1024,3072]{1,0:T(8,128)} %fusion.51.q_ref.k_ref.v_ref, f32[1024,3072]{1,0:T(8,128)} %fusion.51.q_ref.k_ref.v_ref, ...), custom_call_target="tpu_custom_call" | custom-call | tf_op jit(solution)/shard_map/attention_forward/pallas_call | solution.py:453
  241.9 7.0 fusion.44
  248.9 2.0 copy-done.1
  251.6 17.6 %fusion.37 = f32[1024,4096]{1,0:T(8,128)} fusion(bf16[1024,4096]{1,0:T(8,128)(2,1)} %all-gather.3.cloned.1.call-done, f32[1024,1024]{1,0:T(8,128)} %copy-done.1, f32[1024]{0:T(1024)S(1)} %bitcast.117, f32[1024]{0:T(1024)S(1)} %bitcast.119, f32[1024]{0:T(1024)S(1)} %bitcast.92, f32[1024]{0:T(1024)S(1)} %bitcast.96, f32[1024]{0:T(1024)S(1)} %fusion.27, ...), kind=kOutput, calls=%fused_computation.117 | convolution fusion | flops 8598323200 | bytes 29385728 | tf_op jit(solution)/shard_map/dot_general | solution.py:46
  269.1 18.0 %fusion.42 = (f32[1024]{0:T(1024)S(1)}, f32[1024,1024]{1,0:T(8,128)S(1)}, f32[1024,1024]{1,0:T(8,128)}) fusion(f32[1024,1024]{1,0:T(8,128)S(1)} %copy-done.2, f32[1024]{0:T(1024)S(1)} %bitcast.114, f32[1024]{0:T(1024)S(1)} %bitcast.111, pred[1024]{0:T(1024)(128)(4,1)S(1)} %get-tuple-element.260, bf16[4096,1024]{1,0:T(8,128)(2,1)} %bitcast.131, ...), kind=kOutput, calls=%fused_computation.122 | convolution fusion | flops 8631876608 | bytes 37762048 | tf_op jit(solution)/shard_map/dot_general | solution.py:46
  287.2 2.1 copy-done.8
  289.8 13.1 %fusion.50 = (f32[1024]{0:T(1024)S(1)}, f32[1024,4096]{1,0:T(8,128)S(1)}) fusion(bf16[1024,4096]{1,0:T(8,128)(2,1)} %all-gather.5.cloned.1.call-done, f32[1024,1024]{1,0:T(8,128)} %copy-done.8, f32[1024]{0:T(1024)S(1)} %bitcast.100, f32[1024]{0:T(1024)S(1)} %fusion.28, f32[1024]{0:T(1024)S(1)} %broadcast_multiply_fusion), kind=kOutput, calls=%fused_computation.128 | convolution fusion | flops 8598322176 | bytes 29376512 | tf_op jit(solution)/shard_map/dot_general | solution.py:46
  302.9 5.6 select_reduce_fusion
  308.5 1.3 multiply_reduce_fusion.6
  309.8 7.9 %multiply_convert_fusion = bf16[1024,4096]{1,0:T(8,128)(2,1)} fusion(f32[1024,4096]{1,0:T(8,128)S(1)} %get-tuple-element.295, f32[1024]{0:T(1024)S(1)} %get-tuple-element.283, s32[1024]{0:T(1024)S(1)} %copy-done.28, f32[1024]{0:T(1024)S(1)} %get-tuple-element.257), kind=kLoop, calls=%fused_computation.10 | loop fusion | flops 25165824 | bytes 25178112 | tf_op jit(solution)/shard_map/convert_element_type | solution.py:1242
  317.7 15.2 %multiply_reduce_fusion = (f32[1024]{0:T(1024)}, f32[1024]{0:T(1024)S(1)}, f32[1024,1024]{1,0:T(8,128)S(1)}) fusion(f32[1024,1024]{1,0:T(8,128)S(1)} %copy-done.9, f32[1024]{0:T(1024)S(1)} %fusion.28, f32[1024]{0:T(1024)S(1)} %broadcast_multiply_fusion, f32[1024]{0:T(1024)S(1)} %bitcast.101, bf16[1024,4096]{1,0:T(8,128)(2,1)} %multiply_convert_fusion, ...), kind=kOutput, calls=%fused_computation.27 | convolution fusion | flops 8597272576 | bytes 25186304 | tf_op jit(solution)/shard_map/dot_general | solution.py:46
  332.9 1.7 fusion.41
  334.7 25.7 %fusion.6 = bf16[1024,4096]{1,0:T(8,128)(2,1)} fusion(f32[1024,4096]{1,0:T(8,128)} %fusion.37, bf16[4096,1024]{1,0:T(8,128)(2,1)} %bitcast.132, f32[1024,1024]{1,0:T(8,128)S(1)} %get-tuple-element.264, f32[1024]{0:T(1024)S(1)} %negate_multiply_fusion.1, f32[1024]{0:T(1024)S(1)} %bitcast.115, f32[1024]{0:T(1024)S(1)} %bitcast.112, ...), kind=kOutput, calls=%fused_computation.8 | convolution fusion | flops 8678014976 | bytes 37762048 | tf_op jit(solution)/shard_map/dot_general | solution.py:46
  360.4 19.6 %select_reduce_fusion.2 = (f32[1024]{0:T(1024)S(1)}, f32[1024]{0:T(1024)S(1)}, f32[1024]{0:T(1024)S(1)}, f32[1024]{0:T(1024)S(1)}, f32[1024]{0:T(1024)S(1)}, /*i...) fusion(pred[1024]{0:T(1024)(128)(4,1)S(1)} %get-tuple-element.260, f32[1024]{0:T(1024)S(1)} %bitcast.93, ...), kind=kOutput, calls=%fused_computation.29 | convolution fusion | flops 8612996096 | bytes 33604608 | tf_op jit(solution)/shard_map/dot_general | solution.py:46
  380.1 4.7 fusion.40
  384.8 1.2 copy-done.7
  386.0 1.9 select_reduce_fusion.8
  388.0 3.9 convolution_convert_fusion.4
  391.8 3.7 convolution_convert_fusion.3.m_ref
  395.6 15.2 %convolution_convert_fusion.2 = bf16[1024,4096]{1,0:T(8,128)(2,1)} fusion(bf16[1024,4096]{1,0:T(8,128)(2,1)} %multiply_convert_fusion, f32[1024,1024]{1,0:T(8,128)S(1)} %copy-done.11, f32[1024]{0:T(1024)S(1)} %bitcast.103, f32[1024]{0:T(1024)S(1)} %fusion.28, f32[1024]{0:T(1024)S(1)} %broadcast_multiply_fusion), kind=kOutput, calls=%fused_computation.16 | convolution fusion | flops 8598323200 | bytes 20983808 | tf_op jit(solution)/shard_map/dot_general | solution.py:46
  410.7 15.7 %convolution_convert_fusion.1 = bf16[1024,4096]{1,0:T(8,128)(2,1)} fusion(bf16[1024,4096]{1,0:T(8,128)(2,1)} %fusion.6, f32[1024,1024]{1,0:T(8,128)S(1)} %copy-done.3, f32[1024]{0:T(1024)S(1)} %bitcast.118, f32[1024]{0:T(1024)S(1)} %bitcast.120, f32[1024]{0:T(1024)S(1)} %bitcast.95, f32[1024]{0:T(1024)S(1)} %bitcast.99, f32[1024]{0:T(1024)S(1)} %fusion.27, ...), kind=kOutput, calls=%fused_computation.15 | convolution fusion | flops 8602517504 | bytes 20997120 | tf_op jit(solution)/shard_map/dot_general | solution.py:46
  426.4 18.4 %convolution_convert_fusion = bf16[4096,1024]{1,0:T(8,128)(2,1)} fusion(f32[1024,1024]{1,0:T(8,128)S(1)} %copy-done.7, f32[1024]{0:T(1024)S(1)} %negate_multiply_fusion.1, f32[1024]{0:T(1024)S(1)} %bitcast.116, f32[1024]{0:T(1024)S(1)} %bitcast.113, pred[1024]{0:T(1024)(128)(4,1)S(1)} %get-tuple-element.260, f32[1024,4096]{1,0:T(8,128)} %fusion.37), kind=kOutput, calls=%fused_computation.14 | convolution fusion | flops 8636071936 | bytes 29373440 | tf_op jit(solution)/shard_map/dot_general | solution.py:46
  445.0 130.5 %attention_backward.1 = (bf16[3,1024,1024]{2,1,0:T(8,128)(2,1)}, f32[8,1024]{1,0:T(8,128)}, f32[24,32,512]{2,1,0:T(8,128)}) custom-call(f32[1024,3072]{1,0:T(8,128)} %fusion.51.q_ref.k_ref.v_ref, f32[1024,3072]{1,0:T(8,128)} %fusion.51.q_ref.k_ref.v_ref, f32[1024,3072]{1,0:T(8,128)} %fusion.51.q_ref.k_ref.v_ref, ...), custom_call_target="tpu_custom_call" | custom-call | tf_op jit(solution)/shard_map/attention_backward/pallas_call | solution.py:578
  575.5 0.8 slice.224
  577.0 112.2 %last_scatter.1 = (f32[8,32,512]{2,1,0:T(8,128)}, f32[32,128]{1,0:T(8,128)}, f32[32,1152]{1,0:T(8,128)}, f32[32,6144]{1,0:T(8,128)}, f32[10,32,1]{2,1,0:T(8,128)...) custom-call(bf16[2,2,2,2,2,32,1024]{6,5,4,3,2,1,0:T(8,128)(2,1)} %bitcast.80, bf16[1024,3072]{1,0:T(8,128)(2,1)} %bitcast.74, ...), custom_call_target="tpu_custom_call" | custom-call | tf_op jit(solution)/shard_map/last_scatter/pallas_call | solution.py:964
  689.2 1.5 slice_reduce_fusion.2
  690.7 0.9 slice_reduce_fusion
  691.7 0.9 slice.244
  692.6 0.7 slice_reduce_fusion.8
  695.0 6.0 weight_step.1
  701.1 1.4 copy.133
  702.5 1.4 copy.134
  703.9 1.4 copy.135
  705.9 0.7 pad_maximum_fusion.1
  (160 shorter events, 15.0 us)
Async XLA Ops:
  7.2 244.3 %all-gather.3.cloned.1.call-start = ((), (), s32[]{:S(2)}) async-start(), calls=%async_computation | async-start | bytes 8650752 | tf_op jit(solution)/shard_map/all_gather | solution.py:1080
  9.0 280.8 %all-gather.5.cloned.1.call-start = ((), (), s32[]{:S(2)}) async-start(), calls=%async_computation.1 | async-start | bytes 8650752 | tf_op jit(solution)/shard_map/all_gather | solution.py:1080
  21.9 0.7 copy-start.30
  51.3 8.8 %copy-start.13 = (f32[32,6144]{1,0:T(8,128)S(1)}, f32[32,6144]{1,0:T(8,128)}, u32[]{:S(2)}) copy-start(f32[32,6144]{1,0:T(8,128)} %ada_ref.3) | copy-start | bytes 2359300
  56.8 5.2 copy-start.16
  58.7 76.7 %copy-start.18 = (f32[32,1024]{1,0:T(8,128)S(1)}, f32[32,1024]{1,0:T(8,128)}, u32[]{:S(2)}) copy-start(f32[32,1024]{1,0:T(8,128)} %out_master.3) | copy-start | bytes 393220
  59.5 0.6 copy-start.21
  59.5 76.5 %copy-start.14 = (f32[128,1024]{1,0:T(8,128)S(1)}, f32[128,1024]{1,0:T(8,128)}, u32[]{:S(2)}) copy-start(f32[128,1024]{1,0:T(8,128)} %down_master.3) | copy-start | bytes 1572868
  60.4 76.3 %copy-start.19 = (bf16[1024,32]{0,1:T(8,128)(2,1)S(1)}, bf16[1024,32]{0,1:T(8,128)(2,1)}, u32[]{:S(2)}) copy-start(bf16[1024,32]{0,1:T(8,128)(2,1)} %param.28) | copy-start | bytes 196612
  60.4 77.4 %copy-start.27 = (s32[1024]{0:T(1024)S(1)}, s32[1024]{0:T(1024)}, u32[]{:S(2)}) copy-start(s32[1024]{0:T(1024)} %param.30) | copy-start | bytes 12292
  60.5 79.0 %copy-start.39 = (f32[32]{0:T(128)S(1)}, f32[32]{0:T(128)}, u32[]{:S(2)}) copy-start(f32[32]{0:T(128)} %param.43) | copy-start | bytes 388
  60.5 79.0 %copy-start.40 = (f32[32]{0:T(128)S(1)}, f32[32]{0:T(128)}, u32[]{:S(2)}) copy-start(f32[32]{0:T(128)} %param.44) | copy-start | bytes 388
  60.5 79.0 %copy-start.41 = (f32[32]{0:T(128)S(1)}, f32[32]{0:T(128)}, u32[]{:S(2)}) copy-start(f32[32]{0:T(128)} %param.45) | copy-start | bytes 388
  60.5 79.0 %copy-start.42 = (f32[32]{0:T(128)S(1)}, f32[32]{0:T(128)}, u32[]{:S(2)}) copy-start(f32[32]{0:T(128)} %param.46) | copy-start | bytes 388
  60.5 79.0 %copy-start.43 = (f32[32]{0:T(128)S(1)}, f32[32]{0:T(128)}, u32[]{:S(2)}) copy-start(f32[32]{0:T(128)} %param.47) | copy-start | bytes 388
  60.5 79.0 %copy-start.44 = (f32[32]{0:T(128)S(1)}, f32[32]{0:T(128)}, u32[]{:S(2)}) copy-start(f32[32]{0:T(128)} %param.49) | copy-start | bytes 388
  60.5 79.0 %copy-start.45 = (f32[128]{0:T(128)S(1)}, f32[128]{0:T(128)}, u32[]{:S(2)}) copy-start(f32[128]{0:T(128)} %param.48) | copy-start | bytes 1540
  60.5 79.9 %copy-start.31 = (f32[32,9]{0,1:T(8,128)S(1)}, f32[32,9]{0,1:T(8,128)}, u32[]{:S(2)}) copy-start(f32[32,9]{0,1:T(8,128)} %param.50) | copy-start | bytes 3460
  60.6 80.6 %slice-start.2 = ((f32[20498]{0:T(1024)}), f32[1042]{0:T(1024)S(1)}, s32[]{:S(2)}) async-start(f32[20498]{0:T(1024)} %param.51), calls=%async_computation.4 | async-start | bytes 16384 | tf_op jit(solution)/shard_map/slice | solution.py:1292
  60.6 82.0 %copy-start.37 = (s32[1024]{0:T(1024)S(1)}, s32[1024]{0:T(1024)}, u32[]{:S(2)}) copy-start(s32[1024]{0:T(1024)} %param.31) | copy-start | bytes 12292
  141.2 4.2 copy-start
  145.3 5.1 copy-start.22
  145.4 96.5 %copy-start.23 = (f32[1,1024]{1,0:T(1,128)}, f32[1,1024]{1,0:T(1,128)S(1)}, u32[]{:S(2)}) copy-start(f32[1,1024]{1,0:T(1,128)S(1)} %get-tuple-element.275) | copy-start | bytes 12292
  145.4 96.5 %copy-start.25 = (f32[1,1024]{1,0:T(1,128)}, f32[1,1024]{1,0:T(1,128)S(1)}, u32[]{:S(2)}) copy-start(f32[1,1024]{1,0:T(1,128)S(1)} %get-tuple-element.276) | copy-start | bytes 12292
  145.4 106.1 %copy-start.32 = (f32[1,1024]{1,0:T(1,128)}, f32[1,1024]{1,0:T(1,128)S(1)}, u32[]{:S(2)}) copy-start(f32[1,1024]{1,0:T(1,128)S(1)} %get-tuple-element.270) | copy-start | bytes 12292
  145.4 106.1 %copy-start.34 = (f32[1,1024]{1,0:T(1,128)}, f32[1,1024]{1,0:T(1,128)S(1)}, u32[]{:S(2)}) copy-start(f32[1,1024]{1,0:T(1,128)S(1)} %get-tuple-element.271) | copy-start | bytes 12292
  145.4 9.8 %slice-start = ((s8[6291456]{0:T(1024)(128)(4,1)}), s8[4194304]{0:T(1024)(128)(4,1)S(1)}, s32[]{:S(2)}) async-start(s8[6291456]{0:T(1024)(128)(4,1)} %bitcast.75), calls=%async_computation.2 | async-start | bytes 8388608
  150.4 4.8 copy-start.12
  150.4 4.8 slice-start.1
  248.9 2.0 copy-start.1
  251.5 17.6 %copy-start.2 = (f32[1024,1024]{1,0:T(8,128)S(1)}, f32[1024,1024]{1,0:T(8,128)}, u32[]{:S(2)}) copy-start(f32[1024,1024]{1,0:T(8,128)} %copy-done.1) | copy-start | bytes 12582916
  287.1 2.1 copy-start.8
  289.8 13.1 %copy-start.28 = (s32[1024]{0:T(1024)S(1)}, s32[1024]{0:T(1024)}, u32[]{:S(2)}) copy-start(s32[1024]{0:T(1024)} %param.33) | copy-start | bytes 12292
  302.9 5.6 copy-start.29
  309.8 7.9 %copy-start.9 = (f32[1024,1024]{1,0:T(8,128)S(1)}, f32[1024,1024]{1,0:T(8,128)}, u32[]{:S(2)}) copy-start(f32[1024,1024]{1,0:T(8,128)} %copy-done.8) | copy-start | bytes 12582916
  317.7 15.2 %copy-start.10 = (f32[1024,1024]{1,0:T(8,128)S(1)}, f32[1024,1024]{1,0:T(8,128)}, u32[]{:S(2)}) copy-start(f32[1024,1024]{1,0:T(8,128)} %copy-done.8) | copy-start | bytes 12582916
  334.6 25.8 %copy-start.6 = (f32[1024,1024]{1,0:T(8,128)}, f32[1024,1024]{1,0:T(8,128)S(1)}, u32[]{:S(2)}) copy-start(f32[1024,1024]{1,0:T(8,128)S(1)} %get-tuple-element.264) | copy-start | bytes 12582916
  380.1 4.7 copy-start.4
  380.1 5.9 copy-start.7
  386.0 1.9 copy-start.15
  386.0 2.0 copy-start.24
  386.0 2.0 copy-start.26
  387.9 3.9 copy-start.5
  388.0 3.9 copy-start.17
  391.8 3.7 copy-start.11
  395.6 15.2 %copy-start.3 = (f32[1024,1024]{1,0:T(8,128)S(1)}, f32[1024,1024]{1,0:T(8,128)}, u32[]{:S(2)}) copy-start(f32[1024,1024]{1,0:T(8,128)} %copy-done.1) | copy-start | bytes 12582916
  395.6 15.2 %copy-start.33 = (f32[1,1024]{1,0:T(1,128)S(1)}, f32[1,1024]{1,0:T(1,128)}, u32[]{:S(2)}) copy-start(f32[1,1024]{1,0:T(1,128)} %copy-done.32) | copy-start | bytes 12292
  395.6 15.2 %copy-start.35 = (f32[1,1024]{1,0:T(1,128)S(1)}, f32[1,1024]{1,0:T(1,128)}, u32[]{:S(2)}) copy-start(f32[1,1024]{1,0:T(1,128)} %copy-done.34) | copy-start | bytes 12292
  444.9 131.3 %copy-start.36 = (f32[1024]{0:T(1024)S(1)}, f32[1024]{0:T(1024)}, u32[]{:S(2)}) copy-start(f32[1024]{0:T(1024)} %get-tuple-element.239) | copy-start | bytes 12292
  444.9 131.3 %copy-start.38 = (f32[8]{0:T(128)S(1)}, f32[8]{0:T(128)}, u32[]{:S(2)}) copy-start(f32[8]{0:T(128)} %pad.23.clone) | copy-start | bytes 100
  576.2 0.7 copy-start.20
Sparse Core Ops, SparseCore 0:
  11.5 94.4 all-gather.2
  109.4 84.3 all-gather.4

commit v3 on v2

--- a/solution.py
+++ b/solution.py
@@ -32,12 +32,12 @@
 FIVE = (2, 2, 2, 2, 2)
 DIMS = ("w", "u", "y", "x", "c")
 SCATTER_ORDERS = (("c", "x", "y", "w", "u"), ("c", "y", "x", "w", "u"))
-GATHER_ORDERS = (("u", "w", "y", "x", "c"), ("u", "w", "x", "y", "c"))
+GATHER_ORDERS = tuple(order[::-1] for order in SCATTER_ORDERS)
 SCORE_SCALE = HEAD_DIM ** (-0.5)
 EXP_SCALE = SCORE_SCALE * math.log2(math.e)
 VMEM_GRANT = 58 * 1024 * 1024
 FIRST_WIDTH, FIRST_LAG = 256, 1
-ATTEND_WIDTH, ATTEND_LAG = 128, 2
+ATTEND_WIDTH, ATTEND_LAG = 128, 3
 BACK_WIDTH, BACK_LAG = 256, 2
 LAST_WIDTH, LAST_LAG = 256, 2
 
@@ -252,82 +252,264 @@
     return pl.ds(pl.multiple_of(start, 128), size)
 
 
-def small_gather_kernel(rows_ref, tags_ref, rows_full, tags_full, *sems):
+def slot_labels(tags_full, order):
+    pieces = []
+    for number in range(32):
+        bits = {dim: (number >> (4 - at)) & 1 for at, dim in enumerate(order)}
+        pieces.append(tags_full[bits["w"], bits["u"], bits["y"], bits["x"], bits["c"], 0:2])
+    return jnp.concatenate(pieces, axis=0)
+
+
+def hot_of(labels):
+    lanes = lax.broadcasted_iota(jnp.int32, labels.shape, 1).astype(jnp.float32)
+    blocks = [jnp.where(labels == lanes + 128.0 * at, 1.0, 0.0) for at in range(9)]
+    return jnp.concatenate(blocks, axis=1).astype(jnp.bfloat16)
+
+
+def begin_kernel(
+    rows_ref,
+    tags_ref,
+    tables_ref,
+    ada_ref,
+    qkv_ref,
+    out_own_ref,
+    codes_ref,
+    token_columns,
+    token_rows,
+    projected_ref,
+    qkv_out,
+    out_full,
+    embedded_ref,
+    normed_ref,
+    modulation_ref,
+    vectors_ref,
+    hot_ref,
+    cond_ref,
+    act_ref,
+    tag_sums,
+    bias_ref,
+    turned_ref,
+    *scratch,
+):
     place = Place()
     place.meet()
-    gather = Gather(
+    bit = place.bit
+    (
+        rows_full,
+        tags_full,
+        own_qkv,
+        own_out,
+        qkv_full,
+        part,
+        unit,
+        staged,
+        copy_sems,
+        mod_sends,
+        mod_recvs,
+    ) = scratch[:11]
+    mod_land, mod_sums = scratch[11:16], scratch[16:21]
+    own_qkv[...] = qkv_ref[...].astype(jnp.bfloat16)
+    own_out[...] = out_own_ref[...].astype(jnp.bfloat16)
+    small = Gather(
         place,
         [(0, 1, lambda j, p: (rows_ref, tags_ref)[p], lambda j, p, r: (rows_full, tags_full)[p].at[r])],
-        *sems,
-    )
-    for t in range(6):
-        gather.step(t)
-
-
-def small_gather(rows, tags):
-    return pl.pallas_call(
-        small_gather_kernel,
-        out_shape=(
-            jax.ShapeDtypeStruct(FIVE + rows.shape, rows.dtype),
-            jax.ShapeDtypeStruct(FIVE + tags.shape, tags.dtype),
-        ),
-        in_specs=[WHOLE, WHOLE],
-        out_specs=(WHOLE, WHOLE),
-        scratch_shapes=Gather.scratch(),
-        compiler_params=params(0),
-        name="small_gather",
-    )(rows, tags)
-
-
-def first_kernel(part_ref, own_ref, mod_ref, full_ref, *scratch):
-    place = Place()
-    place.meet()
-    rows = part_ref.shape[5] // 2
+        *scratch[21:24],
+    )
     width = FIRST_WIDTH
-
-    def store(j, parity, total):
-        mod_ref[pl.ds(parity * rows, rows)] = total
-
-    scatter = Scatter(
-        place,
-        [(0, 1, lambda j, p, core: part_ref.at[:, :, :, :, core, pl.ds(p * rows, rows)])],
-        store,
-        scratch[:13],
-    )
-    pairs = own_ref.shape[1] // (2 * width)
+    pairs = 3 * D // (2 * width)
+
+    def of_weight(own, full, first):
+        return (
+            lambda j, p: own.at[:, columns((2 * (j - first) + p) * width, width)],
+            lambda j, p, r: full.at[r + (slice(None), columns((2 * (j - first) + p) * width, width))],
+        )
+
     gather = Gather(
         place,
         [
-            (
-                0,
-                pairs,
-                lambda j, p: own_ref.at[:, columns((2 * j + p) * width, width)],
-                lambda j, p, r: full_ref.at[r + (slice(None), columns((2 * j + p) * width, width))],
+            (0, pairs) + of_weight(own_qkv, qkv_full, 0),
+            (pairs, pairs + D // (2 * width)) + of_weight(own_out, out_full, pairs),
+        ],
+        *scratch[24:27],
+        lag=FIRST_LAG,
+    )
+    lanes = 3 * D
+    orders = (("x", "y", "w", "u", "c"), ("y", "x", "w", "u", "c"))
+
+    def mod_half(stage, parity, other):
+        dim = orders[parity][stage]
+        value = 1 - bit[dim] if other else bit[dim]
+        left = [d for d in ("x", "y", "w") if d not in orders[parity][:stage]]
+        return tuple(value if d == dim else slice(None) for d in left)
+
+    def mod_view(stage, parity, other):
+        if stage == 0:
+            at = pl.ds(parity * lanes, lanes)
+            return part, mod_half(0, parity, other) + (slice(None), at)
+        if stage < 3:
+            return mod_sums[stage - 1], (parity,) + mod_half(stage, parity, other)
+        return mod_sums[stage - 1], (parity,)
+
+    def mod_copy(stage, parity):
+        ref, at = mod_view(stage, parity, True)
+        return place.send(
+            ref.at[at],
+            mod_land[stage].at[parity],
+            mod_sends.at[stage, parity],
+            mod_recvs.at[stage, parity],
+            orders[parity][stage],
+        )
+
+    def mod_step(stage):
+        for parity in range(2):
+            if stage:
+                mod_copy(stage - 1, parity).wait()
+                ref, at = mod_view(stage - 1, parity, False)
+                mod_sums[stage - 1][parity] = ref[at] + mod_land[stage - 1][parity]
+            if stage < 5:
+                mod_copy(stage, parity).start()
+
+    def mask(query, key, same):
+        usable = (query[0] == key[0]) & (key[1] <= query[1]) & ((key[2] > 0.5) | same)
+        return jnp.where(usable, 0.0, MASK_VALUE)
+
+    tokens = codes_ref.shape[0]
+    block = tokens // 4
+
+    def masks(index, size):
+        at = slice(index * size, (index + 1) * size)
+        shape = (size, tokens)
+        same = lax.broadcasted_iota(jnp.int32, shape, 0) + index * size == lax.broadcasted_iota(
+            jnp.int32, shape, 1
+        )
+        down = [token_columns[at, i : i + 1] for i in range(3)]
+        across = [token_rows[i : i + 1] for i in range(3)]
+        bias_ref[at] = mask(down, across, same)
+        turned_ref[at] = mask(across, down, same)
+
+    def embed(index):
+        at = slice(index * block, (index + 1) * block)
+        values = dot_last(codes_ref[at], rows_full[...].reshape(D, 128))
+        embedded_ref[at] = values
+        center = values - jnp.sum(values, axis=1, keepdims=True) * (1.0 / D)
+        rate = lax.rsqrt(jnp.sum(center * center, axis=1, keepdims=True) * (1.0 / D) + NORM_EPSILON)
+        unit[at] = center * rate
+
+    masking = iter(range(8))
+    steps = iter(range(gather.steps))
+    for t in range(6):
+        small.step(t)
+        gather.step(next(steps))
+        if t < 5:
+            masks(next(masking), tokens // 8)
+    tag_sums[...] = jnp.sum(tags_full[...].reshape(32, 8, 128), axis=0)
+    low = jnp.bfloat16
+    class_tables = tables_ref[:, :D].astype(low)
+    for order, target in ((DIMS, None), (("x", "y", "w", "u", "c"), part)):
+        hot = hot_of(slot_labels(tags_full, order))
+        cond = dot_last(hot[:, :D], class_tables)
+        act = (cond / (1.0 + jnp.exp(-cond))).astype(low)
+        if target is None:
+            hot_ref[...], cond_ref[...], act_ref[...] = hot, cond, act
+        else:
+            target[...] = dot_plain(act, ada_ref[...].astype(low)).reshape(2, 2, 2, 8, 6 * D)
+    vectors_ref[...] = rows_full[...].reshape(D, 128).astype(jnp.float32).T[0:16]
+    for stage in range(6):
+        mod_step(stage)
+        for step in steps:
+            gather.step(step)
+            break
+        if stage < 4:
+            embed(stage)
+        for index in masking:
+            masks(index, tokens // 8)
+            break
+    for step in steps:
+        gather.step(step)
+    store_qkv = pltpu.make_async_copy(qkv_full, qkv_out, copy_sems.at[2])
+    store_qkv.start()
+    spot = 4 * bit["u"] + 2 * bit["c"]
+    row_ids = lax.broadcasted_iota(jnp.int32, (8, D), 0)
+    for kind in range(6):
+        at = (kind % 3) * D
+        group = mod_sums[4][kind // 3, :, at : at + D]
+        for slot in range(2):
+            row = jnp.sum(jnp.where(row_ids == spot + slot, group, 0.0), axis=0, keepdims=True)
+            modulation_ref[slot : slot + 1, kind * D : (kind + 1) * D] = row + vectors_ref[kind : kind + 1]
+    stores = []
+    for index in range(4):
+        at = slice(index * block, (index + 1) * block)
+        other = token_columns[at, 0:1] > 0.5
+        scale = jnp.where(other, modulation_ref[1:2, 2 * D : 3 * D], modulation_ref[0:1, 2 * D : 3 * D])
+        shift = jnp.where(other, modulation_ref[1:2, 4 * D : 5 * D], modulation_ref[0:1, 4 * D : 5 * D])
+        normed = (unit[at] * (1.0 + scale) + shift).astype(low)
+        normed_ref[at] = normed
+        if index >= 2:
+            stores[index - 2].wait()
+        for column in range(0, 3 * D, 512):
+            weight = qkv_full[:, :, :, :, :, :, column : column + 512].reshape(D, 512)
+            staged[index % 2, :, column : column + 512] = dot_plain(normed, weight)
+        stores.append(
+            pltpu.make_async_copy(
+                staged.at[index % 2], projected_ref.at[pl.ds(index * block, block)], copy_sems.at[index % 2]
             )
-        ],
-        *scratch[13:],
-        lag=FIRST_LAG,
-    )
-    for t in range(6):
-        scatter.step(t)
-        gather.step(t)
-    for t in range(6, gather.steps):
-        gather.step(t)
-
-
-def first_exchange(part, own):
+        )
+        stores[index].start()
+    stores[2].wait()
+    stores[3].wait()
+    store_qkv.wait()
+
+
+def begin(rows, tags, tables, ada_weight, qkv_weight, out_weight, codes, token_columns, token_rows):
+    depth = rows.shape[0]
+    tokens = codes.shape[0]
+    f32, low = jnp.float32, jnp.bfloat16
+    dma = pltpu.SemaphoreType.DMA
+    lanes = 3 * D
+    lands = [
+        pltpu.VMEM((2, 2, 2, 8, lanes), f32),
+        pltpu.VMEM((2, 2, 8, lanes), f32),
+    ] + [pltpu.VMEM((2, 8, lanes), f32)] * 3
+    shape = jax.ShapeDtypeStruct
     return pl.pallas_call(
-        first_kernel,
+        begin_kernel,
         out_shape=(
-            jax.ShapeDtypeStruct(part.shape[5:], jnp.float32),
-            jax.ShapeDtypeStruct(FIVE + own.shape, own.dtype),
+            shape((tokens, 3 * D), f32),
+            shape(FIVE + (depth, 3 * D), low),
+            shape(FIVE + (depth, D), low),
+            shape((tokens, D), f32),
+            shape((tokens, D), low),
+            shape((2, 6 * D), f32),
+            shape((16, D), f32),
+            shape((64, 1152), low),
+            shape((64, depth), f32),
+            shape((64, depth), low),
+            shape((8, 128), f32),
+            shape((tokens, tokens), f32),
+            shape((tokens, tokens), f32),
         ),
-        in_specs=[ANY, ANY],
-        out_specs=(WHOLE, ANY),
-        scratch_shapes=Scatter.scratch((part.shape[5] // 2, 128), jnp.float32) + Gather.scratch(FIRST_LAG),
-        compiler_params=params(1),
-        name="modulation_scatter_qkv_gather",
-    )(part, own)
+        in_specs=[WHOLE] * 9,
+        out_specs=(ANY, ANY, ANY) + (WHOLE,) * 10,
+        scratch_shapes=[
+            pltpu.VMEM(FIVE + (depth, 128), low),
+            pltpu.VMEM(FIVE + (8, 128), f32),
+            pltpu.VMEM((depth, 3 * D), low),
+            pltpu.VMEM((depth, D), low),
+            pltpu.VMEM(FIVE + (depth, 3 * D), low),
+            pltpu.VMEM((2, 2, 2, 8, 6 * D), f32),
+            pltpu.VMEM((tokens, D), f32),
+            pltpu.VMEM((2, tokens // 4, 3 * D), f32),
+            dma((3,)),
+            dma((5, 2)),
+            dma((5, 2)),
+        ]
+        + lands
+        + lands
+        + Gather.scratch()
+        + Gather.scratch(FIRST_LAG),
+        compiler_params=params(0),
+        name="begin",
+    )(rows, tags, tables, ada_weight, qkv_weight, out_weight, codes, token_columns, token_rows)
 
 
 def head_mean(values):
@@ -364,68 +546,60 @@
 
 def attend_kernel(linked, q_ref, k_ref, v_ref, gain_ref, bias_ref, *refs):
     if linked:
-        out_own, down_own, mixed_ref, out_full, down_full, qn, kn, vn = refs[:8]
+        down_own, mixed_ref, exact_ref, total_ref, down_full, qn, kn, vn = refs[:8]
         sems = refs[8:]
         place = Place()
         width = ATTEND_WIDTH
-        split = out_own.shape[1] // (2 * width)
-        depth = out_own.shape[0]
-        parts = down_own.shape[0] // depth
-
-        def spread(j):
-            return lax.div(j - split, split), lax.rem(j - split, split)
+        split = D // (2 * width)
+        depth = down_full.shape[6]
+        parts = down_full.shape[5]
 
         def down_source(j, p):
-            part, column = spread(j)
+            part, column = lax.div(j, split), lax.rem(j, split)
             return down_own.at[
                 pl.ds(pl.multiple_of(part * depth, depth), depth), columns((2 * column + p) * width, width)
             ]
 
         def down_target(j, p, r):
-            part, column = spread(j)
+            part, column = lax.div(j, split), lax.rem(j, split)
             return down_full.at[r + (part, slice(None), columns((2 * column + p) * width, width))]
 
-        gather = Gather(
-            place,
-            [
-                (
-                    0,
-                    split,
-                    lambda j, p: out_own.at[:, columns((2 * j + p) * width, width)],
-                    lambda j, p, r: out_full.at[r + (slice(None), columns((2 * j + p) * width, width))],
-                ),
-                (split, split + split * parts, down_source, down_target),
-            ],
-            *sems,
-            lag=ATTEND_LAG,
-        )
+        gather = Gather(place, [(0, split * parts, down_source, down_target)], *sems, lag=ATTEND_LAG)
         pl.when(pl.program_id(0) == 0)(place.meet)
     else:
-        mixed_ref, qn, kn, vn = refs
+        mixed_ref, exact_ref, total_ref, qn, kn, vn = refs
     qn[...] = normed_head(q_ref[...], gain_ref[0:1])
     kn[...] = normed_head(k_ref[...], gain_ref[1:2])
     vn[...] = v_ref[...].astype(jnp.bfloat16)
-    size = q_ref.shape[0] // UNITS
-
-    @pl.loop(0, UNITS)
-    def unit(u):
-        if linked:
-            gather.step(pl.program_id(0) * UNITS + u)
-        rows = pl.ds(pl.multiple_of(u * size, size), size)
-        both = []
-        for head in range(2):
-            scores = dot_last(of_head(qn[rows], head), kn[...]) * EXP_SCALE + bias_ref[rows]
-            raised = jnp.exp2(scores)
-            share = 1.0 / jnp.sum(raised, axis=1, keepdims=True)
-            both.append(dot_plain((raised * share).astype(jnp.bfloat16), vn[...]))
-        low_lane = lax.broadcasted_iota(jnp.int32, both[0].shape, 1) < HEAD_DIM
-        mixed_ref[rows] = jnp.where(low_lane, both[0], both[1]).astype(jnp.bfloat16)
+    tokens = q_ref.shape[0]
+    both, sums = [], []
+    for head in range(2):
+        query = of_head(qn[...], head)
+        mixed = jnp.zeros((tokens, 128), jnp.float32)
+        lanes = jnp.zeros((tokens, 128), jnp.float32)
+        for order in range(UNITS // 2):
+            if linked:
+                gather.step(pl.program_id(0) * UNITS + head * (UNITS // 2) + order)
+            size = tokens // (UNITS // 2)
+            keys = slice(order * size, (order + 1) * size)
+            raised = jnp.exp2(dot_last(query, kn[keys]) * EXP_SCALE + bias_ref[:, keys])
+            for lane in range(0, size, 128):
+                lanes = lanes + raised[:, lane : lane + 128]
+            mixed = mixed + dot_plain(raised.astype(jnp.bfloat16), vn[keys])
+        total = jnp.sum(lanes, axis=1, keepdims=True)
+        both.append(mixed * (1.0 / total))
+        sums.append(total)
+    low_lane = lax.broadcasted_iota(jnp.int32, both[0].shape, 1) < HEAD_DIM
+    exact = jnp.where(low_lane, both[0], both[1])
+    mixed_ref[...] = exact.astype(jnp.bfloat16)
+    exact_ref[...] = exact
+    total_ref[...] = jnp.log2(jnp.where(low_lane, sums[0], sums[1]))
 
     if linked:
         finish(gather)
 
 
-def attend(projected, gains, bias, out_own=None, down_own=None):
+def attend(projected, gains, bias, down_own=None, depth=None):
     tokens = projected.shape[0]
     pair = pl.BlockSpec((tokens, 128), lambda i: (0, i))
     specs = [
@@ -435,20 +609,16 @@
         pl.BlockSpec((8, 128), lambda i: (0, i)),
         pl.BlockSpec((tokens, tokens), lambda i: (0, 0), pipeline_mode=pl.Buffered(1)),
     ]
-    outs = [jax.ShapeDtypeStruct((tokens, D), jnp.bfloat16)]
-    out_specs = [pair]
+    outs = [jax.ShapeDtypeStruct((tokens, D), kind) for kind in (jnp.bfloat16, jnp.float32, jnp.float32)]
+    out_specs = [pair] * 3
     scratch = [pltpu.VMEM((tokens, 128), jnp.bfloat16)] * 3
     operands = [projected, projected, projected, gains, bias]
-    linked = out_own is not None
+    linked = down_own is not None
     if linked:
-        depth = out_own.shape[0]
-        specs += [ANY, ANY]
-        operands += [out_own, down_own]
-        outs += [
-            jax.ShapeDtypeStruct(FIVE + out_own.shape, jnp.bfloat16),
-            jax.ShapeDtypeStruct(FIVE + (down_own.shape[0] // depth, depth, D), jnp.bfloat16),
-        ]
-        out_specs += [ANY, ANY]
+        specs += [ANY]
+        operands += [down_own]
+        outs += [jax.ShapeDtypeStruct(FIVE + (down_own.shape[0] // depth, depth, D), jnp.bfloat16)]
+        out_specs += [ANY]
         scratch = scratch + Gather.scratch(ATTEND_LAG)
     return pl.pallas_call(
         partial(attend_kernel, linked),
@@ -462,10 +632,10 @@
     )(*operands)
 
 
-def attend_back_kernel(linked, q_ref, k_ref, v_ref, m_ref, gain_ref, bias_ref, *refs):
+def attend_back_kernel(linked, q_ref, k_ref, v_ref, m_ref, exact_ref, total_ref, gain_ref, bias_ref, *refs):
     if linked:
         head_ref, up_ref, down_ref, grad_ref, gain_grad_ref, done_ref = refs[:6]
-        qn, kn, vn, dq, dk, dv = refs[6:12]
+        qn, kn, vn, dk, dv, turned, dq_turned, key_turned = refs[6:14]
         place = Place()
         width = BACK_WIDTH
         wide = up_ref.shape[6] // (2 * width)
@@ -494,44 +664,47 @@
                 (2 * wide, pairs, down_source),
             ],
             store,
-            refs[12:],
+            refs[14:],
             lag=BACK_LAG,
         )
         pl.when(pl.program_id(0) == 0)(place.meet)
     else:
         grad_ref, gain_grad_ref = refs[:2]
-        qn, kn, vn, dq, dk, dv = refs[2:]
+        qn, kn, vn, dk, dv, turned, dq_turned, key_turned = refs[2:]
     qn[...] = normed_head(q_ref[...], gain_ref[0:1])
     kn[...] = normed_head(k_ref[...], gain_ref[1:2])
     vn[...] = v_ref[...].astype(jnp.bfloat16)
-    dk[...] = jnp.zeros_like(dk)
-    dv[...] = jnp.zeros_like(dv)
-    size = q_ref.shape[0] // UNITS
-
-    @pl.loop(0, UNITS)
-    def unit(u):
-        if linked:
-            scatter.step(pl.program_id(0) * UNITS + u)
-        rows = pl.ds(pl.multiple_of(u * size, size), size)
-        query_sum = None
-        for head in range(2):
-            query = of_head(qn[rows], head)
-            mixed = of_head(m_ref[rows], head)
-            raised = jnp.exp2(dot_last(kn[...], query) * EXP_SCALE + bias_ref[:, rows])
-            probs = raised * (1.0 / jnp.sum(raised, axis=0, keepdims=True))
-            prob_grad = dot_last(vn[...], mixed)
-            center = jnp.sum(probs * prob_grad, axis=0, keepdims=True)
+    for head in range(2):
+        key_turned[head] = of_head(kn[...], head).T
+    turned[0] = total_ref[...].T
+    turned[1] = (head_mean(m_ref[...].astype(jnp.float32) * exact_ref[...]) * HEAD_DIM).T
+    tokens = q_ref.shape[0]
+    size = tokens // (UNITS // 2)
+    for head in range(2):
+        query = of_head(qn[...], head)
+        mixed = of_head(m_ref[...], head)
+        at = head * HEAD_DIM
+        total = turned[0, at : at + 1]
+        center = turned[1, at : at + 1]
+        for order in range(UNITS // 2):
+            if linked:
+                scatter.step(pl.program_id(0) * UNITS + head * (UNITS // 2) + order)
+            keys = slice(order * size, (order + 1) * size)
+            scores = dot_last(kn[keys], query) * EXP_SCALE + (bias_ref[keys] - total)
+            probs = jnp.exp2(scores)
+            prob_grad = dot_last(vn[keys], mixed)
             score_grad = (probs * (prob_grad - center)).astype(jnp.bfloat16)
-            dk[...] += dot_plain(score_grad, query)
-            dv[...] += dot_plain(probs.astype(jnp.bfloat16), mixed)
-            part = dot_first(score_grad, of_head(kn[...], head))
-            query_sum = part if query_sum is None else query_sum + part
-        dq[rows] = query_sum
+            key_part = dot_plain(score_grad, query)
+            value_part = dot_plain(probs.astype(jnp.bfloat16), mixed)
+            query_part = dot_plain(key_turned[head, :, keys], score_grad)
+            dk[keys] = key_part if head == 0 else dk[keys] + key_part
+            dv[keys] = value_part if head == 0 else dv[keys] + value_part
+            dq_turned[...] = query_part if head == 0 and order == 0 else dq_turned[...] + query_part
 
     gain_rows = []
-    for place_at, raw_ref, grad in ((0, q_ref, dq), (1, k_ref, dk)):
+    for place_at, raw_ref, grad in ((0, q_ref, dq_turned[...].T), (1, k_ref, dk[...])):
         raw = raw_ref[...]
-        normed_grad = grad[...] * SCORE_SCALE
+        normed_grad = grad * SCORE_SCALE
         rate = lax.rsqrt(head_mean(raw * raw) + NORM_EPSILON)
         scaled = gain_ref[place_at : place_at + 1] * normed_grad
         back = rate * scaled - raw * (rate * rate * rate) * head_mean(raw * scaled)
@@ -543,13 +716,15 @@
         finish(scatter)
 
 
-def attend_back(projected, mixed_grad, gains, bias, head_grad=None, up_grad=None, down_grad=None):
+def attend_back(projected, mixed_grad, exact, totals, gains, bias, head_grad=None, up_grad=None, down_grad=None):
     tokens = projected.shape[0]
     pair = pl.BlockSpec((tokens, 128), lambda i: (0, i))
     specs = [
         pair,
         pl.BlockSpec((tokens, 128), lambda i: (0, i + 8)),
         pl.BlockSpec((tokens, 128), lambda i: (0, i + 16)),
+        pair,
+        pair,
         pair,
         pl.BlockSpec((8, 128), lambda i: (0, i)),
         pl.BlockSpec((tokens, tokens), lambda i: (0, 0), pipeline_mode=pl.Buffered(1)),
@@ -564,8 +739,13 @@
     ]
     scratch = [pltpu.VMEM((tokens, 128), jnp.bfloat16)] * 3 + [
         pltpu.VMEM((tokens, 128), jnp.float32)
-    ] * 3
-    operands = [projected, projected, projected, mixed_grad, gains, bias]
+    ] * 2
+    scratch += [
+        pltpu.VMEM((2, 128, tokens), jnp.float32),
+        pltpu.VMEM((128, tokens), jnp.float32),
+        pltpu.VMEM((2, 128, tokens), jnp.bfloat16),
+    ]
+    operands = [projected, projected, projected, mixed_grad, exact, totals, gains, bias]
     linked = head_grad is not None
     if linked:
         depth = head_grad.shape[5]
@@ -1097,8 +1277,8 @@
     return layer_norm(values) * gain_vector
 
 
-def attention_bias(scale_query, segment_query, scale_key, segment_key, real_key, same):
-    usable = (segment_query == segment_key) & (scale_key <= scale_query) & ((real_key == 1) | same)
+def attention_bias(query, key):
+    usable = (query[1] == key[1]) & (key[0] <= query[0]) & ((key[2] == 1) | (query[3] == key[3]))
     return jnp.where(usable, 0.0, MASK_VALUE)
 
 
@@ -1157,43 +1337,55 @@
     out_low = out_weight.astype(low)
     down_low = down_weight.astype(low)
 
-    small_rows = jnp.concatenate(
-        [
-            tables_low[:, CLASSES:],
-            vectors.astype(low),
-            jnp.zeros((depth, 128 - CODE_DIM - LEVELS - 9), low),
-        ],
-        axis=1,
-    )
-    tags = jnp.zeros((8, 128), jnp.float32)
-    tags = tags.at[0, :2].set(labels.astype(jnp.float32)).at[0, 2].set(local_count)
-    if linked:
-        small_full, tags_full = small_gather(small_rows, tags)
-    else:
-        small_full, tags_full = gathered(small_rows), gathered(tags)
     full_up = gathered(up_weight.astype(low))
     full_head = gathered(head_weight.astype(low))
-    small_full = small_full.reshape(D, 128)
-    tags_full = tags_full.reshape(devices, 8, 128)[:, 0]
-    labels_all = tags_full[:, :2].reshape(2 * devices)
-    weight_total = jnp.sum(tags_full[:, 2])
-    code_tables = small_full[:, : CODE_DIM + LEVELS]
-    gain_vector = small_full[:, CODE_DIM + LEVELS : CODE_DIM + LEVELS + 9].astype(jnp.float32)
-
-    label_hot = (labels_all[:, None] == jnp.arange(1152, dtype=jnp.float32)[None, :]).astype(low)
-    class_cond = bfloat_product(label_hot[:, :CLASSES], tables_low[:, :CLASSES].T)
-    activated = jax.nn.silu(class_cond).astype(low)
-    modulation_part = bfloat_product(activated, ada_low)
+    small_rows = jnp.concatenate(
+        [vectors.astype(low), tables_low[:, CLASSES:], jnp.zeros((depth, 128 - SMALL_LANES), low)], axis=1
+    )
+    tag_row = jnp.concatenate([labels.astype(jnp.float32), local_count[None], jnp.zeros((5,), jnp.float32)])
+    tags = jnp.broadcast_to(tag_row[:, None], (8, 128))
+    level_hot = (scale_ids[:, None] == jnp.arange(LEVELS)[None, :]).astype(low)
+    code_levels = jnp.concatenate([code_vectors, level_hot], axis=1)
+    codes = jnp.pad(code_levels, ((0, 0), (9, 128 - SMALL_LANES)))
+    second = (segment_ids == 1)[:, None]
     if linked:
-        own_modulation, full_qkv = first_exchange(
-            modulation_part.reshape(FIVE + (12 * D // 128, 128)), qkv_low
+        token_rows = jnp.stack([segment_ids, scale_ids, real_mask] + [real_mask] * 5).astype(jnp.float32)
+        token_columns = jnp.pad(token_rows[:3].T, ((0, 0), (0, 125)))
+        (
+            projected,
+            full_qkv,
+            full_out,
+            embedded,
+            normed,
+            modulation,
+            vector_rows,
+            label_hot,
+            class_cond,
+            activated,
+            tag_sums,
+            bias,
+            turned_bias,
+        ) = begin(
+            small_rows, tags, tables, ada_weight, qkv_weight, out_weight, codes, token_columns, token_rows
         )
-        own_modulation = own_modulation.reshape(2, 6 * D)
-        full_qkv = full_qkv.reshape(D, 3 * D)
+        full_qkv, full_out = full_qkv.reshape(D, 3 * D), full_out.reshape(D, D)
+        weight_total = tag_sums[2, 0]
+        gains = vector_rows[6:14]
+        head_gain = vector_rows[8]
     else:
-        own_modulation, full_qkv = scattered(modulation_part), gathered(qkv_low)
-    modulation = own_modulation + gain_vector[:, :6].T.reshape(1, 6 * D)
-    second = (segment_ids == 1)[:, None]
+        small_full = gathered(small_rows)
+        tags_full = gathered(tags).reshape(devices, 8, 128)[:, :, 0]
+        labels_all = tags_full[:, :2].reshape(2 * devices)
+        weight_total = jnp.sum(tags_full[:, 2])
+        gain_vector = small_full[:, :9].astype(jnp.float32)
+        label_hot = (labels_all[:, None] == jnp.arange(1152, dtype=jnp.float32)[None, :]).astype(low)
+        class_cond = bfloat_product(label_hot[:, :CLASSES], tables_low[:, :CLASSES].T)
+        activated = jax.nn.silu(class_cond).astype(low)
+        own_modulation, full_qkv = scattered(bfloat_product(activated, ada_low)), gathered(qkv_low)
+        modulation = own_modulation + gain_vector[:, :6].T.reshape(1, 6 * D)
+        embedded = bfloat_product(codes, small_full.T)
+        gains = jnp.pad(gain_vector[:, 6:8].T, ((0, 6), (0, 0)))
+        head_gain = gain_vector[:, 8]
 
     def of_token(block):
         piece = modulation[:, block * D : (block + 1) * D]
@@ -1202,24 +1394,17 @@
     gamma_one, gamma_two, scale_one, scale_two, shift_one, shift_two = (
         of_token(block) for block in range(6)
     )
-
-    level_hot = (scale_ids[:, None] == jnp.arange(LEVELS)[None, :]).astype(low)
-    code_levels = jnp.concatenate([code_vectors, level_hot], axis=1)
-    embedded = bfloat_product(code_levels, code_tables.T)
-    normed = modulate(embedded, scale_one, shift_one).astype(low)
-    projected = bfloat_product(normed, full_qkv)
-    gains = jnp.pad(gain_vector[:, 6:8].T, ((0, 6), (0, 0)))
-    places = jnp.arange(tokens)
-    same = places[:, None] == places[None, :]
-    bias = attention_bias(
-        scale_ids[:, None], segment_ids[:, None], scale_ids[None, :], segment_ids[None, :], real_mask[None, :], same
-    )
     if linked:
-        mixed_heads, full_out, full_down = attend(projected, gains, bias, out_low, down_low)
-        full_out = full_out.reshape(D, D)
+        mixed_heads, exact, totals, full_down = attend(projected, gains, bias, down_low, depth)
         full_down = full_down.reshape(-1, D)
     else:
-        (mixed_heads,) = attend(projected, gains, bias)
+        normed = modulate(embedded, scale_one, shift_one).astype(low)
+        projected = bfloat_product(normed, full_qkv)
+        places = jnp.arange(tokens)
+        masks = (scale_ids, segment_ids, real_mask, places)
+        bias = attention_bias([m[:, None] for m in masks], [m[None, :] for m in masks])
+        turned_bias = attention_bias([m[None, :] for m in masks], [m[:, None] for m in masks])
+        mixed_heads, exact, totals = attend(projected, gains, bias)
         full_out, full_down = gathered(out_low), gathered(down_low)
     attended = bfloat_product(mixed_heads, full_out)
     residual_one = embedded + gamma_one * attended
@@ -1228,7 +1413,7 @@
     hidden_act = jax.nn.gelu(hidden_pre, approximate=True).astype(low)
     branch = bfloat_product(hidden_act, full_down)
     residual_two = residual_one + gamma_two * branch
-    final_normed = final_norm(residual_two, gain_vector[:, 8]).astype(low)
+    final_normed = final_norm(residual_two, head_gain).astype(low)
     logits = bfloat_product(final_normed, full_head)
     logit_peak = jnp.max(logits, axis=-1, keepdims=True)
     log_total = logit_peak + jnp.log(jnp.sum(jnp.exp(logits - logit_peak), axis=-1, keepdims=True))
@@ -1243,7 +1428,7 @@
 
     head_part = bfloat_product(final_normed.T, logit_grad).astype(part_kind)
     final_grad = bfloat_product(logit_grad, full_head.T)
-    _, final_back = jax.vjp(final_norm, residual_two, gain_vector[:, 8])
+    _, final_back = jax.vjp(final_norm, residual_two, head_gain)
     residual_grad, head_gain_grad = final_back(final_grad)
     branch_grad = (gamma_two * residual_grad).astype(low)
 
@@ -1267,13 +1452,12 @@
     gamma_one_grad = slot_sums(residual_grad * attended)
     out_part = bfloat_product(mixed_heads.T, attended_grad).astype(part_kind)
     mixed_grad = bfloat_product(attended_grad, full_out.T).astype(low)
-    turned_bias = attention_bias(
-        scale_ids[None, :], segment_ids[None, :], scale_ids[:, None], segment_ids[:, None], real_mask[:, None], same
-    )
     if linked:
         heads_grad, gain_grads, attention_done = attend_back(
             projected,
             mixed_grad,
+            exact,
+            totals,
             gains,
             turned_bias,
             head_part.reshape(FIVE + (depth, CODES)),
@@ -1281,7 +1465,7 @@
             down_part.reshape(FIVE + (down_part.shape[0] // D, depth, D)),
         )
     else:
-        heads_grad, gain_grads = attend_back(projected, mixed_grad, gains, turned_bias)
+        heads_grad, gain_grads = attend_back(projected, mixed_grad, exact, totals, gains, turned_bias)
         head_grad, up_grad, down_grad = scattered(head_part), scattered(up_part), scattered(down_part)
     if linked:
         unknown = jnp.zeros((2, D), jnp.float32)
@@ -1295,7 +1479,6 @@
             [gamma_one_grad, gamma_two_grad, unknown, scale_two_grad, unknown, shift_two_grad], axis=1
         )
         gain_rows = jnp.concatenate([gain_grads[:2], head_gain_grad[None], jnp.zeros((5, D), jnp.float32)])
-        codes = jnp.pad(code_levels, ((0, 0), (9, 128 - SMALL_LANES)))
         last = last_exchange(
             (out_part.reshape(FIVE + (depth, D)), full_qkv, embedded, residual_grad),
             (

time: 724 us -> 704 us (0.972)
  Pallas kernels: 416 us -> 438 us
  other arithmetic: 54.8 us -> 35.2 us
  matrix products: 187 us -> 174 us
  local copies, waits for them, and re-layouts: 40.7 us -> 30.6 us
    pallas_call x2 -> x1, Pallas kernels: 89.8 us -> 114 us  [begin(): pl.pallas_call(begin_kernel, out_shape=(shape((tokens, 3 * D), f32), shap...]
    dot_general x16 -> x12, matrix products: 187 us -> 174 us  [bfloat_product(): return jnp.dot(left_side, right_side, preferred_element_type=jnp.float32)]
    convert_element_type x6 -> x2, other arithmetic: 8.62 us -> 0.66 us  [the longest x1 0.66 us: on_device(): labels.astype(jnp.float32)]
  transfers between devices with their start and end apart: 2 -> 2, of which waited for: 0 -> 0; matrix products, arithmetic and copies ran while one was open for 15% -> 9% of each run, Pallas kernels for 23% -> 28%
where the time goes in v3:
time: 704 us; the launch traced here: 693 us
  Pallas kernels  438 us (62%)
  matrix products  174 us (25%)
  other arithmetic  35.2 us (5%)
  local copies, waits for them, and re-layouts  30.6 us (4%)
  between operations  15.5 us (2%)
    dot_general x12, matrix products, bfloat_product(): return jnp.dot(left_side, right_side, preferred_element_type=jnp.float32)  174 us
    pallas_call x1, Pallas kernels, attend_back(): pl.pallas_call(partial(attend_back_kernel, linked), grid=(HEADS // 2,), o...  125 us
    pallas_call x1, Pallas kernels, begin(): pl.pallas_call(begin_kernel, out_shape=(shape((tokens, 3 * D), f32), shap...  114 us
    pallas_call x1, Pallas kernels, last_exchange(): pl.pallas_call(last_kernel, out_shape=(jax.ShapeDtypeStruct((pairs, depth...  113 us
    pallas_call x1, Pallas kernels, attend(): pl.pallas_call(partial(attend_kernel, linked), grid=(HEADS // 2,), out_sh...  80 us
  transfers between devices with their start and end apart: 2, of which 0 were waited for; matrix products, arithmetic and copies ran while one was open for 9% of the time, Pallas kernels for 28%

profile of v3, /device:TPU:0, one launch (start us, length us, event | category | flops | bytes accessed | tf_op | source)
XLA Modules:
  0.0 693.0 jit_solution(1843278879283829187)
XLA Ops:
  7.3 1.8 convert_element_type.86
  9.3 1.8 convert_element_type.89
  11.1 0.8 slice.173
  11.9 0.7 convert_element_type.78
  12.7 1.3 reduce_sum.183
  14.7 0.7 convert_element_type.80
  15.3 0.7 fusion.12
  16.0 0.9 pad_maximum_fusion
  17.1 1.0 stack.56
  18.3 0.8 pad.8.codes_ref
  19.3 0.8 pad.9.clone.token_columns
  20.1 0.6 fusion.33
  20.7 0.7 maximum_maximum_fusion.1.rows_ref
  21.4 0.7 broadcast_in_dim.187.tags_ref
  22.0 113.6 %begin.1 = (f32[1024,3072]{1,0:T(8,128)}, bf16[2,2,2,2,2,32,3072]{6,5,4,3,2,1,0:T(8,128)(2,1)}, bf16[2,2,2,2,2,32,1024]{6,5,4,3,2,1,0:T(8,128)(2,1)}, f32[1024,1...) custom-call(bf16[32,128]{1,0:T(8,128)(2,1)} %maximum_maximum_fusion., ...), custom_call_target="tpu_custom_call" | custom-call | tf_op jit(solution)/shard_map/begin/pallas_call | solution.py:474
  135.6 1.5 slice.125.gain_ref
  137.1 0.8 slice.134
  137.9 0.7 copy.98.vectors_ref
  138.7 0.7 convert_element_type.84.refs_0_
  139.4 1.2 slice.135
  140.6 1.0 copy.97.second_ref
  141.6 1.3 slice.136.scale_ref
  143.1 0.9 reshape.173.moments_ref
  143.9 0.7 copy.100.vector_moment_ref
  144.7 0.7 broadcast_in_dim.216.column_moment_ref
  145.4 80.0 %attention_forward.1 = (bf16[1024,1024]{1,0:T(8,128)(2,1)}, f32[1024,1024]{1,0:T(8,128)}, f32[1024,1024]{1,0:T(8,128)}, bf16[2,2,2,2,2,4,32,1024]{7,6,5,4,3,2,1,0:T(8,128)(2,1)}) custom-call(f32[1024,3072]{1,0:T(8,128)} %get-tuple-element.72.q_ref.k_ref.v_ref, f32[1024,3072]{1,0:T(8,128)} %get-tuple-element.72.q_ref.k_ref.v_ref, ...), custom_call_target="tpu_custom_call" | custom-call | tf_op jit(solution)/shard_map/attention_forward/pallas_call | solution.py:623
  225.5 7.0 %fusion.30 = (f32[1024]{0:T(1024)S(1)}, f32[1024,1024]{1,0:T(8,128)S(1)}, f32[1024,1024]{1,0:T(8,128)}) fusion(f32[1024,1024]{1,0:T(8,128)S(1)} %copy-done.3, f32[1024]{0:T(1024)S(1)} %bitcast.69, f32[1024]{0:T(1024)S(1)} %bitcast.72, pred[1024]{0:T(1024)(128)(4,1)S(1)} %get-tuple-element.256, bf16[1024,1024]{1,0:T(8,128)(2,1)} %get-tuple-element.75, ...), kind=kOutput, calls=%fused_computation.96 | convolution fusion | flops 2151676928 | bytes 16790528 | tf_op jit(solution)/shard_map/dot_general | solution.py:46
  232.5 2.0 copy-done
  235.1 17.6 %fusion.23 = f32[1024,4096]{1,0:T(8,128)} fusion(bf16[1024,4096]{1,0:T(8,128)(2,1)} %all-gather.3.cloned.1.call-done, f32[1024,1024]{1,0:T(8,128)} %copy-done, f32[1024]{0:T(1024)S(1)} %bitcast.98, f32[1024]{0:T(1024)S(1)} %bitcast.100, f32[1024]{0:T(1024)S(1)} %bitcast.75, f32[1024]{0:T(1024)S(1)} %bitcast.79, f32[1024]{0:T(1024)S(1)} %fusion.13, ...), kind=kOutput, calls=%fused_computation.90 | convolution fusion | flops 8598323200 | bytes 29385728 | tf_op jit(solution)/shard_map/dot_general | solution.py:46
  252.7 18.1 %fusion.28 = (f32[1024]{0:T(1024)S(1)}, f32[1024,1024]{1,0:T(8,128)S(1)}, f32[1024,1024]{1,0:T(8,128)}) fusion(f32[1024,1024]{1,0:T(8,128)S(1)} %copy-done.1, f32[1024]{0:T(1024)S(1)} %bitcast.95, f32[1024]{0:T(1024)S(1)} %bitcast.92, pred[1024]{0:T(1024)(128)(4,1)S(1)} %get-tuple-element.256, bf16[4096,1024]{1,0:T(8,128)(2,1)} %bitcast.111, ...), kind=kOutput, calls=%fused_computation.95 | convolution fusion | flops 8631876608 | bytes 37762048 | tf_op jit(solution)/shard_map/dot_general | solution.py:46
  270.8 2.1 copy-done.8
  272.9 0.6 multiply_reduce_fusion.3
  273.5 12.9 %fusion.34 = (f32[1024]{0:T(1024)S(1)}, f32[1024,4096]{1,0:T(8,128)S(1)}) fusion(bf16[1024,4096]{1,0:T(8,128)(2,1)} %all-gather.5.cloned.1.call-done, f32[1024,1024]{1,0:T(8,128)} %copy-done.8, f32[1024]{0:T(1024)S(1)} %bitcast.83, f32[1024]{0:T(1024)S(1)} %fusion.14, f32[1024]{0:T(1024)S(1)} %broadcast_multiply_fusion), kind=kOutput, calls=%fused_computation.99 | convolution fusion | flops 8598322176 | bytes 29376512 | tf_op jit(solution)/shard_map/dot_general | solution.py:46
  286.4 5.6 select_reduce_fusion
  292.1 1.3 multiply_reduce_fusion.5
  293.3 7.9 %multiply_convert_fusion = bf16[1024,4096]{1,0:T(8,128)(2,1)} fusion(f32[1024,4096]{1,0:T(8,128)S(1)} %get-tuple-element.279, f32[1024]{0:T(1024)S(1)} %get-tuple-element.273, s32[1024]{0:T(1024)S(1)} %copy-done.24, f32[1024]{0:T(1024)S(1)} %get-tuple-element.253), kind=kLoop, calls=%fused_computation.10 | loop fusion | flops 25165824 | bytes 25178112 | tf_op jit(solution)/shard_map/convert_element_type | solution.py:1427
  301.2 15.4 %multiply_reduce_fusion = (f32[1024]{0:T(1024)}, f32[1024]{0:T(1024)S(1)}, f32[1024,1024]{1,0:T(8,128)S(1)}) fusion(f32[1024,1024]{1,0:T(8,128)S(1)} %copy-done.9, f32[1024]{0:T(1024)S(1)} %fusion.14, f32[1024]{0:T(1024)S(1)} %broadcast_multiply_fusion, f32[1024]{0:T(1024)S(1)} %bitcast.84, bf16[1024,4096]{1,0:T(8,128)(2,1)} %multiply_convert_fusion, ...), kind=kOutput, calls=%fused_computation.27 | convolution fusion | flops 8597272576 | bytes 25186304 | tf_op jit(solution)/shard_map/dot_general | solution.py:46
  316.6 1.8 fusion.27
  318.4 25.7 %fusion.6 = bf16[1024,4096]{1,0:T(8,128)(2,1)} fusion(f32[1024,4096]{1,0:T(8,128)} %fusion.23, bf16[4096,1024]{1,0:T(8,128)(2,1)} %bitcast.112, f32[1024,1024]{1,0:T(8,128)S(1)} %get-tuple-element.260, f32[1024]{0:T(1024)S(1)} %negate_multiply_fusion.1, f32[1024]{0:T(1024)S(1)} %bitcast.96, f32[1024]{0:T(1024)S(1)} %bitcast.93, ...), kind=kOutput, calls=%fused_computation.8 | convolution fusion | flops 8678014976 | bytes 37762048 | tf_op jit(solution)/shard_map/dot_general | solution.py:46
  344.2 20.1 %select_reduce_fusion.2 = (f32[1024]{0:T(1024)S(1)}, f32[1024]{0:T(1024)S(1)}, f32[1024]{0:T(1024)S(1)}, f32[1024]{0:T(1024)S(1)}, f32[1024]{0:T(1024)S(1)}, /*i...) fusion(pred[1024]{0:T(1024)(128)(4,1)S(1)} %get-tuple-element.256, f32[1024]{0:T(1024)S(1)} %bitcast.76, ...), kind=kOutput, calls=%fused_computation.29 | convolution fusion | flops 8612996096 | bytes 33604608 | tf_op jit(solution)/shard_map/dot_general | solution.py:46
  364.3 4.7 fusion.26
  369.0 1.2 copy-done.7
  370.2 1.5 select_reduce_fusion.8
  371.8 3.9 convolution_convert_fusion.4
  375.6 3.7 convolution_convert_fusion.3.m_ref
  379.4 15.3 %convolution_convert_fusion.2 = bf16[1024,4096]{1,0:T(8,128)(2,1)} fusion(bf16[1024,4096]{1,0:T(8,128)(2,1)} %multiply_convert_fusion, f32[1024,1024]{1,0:T(8,128)S(1)} %copy-done.11, f32[1024]{0:T(1024)S(1)} %bitcast.86, f32[1024]{0:T(1024)S(1)} %fusion.14, f32[1024]{0:T(1024)S(1)} %broadcast_multiply_fusion), kind=kOutput, calls=%fused_computation.16 | convolution fusion | flops 8598323200 | bytes 20983808 | tf_op jit(solution)/shard_map/dot_general | solution.py:46
  394.7 15.6 %convolution_convert_fusion.1 = bf16[1024,4096]{1,0:T(8,128)(2,1)} fusion(bf16[1024,4096]{1,0:T(8,128)(2,1)} %fusion.6, f32[1024,1024]{1,0:T(8,128)S(1)} %copy-done.2, f32[1024]{0:T(1024)S(1)} %bitcast.99, f32[1024]{0:T(1024)S(1)} %bitcast.101, f32[1024]{0:T(1024)S(1)} %bitcast.78, f32[1024]{0:T(1024)S(1)} %bitcast.82, f32[1024]{0:T(1024)S(1)} %fusion.13, ...), kind=kOutput, calls=%fused_computation.15 | convolution fusion | flops 8602517504 | bytes 20997120 | tf_op jit(solution)/shard_map/dot_general | solution.py:46
  410.3 18.4 %convolution_convert_fusion = bf16[4096,1024]{1,0:T(8,128)(2,1)} fusion(f32[1024,1024]{1,0:T(8,128)S(1)} %copy-done.7, f32[1024]{0:T(1024)S(1)} %negate_multiply_fusion.1, f32[1024]{0:T(1024)S(1)} %bitcast.97, f32[1024]{0:T(1024)S(1)} %bitcast.94, pred[1024]{0:T(1024)(128)(4,1)S(1)} %get-tuple-element.256, f32[1024,4096]{1,0:T(8,128)} %fusion.23), kind=kOutput, calls=%fused_computation.14 | convolution fusion | flops 8636071936 | bytes 29373440 | tf_op jit(solution)/shard_map/dot_general | solution.py:46
  428.8 125.0 %attention_backward.1 = (bf16[3,1024,1024]{2,1,0:T(8,128)(2,1)}, f32[8,1024]{1,0:T(8,128)}, f32[24,32,512]{2,1,0:T(8,128)}) custom-call(f32[1024,3072]{1,0:T(8,128)} %get-tuple-element.72.q_ref.k_ref.v_ref, f32[1024,3072]{1,0:T(8,128)} %get-tuple-element.72.q_ref.k_ref.v_ref, f32[1024,3072]{1,0:T(8,128)} %get-tuple-element.72.q_ref.k_ref.v_ref, ...), custom_call_target="tpu_custom_call" | custom-call | tf_op jit(solution)/shard_map/attention_backward/pallas_call | solution.py:758
  553.7 0.8 slice.137
  554.5 0.7 maximum_maximum_fusion.gains_ref
  555.2 113.4 %last_scatter.1 = (f32[8,32,512]{2,1,0:T(8,128)}, f32[32,128]{1,0:T(8,128)}, f32[32,1152]{1,0:T(8,128)}, f32[32,6144]{1,0:T(8,128)}, f32[10,32,1]{2,1,0:T(8,128)...) custom-call(bf16[2,2,2,2,2,32,1024]{6,5,4,3,2,1,0:T(8,128)(2,1)} %bitcast.61, bf16[1024,3072]{1,0:T(8,128)(2,1)} %bitcast.58, ...), custom_call_target="tpu_custom_call" | custom-call | tf_op jit(solution)/shard_map/last_scatter/pallas_call | solution.py:1144
  668.7 1.5 slice_reduce_fusion.1
  670.2 0.9 slice_reduce_fusion
  671.1 0.9 slice.157
  672.0 0.7 slice_reduce_fusion.7
  672.7 0.6 copy.110
  673.3 0.6 slice.140
  674.4 6.0 weight_step.1
  680.5 1.4 copy.103
  681.9 1.4 copy.104
  683.2 1.4 copy.105
  684.6 0.6 slice.152
  685.2 0.7 pad_maximum_fusion.1
  (118 shorter events, 2.5 us)
Async XLA Ops:
  7.2 130.7 %copy-start.23 = (f32[32,9]{0,1:T(8,128)S(1)}, f32[32,9]{0,1:T(8,128)}, u32[]{:S(2)}) copy-start(f32[32,9]{0,1:T(8,128)} %param.32) | copy-start | bytes 3460
  7.2 133.4 %copy-start.26 = (s32[1024]{0:T(1024)S(1)}, s32[1024]{0:T(1024)}, u32[]{:S(2)}) copy-start(s32[1024]{0:T(1024)} %param.26) | copy-start | bytes 12292
  7.2 131.3 %copy-start.16 = (f32[20498]{0:T(1024)S(1)}, f32[20498]{0:T(1024)}, u32[]{:S(2)}) copy-start(f32[20498]{0:T(1024)} %param.47) | copy-start | bytes 245980
  7.2 131.4 %copy-start.12 = (f32[128,1024]{1,0:T(8,128)S(1)}, f32[128,1024]{1,0:T(8,128)}, u32[]{:S(2)}) copy-start(f32[128,1024]{1,0:T(8,128)} %down_master.3) | copy-start | bytes 1572868
  7.3 227.8 %all-gather.3.cloned.1.call-start = ((), (), s32[]{:S(2)}) async-start(), calls=%async_computation | async-start | bytes 8650752 | tf_op jit(solution)/shard_map/all_gather | solution.py:1260
  9.1 133.8 %copy-start.34 = (f32[32]{0:T(128)S(1)}, f32[32]{0:T(128)}, u32[]{:S(2)}) copy-start(f32[32]{0:T(128)} %param.39) | copy-start | bytes 388
  9.1 133.8 %copy-start.35 = (f32[32]{0:T(128)S(1)}, f32[32]{0:T(128)}, u32[]{:S(2)}) copy-start(f32[32]{0:T(128)} %param.40) | copy-start | bytes 388
  9.1 133.8 %copy-start.36 = (f32[32]{0:T(128)S(1)}, f32[32]{0:T(128)}, u32[]{:S(2)}) copy-start(f32[32]{0:T(128)} %param.41) | copy-start | bytes 388
  9.1 133.8 %copy-start.37 = (f32[32]{0:T(128)S(1)}, f32[32]{0:T(128)}, u32[]{:S(2)}) copy-start(f32[32]{0:T(128)} %param.42) | copy-start | bytes 388
  9.1 133.8 %copy-start.38 = (f32[32]{0:T(128)S(1)}, f32[32]{0:T(128)}, u32[]{:S(2)}) copy-start(f32[32]{0:T(128)} %param.43) | copy-start | bytes 388
  9.2 133.8 %copy-start.39 = (f32[32]{0:T(128)S(1)}, f32[32]{0:T(128)}, u32[]{:S(2)}) copy-start(f32[32]{0:T(128)} %param.45) | copy-start | bytes 388
  9.2 133.8 %copy-start.40 = (f32[128]{0:T(128)S(1)}, f32[128]{0:T(128)}, u32[]{:S(2)}) copy-start(f32[128]{0:T(128)} %param.44) | copy-start | bytes 1540
  9.2 134.8 %copy-start.27 = (f32[32,9]{0,1:T(8,128)S(1)}, f32[32,9]{0,1:T(8,128)}, u32[]{:S(2)}) copy-start(f32[32,9]{0,1:T(8,128)} %param.46) | copy-start | bytes 3460
  9.2 135.4 %slice-start = ((f32[20498]{0:T(1024)}), f32[1042]{0:T(1024)S(1)}, s32[]{:S(2)}) async-start(f32[20498]{0:T(1024)} %param.47), calls=%async_computation.2 | async-start | bytes 16384 | tf_op jit(solution)/shard_map/slice | solution.py:1476
  9.2 264.3 %all-gather.5.cloned.1.call-start = ((), (), s32[]{:S(2)}) async-start(), calls=%async_computation.1 | async-start | bytes 8650752 | tf_op jit(solution)/shard_map/all_gather | solution.py:1260
  18.1 3.9 copy-start.15
  145.4 80.0 %copy-start.22 = (f32[2,6144]{1,0:T(2,128)S(1)}, f32[2,6144]{1,0:T(2,128)}, u32[]{:S(2)}) copy-start(f32[2,6144]{1,0:T(2,128)} %get-tuple-element.76) | copy-start | bytes 147460
  145.4 80.1 %copy-start.3 = (f32[1024,1024]{1,0:T(8,128)S(1)}, f32[1024,1024]{1,0:T(8,128)}, u32[]{:S(2)}) copy-start(f32[1024,1024]{1,0:T(8,128)} %get-tuple-element.77.embedded_ref) | copy-start | bytes 12582916
  225.4 7.0 %copy-start.18 = (f32[1,1024]{1,0:T(1,128)}, f32[1,1024]{1,0:T(1,128)S(1)}, u32[]{:S(2)}) copy-start(f32[1,1024]{1,0:T(1,128)S(1)} %get-tuple-element.271) | copy-start | bytes 12292
  225.4 7.0 %copy-start.20 = (f32[1,1024]{1,0:T(1,128)}, f32[1,1024]{1,0:T(1,128)S(1)}, u32[]{:S(2)}) copy-start(f32[1,1024]{1,0:T(1,128)S(1)} %get-tuple-element.272) | copy-start | bytes 12292
  225.4 9.6 %copy-start.28 = (f32[1,1024]{1,0:T(1,128)}, f32[1,1024]{1,0:T(1,128)S(1)}, u32[]{:S(2)}) copy-start(f32[1,1024]{1,0:T(1,128)S(1)} %get-tuple-element.266) | copy-start | bytes 12292
  225.4 9.6 %copy-start.30 = (f32[1,1024]{1,0:T(1,128)}, f32[1,1024]{1,0:T(1,128)S(1)}, u32[]{:S(2)}) copy-start(f32[1,1024]{1,0:T(1,128)S(1)} %get-tuple-element.267) | copy-start | bytes 12292
  232.4 2.0 copy-start
  235.1 17.6 %copy-start.1 = (f32[1024,1024]{1,0:T(8,128)S(1)}, f32[1024,1024]{1,0:T(8,128)}, u32[]{:S(2)}) copy-start(f32[1024,1024]{1,0:T(8,128)} %copy-done) | copy-start | bytes 12582916
  270.8 2.1 copy-start.8
  273.5 12.9 %copy-start.24 = (s32[1024]{0:T(1024)S(1)}, s32[1024]{0:T(1024)}, u32[]{:S(2)}) copy-start(s32[1024]{0:T(1024)} %param.29) | copy-start | bytes 12292
  286.4 5.6 copy-start.25
  293.3 7.9 %copy-start.9 = (f32[1024,1024]{1,0:T(8,128)S(1)}, f32[1024,1024]{1,0:T(8,128)}, u32[]{:S(2)}) copy-start(f32[1024,1024]{1,0:T(8,128)} %copy-done.8) | copy-start | bytes 12582916
  301.2 15.4 %copy-start.10 = (f32[1024,1024]{1,0:T(8,128)S(1)}, f32[1024,1024]{1,0:T(8,128)}, u32[]{:S(2)}) copy-start(f32[1024,1024]{1,0:T(8,128)} %copy-done.8) | copy-start | bytes 12582916
  318.4 25.8 %copy-start.6 = (f32[1024,1024]{1,0:T(8,128)}, f32[1024,1024]{1,0:T(8,128)S(1)}, u32[]{:S(2)}) copy-start(f32[1024,1024]{1,0:T(8,128)S(1)} %get-tuple-element.260) | copy-start | bytes 12582916
  364.2 4.7 copy-start.4
  364.3 5.9 copy-start.7
  370.2 1.6 copy-start.13
  370.2 1.6 copy-start.19
  370.2 1.6 copy-start.21
  371.7 3.9 copy-start.5
  371.8 3.9 copy-start.14
  375.6 3.7 copy-start.11
  379.4 15.4 %copy-start.2 = (f32[1024,1024]{1,0:T(8,128)S(1)}, f32[1024,1024]{1,0:T(8,128)}, u32[]{:S(2)}) copy-start(f32[1024,1024]{1,0:T(8,128)} %copy-done) | copy-start | bytes 12582916
  379.4 15.4 %copy-start.29 = (f32[1,1024]{1,0:T(1,128)S(1)}, f32[1,1024]{1,0:T(1,128)}, u32[]{:S(2)}) copy-start(f32[1,1024]{1,0:T(1,128)} %copy-done.28) | copy-start | bytes 12292
  379.4 15.4 %copy-start.31 = (f32[1,1024]{1,0:T(1,128)S(1)}, f32[1,1024]{1,0:T(1,128)}, u32[]{:S(2)}) copy-start(f32[1,1024]{1,0:T(1,128)} %copy-done.30) | copy-start | bytes 12292
  428.7 125.8 %copy-start.32 = (f32[1024]{0:T(1024)S(1)}, f32[1024]{0:T(1024)}, u32[]{:S(2)}) copy-start(f32[1024]{0:T(1024)} %get-tuple-element.235) | copy-start | bytes 12292
  428.8 125.8 %copy-start.33 = (f32[8]{0:T(128)S(1)}, f32[8]{0:T(128)}, u32[]{:S(2)}) copy-start(f32[8]{0:T(128)} %get-tuple-element.274) | copy-start | bytes 100
  554.5 0.7 copy-start.17
Sparse Core Ops, SparseCore 0:
  11.5 104.3 all-gather.2
  119.3 96.3 all-gather.4

commit v4 on v3

--- a/solution.py
+++ b/solution.py
@@ -36,7 +36,7 @@
 SCORE_SCALE = HEAD_DIM ** (-0.5)
 EXP_SCALE = SCORE_SCALE * math.log2(math.e)
 VMEM_GRANT = 58 * 1024 * 1024
-FIRST_WIDTH, FIRST_LAG = 256, 1
+FIRST_WIDTH, FIRST_LAG = 256, 2
 ATTEND_WIDTH, ATTEND_LAG = 128, 3
 BACK_WIDTH, BACK_LAG = 256, 2
 LAST_WIDTH, LAST_LAG = 256, 2
@@ -205,14 +205,12 @@
                         mine = self.keep[near, parity]
                     else:
                         mine = self.sums[before][(near,) + self.half(before, parity, False)]
-                    total = mine.astype(jnp.float32) + self.land[before][slot, parity].astype(
-                        jnp.float32
-                    )
+                    landed = self.land[before][slot, parity]
                     if stage < 5:
-                        self.sums[stage][near, parity] = total.astype(self.keep.dtype)
+                        self.sums[stage][near, parity] = mine + landed
                         self.copy(stage, parity, j).start()
                     else:
-                        self.store(j, parity, total)
+                        self.store(j, parity, mine.astype(jnp.float32) + landed.astype(jnp.float32))
 
             if stage == 0:
                 for low, high, source in self.groups:
@@ -546,9 +544,52 @@
 
 def attend_kernel(linked, q_ref, k_ref, v_ref, gain_ref, bias_ref, *refs):
     if linked:
-        down_own, mixed_ref, exact_ref, total_ref, down_full, qn, kn, vn = refs[:8]
-        sems = refs[8:]
+        down_own, half_ref, mixed_ref, exact_ref, total_ref, down_full, up_full, head_full = refs[:8]
+        qn, kn, vn, pair_sems, passing, pass_sems = refs[8:14]
+        sems = refs[14:]
         place = Place()
+        core = place.bit["c"]
+
+        def pair_copies():
+            start = 0
+            for order, full in enumerate((up_full, head_full)):
+                size = full.shape[6]
+                source = half_ref.at[:, :, :, :, :, start : start + size]
+                target = full.at[:, :, :, :, core]
+                yield place.send(source, target, pair_sems.at[0, order], pair_sems.at[1, order], "c")
+                start += size
+
+        chunks = HEADS // 2
+        piece = passing.shape[6]
+
+        def load(i):
+            return pltpu.make_async_copy(
+                half_ref.at[:, :, :, :, :, i * piece : (i + 1) * piece], passing.at[i % 2], pass_sems.at[0, i % 2]
+            )
+
+        def save(i):
+            full = (up_full, head_full)[i // (chunks // 2)]
+            at = (i % (chunks // 2)) * piece
+            return pltpu.make_async_copy(
+                passing.at[i % 2], full.at[:, :, :, :, core, :, at : at + piece], pass_sems.at[1, i % 2]
+            )
+
+        def each_chunk(body):
+            for i in range(chunks):
+                pl.when(pl.program_id(0) == i)(partial(body, i))
+
+        def begin_chunk(i):
+            if i >= 2:
+                save(i - 2).wait()
+            load(i).start()
+
+        def end_chunk(i):
+            load(i).wait()
+            save(i).start()
+            if i == chunks - 1:
+                save(i - 1).wait()
+                save(i).wait()
+
         width = ATTEND_WIDTH
         split = D // (2 * width)
         depth = down_full.shape[6]
@@ -565,7 +606,14 @@
             return down_full.at[r + (part, slice(None), columns((2 * column + p) * width, width))]
 
         gather = Gather(place, [(0, split * parts, down_source, down_target)], *sems, lag=ATTEND_LAG)
-        pl.when(pl.program_id(0) == 0)(place.meet)
+
+        @pl.when(pl.program_id(0) == 0)
+        def first():
+            place.meet()
+            for copy in pair_copies():
+                copy.start()
+
+        each_chunk(begin_chunk)
     else:
         mixed_ref, exact_ref, total_ref, qn, kn, vn = refs
     qn[...] = normed_head(q_ref[...], gain_ref[0:1])
@@ -597,9 +645,15 @@
 
     if linked:
         finish(gather)
-
-
-def attend(projected, gains, bias, down_own=None, depth=None):
+        each_chunk(end_chunk)
+
+        @pl.when(pl.program_id(0) == HEADS // 2 - 1)
+        def pair_done():
+            for copy in pair_copies():
+                copy.wait()
+
+
+def attend(projected, gains, bias, down_own=None, half=None):
     tokens = projected.shape[0]
     pair = pl.BlockSpec((tokens, 128), lambda i: (0, i))
     specs = [
@@ -615,11 +669,15 @@
     operands = [projected, projected, projected, gains, bias]
     linked = down_own is not None
     if linked:
-        specs += [ANY]
-        operands += [down_own]
+        depth = half.shape[4]
+        specs += [ANY, ANY]
+        operands += [down_own, half]
         outs += [jax.ShapeDtypeStruct(FIVE + (down_own.shape[0] // depth, depth, D), jnp.bfloat16)]
-        out_specs += [ANY]
-        scratch = scratch + Gather.scratch(ATTEND_LAG)
+        outs += [jax.ShapeDtypeStruct(FIVE + (depth, half.shape[5] // 2), jnp.bfloat16)] * 2
+        out_specs += [ANY] * 3
+        scratch = scratch + [pltpu.SemaphoreType.DMA((2, 2))]
+        scratch += [pltpu.VMEM((2,) + half.shape[:5] + (half.shape[5] // (HEADS // 2),), jnp.bfloat16)]
+        scratch += [pltpu.SemaphoreType.DMA((2, 2))] + Gather.scratch(ATTEND_LAG)
     return pl.pallas_call(
         partial(attend_kernel, linked),
         grid=(HEADS // 2,),
@@ -634,8 +692,8 @@
 
 def attend_back_kernel(linked, q_ref, k_ref, v_ref, m_ref, exact_ref, total_ref, gain_ref, bias_ref, *refs):
     if linked:
-        head_ref, up_ref, down_ref, grad_ref, gain_grad_ref, done_ref = refs[:6]
-        qn, kn, vn, dk, dv, turned, dq_turned, key_turned = refs[6:14]
+        up_ref, down_ref, grad_ref, gain_grad_ref, done_ref = refs[:5]
+        qn, kn, vn, dk, dv, turned, dq_turned, key_turned = refs[5:13]
         place = Place()
         width = BACK_WIDTH
         wide = up_ref.shape[6] // (2 * width)
@@ -648,23 +706,22 @@
             ]
 
         def down_source(j, p, core):
-            spread = j - 2 * wide
+            spread = j - wide
             part, column = lax.div(spread, narrow), lax.rem(spread, narrow)
             return down_ref.at[:, :, :, :, core, part, :, columns((2 * column + p) * width, width)]
 
         def store(j, parity, total):
             done_ref[j, :, parity * width : (parity + 1) * width] = total
 
-        pairs = 2 * wide + parts * narrow
+        pairs = wide + parts * narrow
         scatter = Scatter(
             place,
             [
-                (0, wide, columns_of(head_ref, 0)),
-                (wide, 2 * wide, columns_of(up_ref, wide)),
-                (2 * wide, pairs, down_source),
+                (0, wide, columns_of(up_ref, 0)),
+                (wide, pairs, down_source),
             ],
             store,
-            refs[14:],
+            refs[13:],
             lag=BACK_LAG,
         )
         pl.when(pl.program_id(0) == 0)(place.meet)
@@ -716,7 +773,7 @@
         finish(scatter)
 
 
-def attend_back(projected, mixed_grad, exact, totals, gains, bias, head_grad=None, up_grad=None, down_grad=None):
+def attend_back(projected, mixed_grad, exact, totals, gains, bias, up_grad=None, down_grad=None):
     tokens = projected.shape[0]
     pair = pl.BlockSpec((tokens, 128), lambda i: (0, i))
     specs = [
@@ -746,12 +803,12 @@
         pltpu.VMEM((2, 128, tokens), jnp.bfloat16),
     ]
     operands = [projected, projected, projected, mixed_grad, exact, totals, gains, bias]
-    linked = head_grad is not None
+    linked = up_grad is not None
     if linked:
-        depth = head_grad.shape[5]
-        specs += [ANY, ANY, ANY]
-        operands += [head_grad, up_grad, down_grad]
-        pairs = (head_grad.shape[6] + up_grad.shape[6] + down_grad.shape[5] * down_grad.shape[7]) // (2 * BACK_WIDTH)
+        depth = up_grad.shape[5]
+        specs += [ANY, ANY]
+        operands += [up_grad, down_grad]
+        pairs = (up_grad.shape[6] + down_grad.shape[5] * down_grad.shape[7]) // (2 * BACK_WIDTH)
         outs += [jax.ShapeDtypeStruct((pairs, depth, 2 * BACK_WIDTH), jnp.float32)]
         out_specs += [WHOLE]
         scratch = scratch + Scatter.scratch((depth, BACK_WIDTH), jnp.bfloat16, BACK_LAG)
@@ -767,6 +824,160 @@
     )(*operands)
 
 
+TANH_RATE = math.sqrt(2.0 / math.pi)
+DENSE_WIDTH = 512
+
+
+def dense_back_kernel(
+    branch_ref,
+    normed_ref,
+    pre_ref,
+    down_ref,
+    up_ref,
+    residual_ref,
+    grad_ref,
+    attended_ref,
+    token_columns,
+    mods_ref,
+    head_ref,
+    up_grad,
+    down_grad,
+    residual_grad,
+    attended_grad,
+    rows_ref,
+    done_ref,
+    normed_turned,
+    pre_grad,
+    hidden,
+    back,
+    *scratch,
+):
+    place = Place()
+    index = pl.program_id(0)
+    width = BACK_WIDTH
+
+    def store(j, parity, total):
+        done_ref[j, :, parity * width : (parity + 1) * width] = total
+
+    pairs = head_ref.shape[6] // (2 * width)
+    scatter = Scatter(
+        place,
+        [
+            (
+                0,
+                pairs,
+                lambda j, p, core: head_ref.at[:, :, :, :, core, :, columns((2 * j + p) * width, width)],
+            )
+        ],
+        store,
+        scratch,
+        lag=BACK_LAG,
+    )
+
+    @pl.when(index == 0)
+    def first():
+        place.meet()
+        normed_turned[...] = normed_ref[...].T
+        back[...] = jnp.zeros_like(back)
+
+    tokens = branch_ref.shape[0]
+    block = tokens // 4
+    blocks = [slice(i * block, (i + 1) * block) for i in range(4)]
+    scatter.step(index * 3)
+    for rows in blocks:
+        act_grad = dot_last(branch_ref[rows], down_ref[...])
+        value = pre_ref[rows]
+        square = value * value
+        bent = jnp.tanh(TANH_RATE * value * (1.0 + 0.044715 * square))
+        half = 0.5 * (1.0 + bent)
+        slope = half + 0.5 * value * (1.0 - bent * bent) * (TANH_RATE * (1.0 + 3 * 0.044715 * square))
+        pre_grad[rows] = (slope * act_grad).astype(jnp.bfloat16)
+        hidden[rows] = (value * half).astype(jnp.bfloat16)
+    scatter.step(index * 3 + 1)
+    down_grad[...] = dot_first(hidden[...], branch_ref[...]).astype(jnp.bfloat16)
+    up_grad[...] = dot_plain(normed_turned[...], pre_grad[...]).astype(jnp.bfloat16)
+    scatter.step(index * 3 + 2)
+    for rows in blocks:
+        back[rows] += dot_last(pre_grad[rows], up_ref[...])
+
+    @pl.when(index == pl.num_programs(0) - 1)
+    def last():
+        sums = [jnp.zeros((1, D), jnp.float32)] * 6
+        for rows in blocks:
+            values, slope = residual_ref[rows], back[rows]
+            center = values - jnp.sum(values, axis=1, keepdims=True) * (1.0 / D)
+            rate = lax.rsqrt(
+                jnp.sum(center * center, axis=1, keepdims=True) * (1.0 / D) + NORM_EPSILON
+            )
+            unit = center * rate
+            other = token_columns[rows, 0:1] > 0.5
+            unit_back = slope * (1.0 + jnp.where(other, mods_ref[1:2], mods_ref[0:1]))
+            mean_back = jnp.sum(unit_back, axis=1, keepdims=True) * (1.0 / D)
+            mean_along = jnp.sum(unit_back * unit, axis=1, keepdims=True) * (1.0 / D)
+            total = grad_ref[rows] + rate * (unit_back - mean_back - unit * mean_along)
+            residual_grad[rows] = total
+            attended_grad[rows] = (total * jnp.where(other, mods_ref[3:4], mods_ref[2:3])).astype(
+                jnp.bfloat16
+            )
+            for at, value in enumerate((slope * unit, slope, total * attended_ref[rows])):
+                second = jnp.sum(jnp.where(other, value, 0.0), axis=0, keepdims=True)
+                first_slot = jnp.sum(jnp.where(other, 0.0, value), axis=0, keepdims=True)
+                sums[2 * at] = sums[2 * at] + first_slot
+                sums[2 * at + 1] = sums[2 * at + 1] + second
+        for at in range(6):
+            rows_ref[at : at + 1] = sums[at]
+
+
+def dense_back(branch_grad, normed, pre, down, up, residual, grad, attended, token_columns, mods, head):
+    tokens, wide = pre.shape
+    depth = head.shape[5]
+    pairs = head.shape[6] // (2 * BACK_WIDTH)
+    f32, low = jnp.float32, jnp.bfloat16
+    width = DENSE_WIDTH
+
+    def fixed(*shape):
+        return pl.BlockSpec(shape, lambda i: (0,) * len(shape), pipeline_mode=pl.Buffered(1))
+
+    across = pl.BlockSpec((D, width), lambda i: (0, i))
+    along = pl.BlockSpec((width, D), lambda i: (i, 0))
+    shape = jax.ShapeDtypeStruct
+    return pl.pallas_call(
+        dense_back_kernel,
+        grid=(wide // width,),
+        out_shape=(
+            shape((D, wide), low),
+            shape((wide, D), low),
+            shape((tokens, D), f32),
+            shape((tokens, D), low),
+            shape((8, D), f32),
+            shape((pairs, depth, 2 * BACK_WIDTH), f32),
+        ),
+        in_specs=[
+            fixed(tokens, D),
+            fixed(tokens, D),
+            pl.BlockSpec((tokens, width), lambda i: (0, i)),
+            along,
+            across,
+            fixed(tokens, D),
+            fixed(tokens, D),
+            fixed(tokens, D),
+            fixed(tokens, 128),
+            fixed(8, D),
+            ANY,
+        ],
+        out_specs=(across, along, fixed(tokens, D), fixed(tokens, D), fixed(8, D), WHOLE),
+        scratch_shapes=[
+            pltpu.VMEM((D, tokens), low),
+            pltpu.VMEM((tokens, width), low),
+            pltpu.VMEM((tokens, width), low),
+            pltpu.VMEM((tokens, D), f32),
+        ]
+        + Scatter.scratch((depth, BACK_WIDTH), low, BACK_LAG),
+        compiler_params=params(5),
+        name="dense_backward",
+    )(branch_grad, normed, pre, down, up, residual, grad, attended, token_columns, mods, head)
+
+
 WEIGHT_COLUMNS = (CLASSES + CODE_DIM + LEVELS, 9, 6 * D, 3 * D, D, 4 * D, D, CODES)
 SUM_STARTS = (0, None, 1152, 1152 + 6144, 1152 + 9216, 1152 + 10240, 1152 + 14336, 1152 + 15360)
 SCALARS = 1152 + 19456
@@ -794,7 +1005,7 @@
     return jnp.sum(jnp.sum(values, axis=0, keepdims=True), axis=1, keepdims=True)
 
 
-def weight_tiles(tables_grad, ada_grad, done_attention, done_last, depth):
+def weight_tiles(tables_grad, ada_grad, done_head, done_attention, done_last):
     def blocks(ref, first, count, width):
         return [(lambda at=first + i: ref[at], i * width, width) for i in range(count)]
 
@@ -806,9 +1017,9 @@
         2: [(1, [(lambda: ada_grad[...], 0, 6 * D)])],
         3: [(2, blocks(done_last, D // near, 3 * D // near, near))],
         4: [(3, blocks(done_last, 0, D // near, near))],
-        5: [(4, blocks(done_attention, wide, wide, far))],
-        6: [(6 + part, blocks(done_attention, 2 * wide + part * (D // far), D // far, far)) for part in range(4)],
-        7: [(5, blocks(done_attention, 0, wide, far))],
+        5: [(4, blocks(done_attention, 0, wide, far))],
+        6: [(6 + part, blocks(done_attention, wide + part * (D // far), D // far, far)) for part in range(4)],
+        7: [(5, blocks(done_head, 0, wide, far))],
     }
 
 
@@ -853,6 +1064,7 @@
     cond_ref,
     hot_ref,
     loss_ref,
+    done_head,
     attention_ref,
     tables_ref,
     vectors_ref,
@@ -949,7 +1161,7 @@
     first_total = Total(place, *scratch[31:35])
     second_total = Total(place, *scratch[35:39])
     sums, facts = first_total.sums, scratch[39]
-    tiles = weight_tiles(tables_grad, ada_grad, attention_ref, done_ref, depth)
+    tiles = weight_tiles(tables_grad, ada_grad, done_head, attention_ref, done_ref)
     masters = (
         tables_ref,
         vectors_ref,
@@ -1068,7 +1280,8 @@
         load.wait()
     for index in range(4):
         norm_back(index)
-        scatter.step(next(steps))
+        if index % 2:
+            scatter.step(next(steps))
     gather_rows()
     beside = [
         partial(stats, 5),
@@ -1085,9 +1298,9 @@
         for step in steps:
             scatter.step(step)
             break
+    ada_part()
     for step in steps:
         scatter.step(step)
-    ada_part()
     stats(0)
     stats(2)
     stats(3)
@@ -1134,13 +1347,13 @@
     facts_ref[2] = sums[5, :, SCALARS:]
 
 
-def last_exchange(far, near, attention_done, masters, moments):
+def last_exchange(far, near, done, masters, moments):
     depth = far[0].shape[5]
     pairs = 4 * D // (2 * LAST_WIDTH)
     dma = pltpu.SemaphoreType.DMA
     f32, low = jnp.float32, jnp.bfloat16
     tokens = far[2].shape[0]
-    operands = list(far) + list(near) + [attention_done] + list(masters) + list(moments)
+    operands = list(far) + list(near) + list(done) + list(masters) + list(moments)
     return pl.pallas_call(
         last_kernel,
         out_shape=(
@@ -1189,6 +1402,7 @@
     rows_ref,
     columns_ref,
     facts_ref,
+    done_head,
     attention_ref,
     vector_moment_ref,
     tables_ref,
@@ -1213,7 +1427,7 @@
         head_master,
     )
     vector_stat = outs[16]
-    tiles = weight_tiles(tables_grad, ada_grad, attention_ref, done_ref, depth)
+    tiles = weight_tiles(tables_grad, ada_grad, done_head, attention_ref, done_ref)
     for position, groups in tiles.items():
         grad_ref, next_ref, master = outs[2 * position], outs[2 * position + 1], masters[position]
         factor = facts_ref[1, :, position : position + 1]
@@ -1236,8 +1450,8 @@
     outs[3][...] = vectors_ref[...] - facts_ref[1, :, 1:2] * (gradient * lax.rsqrt(moment))
 
 
-def take_step(last, attention_done, vector_moment, masters):
-    operands = list(last) + [attention_done, vector_moment] + list(masters)
+def take_step(last, done, vector_moment, masters):
+    operands = list(last) + list(done) + [vector_moment] + list(masters)
     shapes = []
     for master in masters:
         shapes += [jax.ShapeDtypeStruct(master.shape, jnp.float32)] * 2
@@ -1337,8 +1551,18 @@
     out_low = out_weight.astype(low)
     down_low = down_weight.astype(low)
 
-    full_up = gathered(up_weight.astype(low))
-    full_head = gathered(head_weight.astype(low))
+    if linked:
+        cores = [[core + 2 * chip for chip in range(devices // 2)] for core in range(2)]
+        up_head = lax.all_gather(
+            jnp.concatenate([up_weight, head_weight], axis=1).astype(low),
+            AXES,
+            axis_index_groups=cores,
+            axis=0,
+            tiled=True,
+        ).reshape(2, 2, 2, 2, depth, -1)
+    else:
+        full_up = gathered(up_weight.astype(low))
+        full_head = gathered(head_weight.astype(low))
     small_rows = jnp.concatenate(
         [vectors.astype(low), tables_low[:, CLASSES:], jnp.zeros((depth, 128 - SMALL_LANES), low)], axis=1
     )
@@ -1395,8 +1619,11 @@
         of_token(block) for block in range(6)
     )
     if linked:
-        mixed_heads, exact, totals, full_down = attend(projected, gains, bias, down_low, depth)
+        mixed_heads, exact, totals, full_down, full_up, full_head = attend(
+            projected, gains, bias, down_low, up_head
+        )
         full_down = full_down.reshape(-1, D)
+        full_up, full_head = full_up.reshape(D, -1), full_head.reshape(D, -1)
     else:
         normed = modulate(embedded, scale_one, shift_one).astype(low)
         projected = bfloat_product(normed, full_qkv)
@@ -1438,18 +1665,35 @@
         return jnp.stack([first, other])
 
     gamma_two_grad = slot_sums(residual_grad * branch)
-    down_part = bfloat_product(hidden_act.T, branch_grad).astype(part_kind)
-    act_grad = bfloat_product(branch_grad, full_down.T)
-    _, gelu_back = jax.vjp(partial(jax.nn.gelu, approximate=True), hidden_pre)
-    pre_grad = gelu_back(act_grad)[0].astype(low)
-    up_part = bfloat_product(normed_two.T, pre_grad).astype(part_kind)
-    normed_two_grad = bfloat_product(pre_grad, full_up.T)
-    _, modulate_two_back = jax.vjp(modulate, residual_one, scale_two, shift_two)
-    norm_grad, scale_two_grad, shift_two_grad = modulate_two_back(normed_two_grad)
-    scale_two_grad, shift_two_grad = slot_sums(scale_two_grad), slot_sums(shift_two_grad)
-    residual_grad = residual_grad + norm_grad
-    attended_grad = (gamma_one * residual_grad).astype(low)
-    gamma_one_grad = slot_sums(residual_grad * attended)
+    if linked:
+        mods = jnp.concatenate([modulation[:, 3 * D : 4 * D], modulation[:, :D], jnp.zeros((4, D), jnp.float32)])
+        up_part, down_part, residual_grad, attended_grad, slot_rows, head_done = dense_back(
+            branch_grad,
+            normed_two,
+            hidden_pre,
+            full_down,
+            full_up,
+            residual_one,
+            residual_grad,
+            attended,
+            token_columns,
+            mods,
+            head_part.reshape(FIVE + (depth, CODES)),
+        )
+        scale_two_grad, shift_two_grad, gamma_one_grad = slot_rows[0:2], slot_rows[2:4], slot_rows[4:6]
+    else:
+        down_part = bfloat_product(hidden_act.T, branch_grad).astype(part_kind)
+        act_grad = bfloat_product(branch_grad, full_down.T)
+        _, gelu_back = jax.vjp(partial(jax.nn.gelu, approximate=True), hidden_pre)
+        pre_grad = gelu_back(act_grad)[0].astype(low)
+        up_part = bfloat_product(normed_two.T, pre_grad).astype(part_kind)
+        normed_two_grad = bfloat_product(pre_grad, full_up.T)
+        _, modulate_two_back = jax.vjp(modulate, residual_one, scale_two, shift_two)
+        norm_grad, scale_two_grad, shift_two_grad = modulate_two_back(normed_two_grad)
+        scale_two_grad, shift_two_grad = slot_sums(scale_two_grad), slot_sums(shift_two_grad)
+        residual_grad = residual_grad + norm_grad
+        attended_grad = (gamma_one * residual_grad).astype(low)
+        gamma_one_grad = slot_sums(residual_grad * attended)
     out_part = bfloat_product(mixed_heads.T, attended_grad).astype(part_kind)
     mixed_grad = bfloat_product(attended_grad, full_out.T).astype(low)
     if linked:
@@ -1460,7 +1704,6 @@
             totals,
             gains,
             turned_bias,
-            head_part.reshape(FIVE + (depth, CODES)),
             up_part.reshape(FIVE + (depth, up_part.shape[1])),
             down_part.reshape(FIVE + (down_part.shape[0] // D, depth, D)),
         )
@@ -1494,11 +1737,11 @@
                 label_hot,
                 local_loss[None, None],
             ),
-            attention_done,
+            (head_done, attention_done),
             masters,
             (row_moments, vector_moment, column_moments),
         )
-        stepped = take_step(last, attention_done, vector_moment, masters)
+        stepped = take_step(last, (head_done, attention_done), vector_moment, masters)
         rows_new, cols_new, facts = last[4].reshape(10 * depth), last[5][0], last[6][:, 0]
         stats = [rows_new[i * depth : (i + 1) * depth] for i in range(6)] + [rows_new[6 * depth :]]
         moment_of = (stats[0], stepped[16], stats[1], stats[2], stats[3], stats[4], stats[6], stats[5])

time: 704 us -> 669 us (0.950)
  matrix products: 174 us -> 86.9 us
  Pallas kernels: 438 us -> 489 us
  waiting for transfers between devices: 0.08 us -> 8.97 us
    dot_general x12 -> x8, matrix products: 174 us -> 86.9 us  [bfloat_product(): return jnp.dot(left_side, right_side, preferred_element_type=jnp.float32)]
    pallas_call x0 -> x1, Pallas kernels: none -> 84.5 us  [dense_back(): pl.pallas_call(dense_back_kernel, grid=(wide // width,), out_shape=(shape...]
    pallas_call x1, Pallas kernels: 125 us -> 106 us  [attend_back(): pl.pallas_call(partial(attend_back_kernel, linked), grid=(HEADS // 2,), o...]
    pallas_call x1, Pallas kernels: 80 us -> 64.6 us  [attend(): pl.pallas_call(partial(attend_kernel, linked), grid=(HEADS // 2,), out_sh...]
    all_gather x2 -> x1, waiting for transfers between devices: 0.04 us -> 8.95 us  [on_device(): lax.all_gather(jnp.concatenate([up_weight, head_weight], axis=1).astype(l...]
  transfers between devices with their start and end apart: 2 -> 1, of which waited for: 0 -> 1; matrix products, arithmetic and copies ran while one was open for 9% -> 3% of each run, Pallas kernels for 28% -> 18%
where the time goes in v4:
time: 669 us; the launch traced here: 665 us
  Pallas kernels  489 us (73%)
  matrix products  86.9 us (13%)
  other arithmetic  37.4 us (6%)
  local copies, waits for them, and re-layouts  27.1 us (4%)
  between operations  15.5 us (2%)
  waiting for transfers between devices  8.97 us (1%)
    pallas_call x1, Pallas kernels, begin(): pl.pallas_call(begin_kernel, out_shape=(shape((tokens, 3 * D), f32), shap...  116 us
    pallas_call x1, Pallas kernels, last_exchange(): pl.pallas_call(last_kernel, out_shape=(jax.ShapeDtypeStruct((pairs, depth...  111 us
    pallas_call x1, Pallas kernels, attend_back(): pl.pallas_call(partial(attend_back_kernel, linked), grid=(HEADS // 2,), o...  106 us
    dot_general x8, matrix products, bfloat_product(): return jnp.dot(left_side, right_side, preferred_element_type=jnp.float32)  86.9 us
    pallas_call x1, Pallas kernels, dense_back(): pl.pallas_call(dense_back_kernel, grid=(wide // width,), out_shape=(shape...  84.5 us
    pallas_call x1, Pallas kernels, attend(): pl.pallas_call(partial(attend_kernel, linked), grid=(HEADS // 2,), out_sh...  64.6 us
  transfers between devices with their start and end apart: 1, of which 1 were waited for; matrix products, arithmetic and copies ran while one was open for 3% of the time, Pallas kernels for 18%

profile of v4, /device:TPU:0, one launch (start us, length us, event | category | flops | bytes accessed | tf_op | source)
XLA Modules:
  0.0 665.0 jit_solution(127527167176933733)
XLA Ops:
  7.3 1.1 convert.8
  8.4 1.1 convert.7
  9.6 0.8 pad_maximum_fusion
  10.5 0.8 slice.195
  11.3 0.7 convert_element_type.61
  12.1 1.3 reduce_sum.113
  14.1 0.7 convert_element_type.63
  14.7 0.7 fusion.12
  15.4 0.9 pad_maximum_fusion.1
  16.5 1.0 stack.29
  17.7 0.8 pad.8.codes_ref
  18.6 0.8 pad.9.token_columns
  19.5 0.6 fusion.26
  20.1 0.7 maximum_maximum_fusion.2.rows_ref
  20.7 0.7 broadcast_in_dim.158.tags_ref
  21.4 116.5 %begin.1 = (f32[1024,3072]{1,0:T(8,128)}, bf16[2,2,2,2,2,32,3072]{6,5,4,3,2,1,0:T(8,128)(2,1)}, bf16[2,2,2,2,2,32,1024]{6,5,4,3,2,1,0:T(8,128)(2,1)}, f32[1024,1...) custom-call(bf16[32,128]{1,0:T(8,128)(2,1)} %maximum_maximum_fusion., ...), custom_call_target="tpu_custom_call" | custom-call | tf_op jit(solution)/shard_map/begin/pallas_call | solution.py:472
  137.9 1.5 slice.140.gain_ref
  139.3 0.8 slice.149
  140.1 0.7 copy.115.vectors_ref
  140.9 0.7 convert_element_type.67.refs_0_
  141.6 1.2 slice.150
  142.8 1.0 copy.114.second_ref
  144.0 0.9 reshape.173.moments_ref
  144.9 0.7 copy.117.vector_moment_ref
  145.6 0.7 broadcast_in_dim.186.column_moment_ref
  146.4 1.3 fusion.24
  147.7 0.7 maximum_maximum_fusion.mods_ref
  148.4 0.8 fusion.25
  149.3 8.9 %all-gather.2.cloned.1.call-done = bf16[512,8192]{1,0:T(8,128)(2,1)} async-done(((bf16[32,8192]{1,0:T(8,128)(2,1)}), bf16[512,8192]{1,0:T(8,128)(2,1)}) %all-gather.2.cloned.1.call-update) | async-done | bytes 8388624 | tf_op jit(solution)/shard_map/all_gather | solution.py:1556
  158.2 64.6 %attention_forward.1 = (bf16[1024,1024]{1,0:T(8,128)(2,1)}, f32[1024,1024]{1,0:T(8,128)}, f32[1024,1024]{1,0:T(8,128)}, bf16[2,2,2,2,2,4,32,1024]{7,6,5,4,3,2,1,...) custom-call(f32[1024,3072]{1,0:T(8,128)} %get-tuple-element.80.q_ref.k_ref.v_ref, ...), custom_call_target="tpu_custom_call" | custom-call | tf_op jit(solution)/shard_map/attention_forward/pallas_call | solution.py:681
  222.9 7.0 %fusion.23 = (f32[1024]{0:T(1024)S(1)}, f32[1024,1024]{1,0:T(8,128)S(1)}, f32[1024,1024]{1,0:T(8,128)}) fusion(f32[1024,1024]{1,0:T(8,128)S(1)} %copy-done.2, f32[1024]{0:T(1024)S(1)} %bitcast.72, f32[1024]{0:T(1024)S(1)} %bitcast.73, pred[1024]{0:T(1024)(128)(4,1)S(1)} %get-tuple-element.260, bf16[1024,1024]{1,0:T(8,128)(2,1)} %get-tuple-element.83, ...), kind=kOutput, calls=%fused_computation.77 | convolution fusion | flops 2151676928 | bytes 16790528 | tf_op jit(solution)/shard_map/dot_general | solution.py:46
  229.9 0.6 multiply_reduce_fusion.3
  230.5 5.0 add_convert_fusion.normed_ref
  235.5 11.6 %fusion.28.pre_ref = f32[1024,4096]{1,0:T(8,128)} fusion(bf16[1024,1024]{1,0:T(8,128)(2,1)S(1)} %add_convert_fusion.normed_ref, bf16[1024,4096]{1,0:T(8,128)(2,1)S(1)} %bitcast.55), kind=kOutput, calls=%fused_computation.82 | convolution fusion | flops 8589934592 | bytes 27262976 | tf_op jit(solution)/shard_map/dot_general | solution.py:46
  247.1 18.5 %fusion.21 = (f32[1024]{0:T(1024)S(1)}, f32[1024,1024]{1,0:T(8,128)S(1)}, f32[1024,1024]{1,0:T(8,128)}) fusion(f32[1024,1024]{1,0:T(8,128)S(1)} %get-tuple-element.266.residual_ref, f32[1024]{0:T(1024)S(1)} %bitcast.85, f32[1024]{0:T(1024)S(1)} %bitcast.83, pred[1024]{0:T(1024)(128)(4,1)S(1)} %get-tuple-element.260, bf16[4096,1024]{1,0:T(8,128)(2,1)} %bitcast.50, ...), kind=kOutput, calls=%fused_computation.76 | convolution fusion | flops 8631876608 | bytes 37762048 | tf_op jit(solution)/shard_map/dot_general | solution.py:46
  266.2 11.7 %fusion.27 = (f32[1024]{0:T(1024)S(1)}, f32[1024,4096]{1,0:T(8,128)S(1)}) fusion(bf16[1024,4096]{1,0:T(8,128)(2,1)} %bitcast.94, f32[1024,1024]{1,0:T(8,128)S(1)} %get-tuple-element.264, f32[1024]{0:T(1024)S(1)} %bitcast.74, f32[1024]{0:T(1024)S(1)} %fusion.13, f32[1024]{0:T(1024)S(1)} %broadcast_multiply_fusion), kind=kOutput, calls=%fused_computation.81 | convolution fusion | flops 8598322176 | bytes 29376512 | tf_op jit(solution)/shard_map/dot_general | solution.py:46
  277.9 5.6 select_reduce_fusion
  283.5 1.3 multiply_reduce_fusion.4
  284.8 7.8 %multiply_convert_fusion = bf16[1024,4096]{1,0:T(8,128)(2,1)} fusion(f32[1024,4096]{1,0:T(8,128)S(1)} %get-tuple-element.284, f32[1024]{0:T(1024)S(1)} %get-tuple-element.278, s32[1024]{0:T(1024)S(1)} %copy-done.13, f32[1024]{0:T(1024)S(1)} %get-tuple-element.257), kind=kLoop, calls=%fused_computation.10 | loop fusion | flops 25165824 | bytes 25178112 | tf_op jit(solution)/shard_map/convert_element_type | solution.py:1654
  292.6 15.7 %multiply_reduce_fusion = (f32[1024]{0:T(1024)S(1)}, f32[1024]{0:T(1024)S(1)}, f32[1024,1024]{1,0:T(8,128)S(1)}) fusion(f32[1024,1024]{1,0:T(8,128)S(1)} %get-tuple-element.264, f32[1024]{0:T(1024)S(1)} %fusion.13, f32[1024]{0:T(1024)S(1)} %broadcast_multiply_fusion, f32[1024]{0:T(1024)S(1)} %bitcast.75, bf16[1024,4096]{1,0:T(8,128)(2,1)} %multiply_convert_fusion, ...), kind=kOutput, calls=%fused_computation.20 | convolution fusion | flops 8597272576 | bytes 25186304 | tf_op jit(solution)/shard_map/dot_general | solution.py:46
  308.3 12.5 %convolution_convert_fusion = bf16[1024,4096]{1,0:T(8,128)(2,1)} fusion(bf16[1024,4096]{1,0:T(8,128)(2,1)S(1)} %copy-done.3, f32[1024,1024]{1,0:T(8,128)S(1)} %get-tuple-element.264, f32[1024]{0:T(1024)S(1)} %bitcast.76, f32[1024]{0:T(1024)S(1)} %fusion.13, f32[1024]{0:T(1024)S(1)} %broadcast_multiply_fusion), kind=kOutput, calls=%fused_computation.14 | convolution fusion | flops 8598323200 | bytes 20983808 | tf_op jit(solution)/shard_map/dot_general | solution.py:46
  320.8 1.9 fusion.20
  323.0 1.3 select_reduce_fusion.2
  324.3 2.1 fusion.11.branch_ref
  326.4 0.6 copy-done.1
  327.0 84.5 %dense_backward.1 = (bf16[1024,4096]{1,0:T(8,128)(2,1)}, bf16[4096,1024]{1,0:T(8,128)(2,1)}, f32[1024,1024]{1,0:T(8,128)}, bf16[1024,1024]{1,0:T(8,128)(2,1)}, f32[8,1024]{1,0:T(8,128)}, /*index=5*/f32[8,32,512]{2,1,0:T(8,128)}) custom-call(bf16[1024,1024]{1,0:T(8,128)(2,1)} %fusion.11.branch_ref, bf16[1024,1024]{1,0:T(8,128)(2,1)} %copy-done.4, ...), custom_call_target="tpu_custom_call" | custom-call | tf_op jit(solution)/shard_map/dense_backward/pallas_call | solution.py:944
  411.5 6.1 convolution_convert_fusion.2
  417.6 3.8 convolution_convert_fusion.1.m_ref
  421.5 106.0 %attention_backward.1 = (bf16[3,1024,1024]{2,1,0:T(8,128)(2,1)}, f32[8,1024]{1,0:T(8,128)}, f32[16,32,512]{2,1,0:T(8,128)}) custom-call(f32[1024,3072]{1,0:T(8,128)} %get-tuple-element.80.q_ref.k_ref.v_ref, f32[1024,3072]{1,0:T(8,128)} %get-tuple-element.80.q_ref.k_ref.v_ref, f32[1024,3072]{1,0:T(8,128)} %get-tuple-element.80.q_ref.k_ref.v_ref, ...), custom_call_target="tpu_custom_call" | custom-call | tf_op jit(solution)/shard_map/attention_backward/pallas_call | solution.py:815
  527.6 0.8 slice.157
  528.4 0.7 maximum_maximum_fusion.1.gains_ref
  529.0 111.5 %last_scatter.1 = (f32[8,32,512]{2,1,0:T(8,128)}, f32[32,128]{1,0:T(8,128)}, f32[32,1152]{1,0:T(8,128)}, f32[32,6144]{1,0:T(8,128)}, f32[10,32,1]{2,1,0:T(8,128)...) custom-call(bf16[2,2,2,2,2,32,1024]{6,5,4,3,2,1,0:T(8,128)(2,1)} %bitcast.63, bf16[1024,3072]{1,0:T(8,128)(2,1)} %bitcast.60, ...), custom_call_target="tpu_custom_call" | custom-call | tf_op jit(solution)/shard_map/last_scatter/pallas_call | solution.py:1357
  640.5 1.5 slice_reduce_fusion.1
  642.1 0.9 slice_reduce_fusion
  643.0 0.9 slice.177
  643.9 0.7 slice_reduce_fusion.7
  644.6 0.7 copy.127
  645.3 0.6 slice.160
  646.4 6.1 weight_step.1
  652.4 1.4 copy.120
  653.8 1.4 copy.121
  655.2 1.4 copy.122
  656.6 0.6 slice.172
  657.2 0.7 pad_maximum_fusion.2
  (90 shorter events, 2.6 us)
Async XLA Ops:
  7.2 132.9 %copy-start.11 = (f32[32,9]{0,1:T(8,128)S(1)}, f32[32,9]{0,1:T(8,128)}, u32[]{:S(2)}) copy-start(f32[32,9]{0,1:T(8,128)} %param.32) | copy-start | bytes 3460
  7.2 133.6 %copy-start.9 = (f32[20498]{0:T(1024)S(1)}, f32[20498]{0:T(1024)}, u32[]{:S(2)}) copy-start(f32[20498]{0:T(1024)} %param.47) | copy-start | bytes 245980
  7.2 133.6 %copy-start.5 = (f32[128,1024]{1,0:T(8,128)S(1)}, f32[128,1024]{1,0:T(8,128)}, u32[]{:S(2)}) copy-start(f32[128,1024]{1,0:T(8,128)} %down_master.3) | copy-start | bytes 1572868
  7.2 151.0 %all-gather.2.cloned.1.call-start = ((), (), s32[]{:S(2)}) async-start(), calls=%async_computation | async-start | bytes 8912896 | tf_op jit(solution)/shard_map/all_gather | solution.py:1556
  8.4 134.4 %copy-start.15 = (s32[1024]{0:T(1024)S(1)}, s32[1024]{0:T(1024)}, u32[]{:S(2)}) copy-start(s32[1024]{0:T(1024)} %param.26) | copy-start | bytes 12292
  9.5 134.3 %copy-start.18 = (f32[32]{0:T(128)S(1)}, f32[32]{0:T(128)}, u32[]{:S(2)}) copy-start(f32[32]{0:T(128)} %param.39) | copy-start | bytes 388
  9.5 134.3 %copy-start.19 = (f32[32]{0:T(128)S(1)}, f32[32]{0:T(128)}, u32[]{:S(2)}) copy-start(f32[32]{0:T(128)} %param.40) | copy-start | bytes 388
  9.5 134.3 %copy-start.20 = (f32[32]{0:T(128)S(1)}, f32[32]{0:T(128)}, u32[]{:S(2)}) copy-start(f32[32]{0:T(128)} %param.41) | copy-start | bytes 388
  9.5 134.3 %copy-start.21 = (f32[32]{0:T(128)S(1)}, f32[32]{0:T(128)}, u32[]{:S(2)}) copy-start(f32[32]{0:T(128)} %param.42) | copy-start | bytes 388
  9.6 134.3 %copy-start.22 = (f32[32]{0:T(128)S(1)}, f32[32]{0:T(128)}, u32[]{:S(2)}) copy-start(f32[32]{0:T(128)} %param.43) | copy-start | bytes 388
  9.6 134.3 %copy-start.23 = (f32[32]{0:T(128)S(1)}, f32[32]{0:T(128)}, u32[]{:S(2)}) copy-start(f32[32]{0:T(128)} %param.45) | copy-start | bytes 388
  9.6 134.3 %copy-start.24 = (f32[128]{0:T(128)S(1)}, f32[128]{0:T(128)}, u32[]{:S(2)}) copy-start(f32[128]{0:T(128)} %param.44) | copy-start | bytes 1540
  9.6 135.3 %copy-start.16 = (f32[32,9]{0,1:T(8,128)S(1)}, f32[32,9]{0,1:T(8,128)}, u32[]{:S(2)}) copy-start(f32[32,9]{0,1:T(8,128)} %param.46) | copy-start | bytes 3460
  9.6 135.9 %slice-start.2 = ((f32[20498]{0:T(1024)}), f32[1042]{0:T(1024)S(1)}, s32[]{:S(2)}) async-start(f32[20498]{0:T(1024)} %param.47), calls=%async_computation.3 | async-start | bytes 16384 | tf_op jit(solution)/shard_map/slice | solution.py:1719
  17.5 3.9 copy-start.8
  158.2 64.6 %copy-start.2 = (f32[1024,1024]{1,0:T(8,128)S(1)}, f32[1024,1024]{1,0:T(8,128)}, u32[]{:S(2)}) copy-start(f32[1024,1024]{1,0:T(8,128)} %get-tuple-element.85.embedded_ref) | copy-start | bytes 12582916
  222.8 12.6 %slice-start = ((s8[8388608]{0:T(1024)(128)(4,1)}), s8[4194304]{0:T(1024)(128)(4,1)S(1)}, s32[]{:S(2)}) async-start(s8[8388608]{0:T(1024)(128)(4,1)} %bitcast.53), calls=%async_computation.1 | async-start | bytes 8388608
  222.8 12.6 %slice-start.1 = ((s8[8388608]{0:T(1024)(128)(4,1)}), s8[4194304]{0:T(1024)(128)(4,1)S(1)}, s32[]{:S(2)}) async-start(s8[8388608]{0:T(1024)(128)(4,1)} %bitcast.53), calls=%async_computation.2 | async-start | bytes 8388608
  229.9 17.2 %copy-start = (f32[1024,1024]{1,0:T(8,128)}, f32[1024,1024]{1,0:T(8,128)S(1)}, u32[]{:S(2)}) copy-start(f32[1024,1024]{1,0:T(8,128)S(1)} %get-tuple-element.266.residual_ref) | copy-start | bytes 12582916
  235.4 11.7 %copy-start.4 = (bf16[1024,1024]{1,0:T(8,128)(2,1)}, bf16[1024,1024]{1,0:T(8,128)(2,1)S(1)}, u32[]{:S(2)}) copy-start(bf16[1024,1024]{1,0:T(8,128)(2,1)S(1)} %add_convert_fusion.normed_ref) | copy-start | bytes 6291460
  266.1 11.8 %copy-start.13 = (s32[1024]{0:T(1024)S(1)}, s32[1024]{0:T(1024)}, u32[]{:S(2)}) copy-start(s32[1024]{0:T(1024)} %param.29) | copy-start | bytes 12292
  277.9 5.6 copy-start.14
  292.6 15.7 %copy-start.3 = (bf16[1024,4096]{1,0:T(8,128)(2,1)S(1)}, bf16[1024,4096]{1,0:T(8,128)(2,1)}, u32[]{:S(2)}) copy-start(bf16[1024,4096]{1,0:T(8,128)(2,1)} %multiply_convert_fusion) | copy-start | bytes 25165828
  320.8 2.2 copy-start.6
  324.3 2.7 copy-start.1
  411.5 6.1 copy-start.7
  411.5 6.1 copy-start.25
  417.6 3.8 copy-start.12
  421.5 106.1 %copy-start.10 = (f32[2,6144]{1,0:T(2,128)}, f32[2,6144]{1,0:T(2,128)S(1)}, u32[]{:S(2)}) copy-start(f32[2,6144]{1,0:T(2,128)S(1)} %constant_dynamic-update-slice_fusion.known_ref) | copy-start | bytes 147460
  421.5 106.8 %copy-start.17 = (f32[8]{0:T(128)S(1)}, f32[8]{0:T(128)}, u32[]{:S(2)}) copy-start(f32[8]{0:T(128)} %get-tuple-element.279) | copy-start | bytes 100
Sparse Core Ops, SparseCore 0:
  11.4 146.7 all-gather.1

commit v5 on v4

--- a/solution.py
+++ b/solution.py
@@ -38,7 +38,7 @@
 VMEM_GRANT = 58 * 1024 * 1024
 FIRST_WIDTH, FIRST_LAG = 256, 2
 ATTEND_WIDTH, ATTEND_LAG = 128, 3
-BACK_WIDTH, BACK_LAG = 256, 2
+BACK_WIDTH, BACK_LAG = 256, 3
 LAST_WIDTH, LAST_LAG = 256, 2
 
 
@@ -153,15 +153,27 @@
         self.sends, self.recvs, self.keep_sems = scratch[10:13]
         self.first, self.end = groups[0][0], groups[-1][1]
         self.steps = self.end + 5 * lag
+        rows, lanes = self.land[4].shape[2:]
+        by_rows = self.keep.shape[5] != rows
+        self.parts = [
+            (slice(None),) * 4
+            + (
+                (slice(p * rows, (p + 1) * rows), slice(None))
+                if by_rows
+                else (slice(None), slice(p * lanes, (p + 1) * lanes))
+            )
+            for p in range(2)
+        ]
 
     @staticmethod
-    def scratch(piece, kind, lag=1):
+    def scratch(piece, kind, lag=1, by_rows=False):
         dma = pltpu.SemaphoreType.DMA
+        whole = (2 * piece[0], piece[1]) if by_rows else (piece[0], 2 * piece[1])
         return (
-            [pltpu.VMEM((lag, 2) + (2,) * 4 + piece, kind)]
-            + [pltpu.VMEM((2 * lag, 2) + (2,) * (4 - k) + piece, kind) for k in range(5)]
+            [pltpu.VMEM((lag,) + (2,) * 4 + whole, kind), pltpu.VMEM((2 * lag,) + (2,) * 4 + whole, kind)]
+            + [pltpu.VMEM((2 * lag, 2) + (2,) * (4 - k) + piece, kind) for k in range(1, 5)]
             + [pltpu.VMEM((lag, 2) + (2,) * (5 - k) + piece, kind) for k in range(1, 5)]
-            + [dma((5, 2, 2 * lag)), dma((5, 2, 2 * lag)), dma((2, lag))]
+            + [dma((5, 2, 2 * lag)), dma((5, 2, 2 * lag)), dma((lag,))]
         )
 
     def half(self, stage, parity, other):
@@ -169,22 +181,37 @@
         left = [d for d in DIMS if d not in order[:stage]]
         bit = self.place.bit[order[stage]]
         value = 1 - bit if other else bit
-        return (parity,) + tuple(value if d == order[stage] else slice(None) for d in left)
-
-    def copy(self, stage, parity, j, source=None):
-        slot = lax.rem(j, 2 * self.lag)
-        if source is None:
-            if stage == 0:
-                source = self.keep.at[lax.rem(j, self.lag), parity]
-            else:
-                source = self.sums[stage].at[(lax.rem(j, self.lag),) + self.half(stage, parity, True)]
-        return self.place.send(
-            source,
-            self.land[stage].at[slot, parity],
-            self.sends.at[stage, parity, slot],
-            self.recvs.at[stage, parity, slot],
-            SCATTER_ORDERS[parity][stage],
-        )
+        return tuple(value if d == order[stage] else slice(None) for d in left)
+
+    def copies(self, stage, j, source=None):
+        slot, near = lax.rem(j, 2 * self.lag), lax.rem(j, self.lag)
+        if stage == 0:
+            pieces = [(self.keep.at[near] if source is None else source, self.land[0].at[slot])]
+        elif stage < 3:
+            pieces = [
+                (
+                    self.sums[stage].at[(near, parity) + self.half(stage, parity, True)],
+                    self.land[stage].at[slot, parity],
+                )
+                for parity in range(2)
+            ]
+        else:
+            at = (near, slice(None)) + self.half(stage, 0, True)
+            pieces = [(self.sums[stage].at[at], self.land[stage].at[slot])]
+        return [
+            self.place.send(
+                piece,
+                target,
+                self.sends.at[stage, parity, slot],
+                self.recvs.at[stage, parity, slot],
+                SCATTER_ORDERS[parity][stage],
+            )
+            for parity, (piece, target) in enumerate(pieces)
+        ]
+
+    def kept(self, j):
+        near = lax.rem(j, self.lag)
+        return self.keep.at[near], self.keep_sems.at[near]
 
     def step(self, t):
         for stage in reversed(range(6)):
@@ -192,39 +219,42 @@
 
             def body(stage=stage, j=j):
                 slot, near = lax.rem(j, 2 * self.lag), lax.rem(j, self.lag)
-                for parity in range(2):
-                    before = stage - 1
-                    if before == 0:
-                        pltpu.make_async_copy(
-                            self.keep.at[near, parity],
-                            self.keep.at[near, parity],
-                            self.keep_sems.at[parity, near],
-                        ).wait()
-                    self.copy(before, parity, j).wait()
-                    if before == 0:
-                        mine = self.keep[near, parity]
+                before = stage - 1
+                if before == 0:
+                    keep, sem = self.kept(j)
+                    pltpu.make_async_copy(keep, keep, sem).wait()
+                for copy in self.copies(before, j):
+                    copy.wait()
+                if before < 3:
+                    for parity in range(2):
+                        if before == 0:
+                            mine = self.keep[(near,) + self.parts[parity]]
+                            landed = self.land[0][(slot,) + self.parts[parity]]
+                        else:
+                            mine = self.sums[before][(near, parity) + self.half(before, parity, False)]
+                            landed = self.land[before][slot, parity]
+                        self.sums[stage][near, parity] = mine + landed
+                else:
+                    mine = self.sums[before][(near, slice(None)) + self.half(before, 0, False)]
+                    landed = self.land[before][slot]
+                    if stage < 5:
+                        self.sums[stage][near] = mine + landed
                     else:
-                        mine = self.sums[before][(near,) + self.half(before, parity, False)]
-                    landed = self.land[before][slot, parity]
-                    if stage < 5:
-                        self.sums[stage][near, parity] = mine + landed
-                        self.copy(stage, parity, j).start()
-                    else:
-                        self.store(j, parity, mine.astype(jnp.float32) + landed.astype(jnp.float32))
+                        total = mine.astype(jnp.float32) + landed.astype(jnp.float32)
+                        for parity in range(2):
+                            self.store(j, parity, total[parity])
+                if stage < 5:
+                    for copy in self.copies(stage, j):
+                        copy.start()
 
             if stage == 0:
                 for low, high, source in self.groups:
 
                     def begin(source=source, j=j):
-                        near = lax.rem(j, self.lag)
                         core = self.place.bit["c"]
-                        for parity in range(2):
-                            self.copy(0, parity, j, source(j, parity, 1 - core)).start()
-                            pltpu.make_async_copy(
-                                source(j, parity, core),
-                                self.keep.at[near, parity],
-                                self.keep_sems.at[parity, near],
-                            ).start()
+                        for copy in self.copies(0, j, source(j, 1 - core)):
+                            copy.start()
+                        pltpu.make_async_copy(source(j, core), *self.kept(j)).start()
 
                     when_in(j, low, high, begin)
             else:
@@ -701,14 +731,14 @@
         parts = down_ref.shape[5]
 
         def columns_of(ref, first):
-            return lambda j, p, core: ref.at[
-                :, :, :, :, core, :, columns((2 * (j - first) + p) * width, width)
+            return lambda j, core: ref.at[
+                :, :, :, :, core, :, columns(2 * (j - first) * width, 2 * width)
             ]
 
-        def down_source(j, p, core):
+        def down_source(j, core):
             spread = j - wide
             part, column = lax.div(spread, narrow), lax.rem(spread, narrow)
-            return down_ref.at[:, :, :, :, core, part, :, columns((2 * column + p) * width, width)]
+            return down_ref.at[:, :, :, :, core, part, :, columns(2 * column * width, 2 * width)]
 
         def store(j, parity, total):
             done_ref[j, :, parity * width : (parity + 1) * width] = total
@@ -866,7 +896,7 @@
             (
                 0,
                 pairs,
-                lambda j, p, core: head_ref.at[:, :, :, :, core, :, columns((2 * j + p) * width, width)],
+                lambda j, core: head_ref.at[:, :, :, :, core, :, columns(2 * j * width, 2 * width)],
             )
         ],
         store,
@@ -1103,8 +1133,8 @@
         load.start()
 
     def columns_of(ref, first):
-        return lambda j, p, core: ref.at[
-            :, :, :, :, core, :, columns((2 * (j - first) + p) * width, width)
+        return lambda j, core: ref.at[
+            :, :, :, :, core, :, columns(2 * (j - first) * width, 2 * width)
         ]
 
     def store(j, parity, total):
@@ -1129,7 +1159,7 @@
 
     small = Scatter(
         place,
-        [(0, 1, lambda j, p, core: small_ref.at[:, :, :, :, core, pl.ds(p * half, half)])],
+        [(0, 1, lambda j, core: small_ref.at[:, :, :, :, core])],
         small_store,
         scratch[13:26],
     )
@@ -1368,7 +1398,7 @@
         in_specs=[ANY] * 4 + [WHOLE] * (len(operands) - 4),
         out_specs=(WHOLE,) * 7,
         scratch_shapes=Scatter.scratch((depth, LAST_WIDTH), low, LAST_LAG)
-        + Scatter.scratch((depth // 2, 128), f32)
+        + Scatter.scratch((depth // 2, 128), f32, 1, True)
         + [
             pltpu.VMEM((2, 16, 6 * D), low),
             pltpu.VMEM((3, 16, 6 * D), low),

time: 669 us -> 661 us (0.988)
  Pallas kernels: 489 us -> 482 us
where the time goes in v5:
time: 661 us; the launch traced here: 658 us
  Pallas kernels  482 us (73%)
  matrix products  86.9 us (13%)
  other arithmetic  37.4 us (6%)
  local copies, waits for them, and re-layouts  27.1 us (4%)
  between operations  15.5 us (2%)
  waiting for transfers between devices  8.97 us (1%)
    pallas_call x1, Pallas kernels, begin(): pl.pallas_call(begin_kernel, out_shape=(shape((tokens, 3 * D), f32), shap...  116 us
    pallas_call x1, Pallas kernels, last_exchange(): pl.pallas_call(last_kernel, out_shape=(jax.ShapeDtypeStruct((pairs, depth...  113 us
    pallas_call x1, Pallas kernels, attend_back(): pl.pallas_call(partial(attend_back_kernel, linked), grid=(HEADS // 2,), o...  100 us
    dot_general x8, matrix products, bfloat_product(): return jnp.dot(left_side, right_side, preferred_element_type=jnp.float32)  86.9 us
    pallas_call x1, Pallas kernels, dense_back(): pl.pallas_call(dense_back_kernel, grid=(wide // width,), out_shape=(shape...  81.9 us
    pallas_call x1, Pallas kernels, attend(): pl.pallas_call(partial(attend_kernel, linked), grid=(HEADS // 2,), out_sh...  64.6 us
  transfers between devices with their start and end apart: 1, of which 1 were waited for; matrix products, arithmetic and copies ran while one was open for 3% of the time, Pallas kernels for 18%

profile of v5, /device:TPU:0, one launch (start us, length us, event | category | flops | bytes accessed | tf_op | source)
XLA Modules:
  0.0 657.6 jit_solution(2136932666692273271)
XLA Ops:
  7.3 1.1 convert.8
  8.4 1.1 convert.7
  9.6 0.8 pad_maximum_fusion
  10.5 0.8 slice.195
  11.3 0.7 convert_element_type.61
  12.1 1.3 reduce_sum.113
  14.1 0.7 convert_element_type.63
  14.7 0.7 fusion.12
  15.4 0.9 pad_maximum_fusion.1
  16.5 1.0 stack.29
  17.7 0.8 pad.8.codes_ref
  18.6 0.8 pad.9.token_columns
  19.5 0.6 fusion.26
  20.1 0.7 maximum_maximum_fusion.2.rows_ref
  20.7 0.7 broadcast_in_dim.158.tags_ref
  21.4 116.5 %begin.1 = (f32[1024,3072]{1,0:T(8,128)}, bf16[2,2,2,2,2,32,3072]{6,5,4,3,2,1,0:T(8,128)(2,1)}, bf16[2,2,2,2,2,32,1024]{6,5,4,3,2,1,0:T(8,128)(2,1)}, f32[1024,1...) custom-call(bf16[32,128]{1,0:T(8,128)(2,1)} %maximum_maximum_fusion., ...), custom_call_target="tpu_custom_call" | custom-call | tf_op jit(solution)/shard_map/begin/pallas_call | solution.py:502
  137.9 1.5 slice.140.gain_ref
  139.3 0.8 slice.149
  140.1 0.7 copy.115.vectors_ref
  140.9 0.7 convert_element_type.67.refs_0_
  141.6 1.2 slice.150
  142.8 1.0 copy.114.second_ref
  144.0 0.9 reshape.173.moments_ref
  144.9 0.7 copy.117.vector_moment_ref
  145.6 0.7 broadcast_in_dim.186.column_moment_ref
  146.4 1.3 fusion.24
  147.7 0.7 maximum_maximum_fusion.mods_ref
  148.4 0.8 fusion.25
  149.3 8.9 %all-gather.2.cloned.1.call-done = bf16[512,8192]{1,0:T(8,128)(2,1)} async-done(((bf16[32,8192]{1,0:T(8,128)(2,1)}), bf16[512,8192]{1,0:T(8,128)(2,1)}) %all-gather.2.cloned.1.call-update) | async-done | bytes 8388624 | tf_op jit(solution)/shard_map/all_gather | solution.py:1586
  158.2 64.6 %attention_forward.1 = (bf16[1024,1024]{1,0:T(8,128)(2,1)}, f32[1024,1024]{1,0:T(8,128)}, f32[1024,1024]{1,0:T(8,128)}, bf16[2,2,2,2,2,4,32,1024]{7,6,5,4,3,2,1,...) custom-call(f32[1024,3072]{1,0:T(8,128)} %get-tuple-element.80.q_ref.k_ref.v_ref, ...), custom_call_target="tpu_custom_call" | custom-call | tf_op jit(solution)/shard_map/attention_forward/pallas_call | solution.py:711
  222.9 7.0 %fusion.23 = (f32[1024]{0:T(1024)S(1)}, f32[1024,1024]{1,0:T(8,128)S(1)}, f32[1024,1024]{1,0:T(8,128)}) fusion(f32[1024,1024]{1,0:T(8,128)S(1)} %copy-done.2, f32[1024]{0:T(1024)S(1)} %bitcast.72, f32[1024]{0:T(1024)S(1)} %bitcast.73, pred[1024]{0:T(1024)(128)(4,1)S(1)} %get-tuple-element.260, bf16[1024,1024]{1,0:T(8,128)(2,1)} %get-tuple-element.83, ...), kind=kOutput, calls=%fused_computation.77 | convolution fusion | flops 2151676928 | bytes 16790528 | tf_op jit(solution)/shard_map/dot_general | solution.py:46
  229.9 0.6 multiply_reduce_fusion.3
  230.5 5.0 add_convert_fusion.normed_ref
  235.5 11.6 %fusion.28.pre_ref = f32[1024,4096]{1,0:T(8,128)} fusion(bf16[1024,1024]{1,0:T(8,128)(2,1)S(1)} %add_convert_fusion.normed_ref, bf16[1024,4096]{1,0:T(8,128)(2,1)S(1)} %bitcast.55), kind=kOutput, calls=%fused_computation.82 | convolution fusion | flops 8589934592 | bytes 27262976 | tf_op jit(solution)/shard_map/dot_general | solution.py:46
  247.1 18.5 %fusion.21 = (f32[1024]{0:T(1024)S(1)}, f32[1024,1024]{1,0:T(8,128)S(1)}, f32[1024,1024]{1,0:T(8,128)}) fusion(f32[1024,1024]{1,0:T(8,128)S(1)} %get-tuple-element.266.residual_ref, f32[1024]{0:T(1024)S(1)} %bitcast.85, f32[1024]{0:T(1024)S(1)} %bitcast.83, pred[1024]{0:T(1024)(128)(4,1)S(1)} %get-tuple-element.260, bf16[4096,1024]{1,0:T(8,128)(2,1)} %bitcast.50, ...), kind=kOutput, calls=%fused_computation.76 | convolution fusion | flops 8631876608 | bytes 37762048 | tf_op jit(solution)/shard_map/dot_general | solution.py:46
  266.2 11.7 %fusion.27 = (f32[1024]{0:T(1024)S(1)}, f32[1024,4096]{1,0:T(8,128)S(1)}) fusion(bf16[1024,4096]{1,0:T(8,128)(2,1)} %bitcast.94, f32[1024,1024]{1,0:T(8,128)S(1)} %get-tuple-element.264, f32[1024]{0:T(1024)S(1)} %bitcast.74, f32[1024]{0:T(1024)S(1)} %fusion.13, f32[1024]{0:T(1024)S(1)} %broadcast_multiply_fusion), kind=kOutput, calls=%fused_computation.81 | convolution fusion | flops 8598322176 | bytes 29376512 | tf_op jit(solution)/shard_map/dot_general | solution.py:46
  277.9 5.6 select_reduce_fusion
  283.5 1.3 multiply_reduce_fusion.4
  284.8 7.8 %multiply_convert_fusion = bf16[1024,4096]{1,0:T(8,128)(2,1)} fusion(f32[1024,4096]{1,0:T(8,128)S(1)} %get-tuple-element.284, f32[1024]{0:T(1024)S(1)} %get-tuple-element.278, s32[1024]{0:T(1024)S(1)} %copy-done.13, f32[1024]{0:T(1024)S(1)} %get-tuple-element.257), kind=kLoop, calls=%fused_computation.10 | loop fusion | flops 25165824 | bytes 25178112 | tf_op jit(solution)/shard_map/convert_element_type | solution.py:1684
  292.6 15.7 %multiply_reduce_fusion = (f32[1024]{0:T(1024)S(1)}, f32[1024]{0:T(1024)S(1)}, f32[1024,1024]{1,0:T(8,128)S(1)}) fusion(f32[1024,1024]{1,0:T(8,128)S(1)} %get-tuple-element.264, f32[1024]{0:T(1024)S(1)} %fusion.13, f32[1024]{0:T(1024)S(1)} %broadcast_multiply_fusion, f32[1024]{0:T(1024)S(1)} %bitcast.75, bf16[1024,4096]{1,0:T(8,128)(2,1)} %multiply_convert_fusion, ...), kind=kOutput, calls=%fused_computation.20 | convolution fusion | flops 8597272576 | bytes 25186304 | tf_op jit(solution)/shard_map/dot_general | solution.py:46
  308.3 12.5 %convolution_convert_fusion = bf16[1024,4096]{1,0:T(8,128)(2,1)} fusion(bf16[1024,4096]{1,0:T(8,128)(2,1)S(1)} %copy-done.3, f32[1024,1024]{1,0:T(8,128)S(1)} %get-tuple-element.264, f32[1024]{0:T(1024)S(1)} %bitcast.76, f32[1024]{0:T(1024)S(1)} %fusion.13, f32[1024]{0:T(1024)S(1)} %broadcast_multiply_fusion), kind=kOutput, calls=%fused_computation.14 | convolution fusion | flops 8598323200 | bytes 20983808 | tf_op jit(solution)/shard_map/dot_general | solution.py:46
  320.8 1.9 fusion.20
  323.0 1.3 select_reduce_fusion.2
  324.3 2.1 fusion.11.branch_ref
  326.4 0.6 copy-done.1
  327.0 81.9 %dense_backward.1 = (bf16[1024,4096]{1,0:T(8,128)(2,1)}, bf16[4096,1024]{1,0:T(8,128)(2,1)}, f32[1024,1024]{1,0:T(8,128)}, bf16[1024,1024]{1,0:T(8,128)(2,1)}, f32[8,1024]{1,0:T(8,128)}, /*index=5*/f32[8,32,512]{2,1,0:T(8,128)}) custom-call(bf16[1024,1024]{1,0:T(8,128)(2,1)} %fusion.11.branch_ref, bf16[1024,1024]{1,0:T(8,128)(2,1)} %copy-done.4, ...), custom_call_target="tpu_custom_call" | custom-call | tf_op jit(solution)/shard_map/dense_backward/pallas_call | solution.py:974
  408.9 6.1 convolution_convert_fusion.2
  415.0 3.8 convolution_convert_fusion.1.m_ref
  418.9 100.0 %attention_backward.1 = (bf16[3,1024,1024]{2,1,0:T(8,128)(2,1)}, f32[8,1024]{1,0:T(8,128)}, f32[16,32,512]{2,1,0:T(8,128)}) custom-call(f32[1024,3072]{1,0:T(8,128)} %get-tuple-element.80.q_ref.k_ref.v_ref, f32[1024,3072]{1,0:T(8,128)} %get-tuple-element.80.q_ref.k_ref.v_ref, f32[1024,3072]{1,0:T(8,128)} %get-tuple-element.80.q_ref.k_ref.v_ref, ...), custom_call_target="tpu_custom_call" | custom-call | tf_op jit(solution)/shard_map/attention_backward/pallas_call | solution.py:845
  519.0 0.8 slice.157
  519.8 0.7 maximum_maximum_fusion.1.gains_ref
  520.4 112.7 %last_scatter.1 = (f32[8,32,512]{2,1,0:T(8,128)}, f32[32,128]{1,0:T(8,128)}, f32[32,1152]{1,0:T(8,128)}, f32[32,6144]{1,0:T(8,128)}, f32[10,32,1]{2,1,0:T(8,128)...) custom-call(bf16[2,2,2,2,2,32,1024]{6,5,4,3,2,1,0:T(8,128)(2,1)} %bitcast.63, bf16[1024,3072]{1,0:T(8,128)(2,1)} %bitcast.60, ...), custom_call_target="tpu_custom_call" | custom-call | tf_op jit(solution)/shard_map/last_scatter/pallas_call | solution.py:1387
  633.1 1.5 slice_reduce_fusion.1
  634.7 0.9 slice_reduce_fusion
  635.6 0.9 slice.177
  636.5 0.7 slice_reduce_fusion.7
  637.2 0.7 copy.127
  637.9 0.6 slice.160
  639.0 6.1 weight_step.1
  645.0 1.4 copy.120
  646.4 1.4 copy.121
  647.8 1.4 copy.122
  649.2 0.6 slice.172
  649.8 0.7 pad_maximum_fusion.2
  (90 shorter events, 2.6 us)
Async XLA Ops:
  7.2 132.9 %copy-start.11 = (f32[32,9]{0,1:T(8,128)S(1)}, f32[32,9]{0,1:T(8,128)}, u32[]{:S(2)}) copy-start(f32[32,9]{0,1:T(8,128)} %param.32) | copy-start | bytes 3460
  7.2 133.6 %copy-start.9 = (f32[20498]{0:T(1024)S(1)}, f32[20498]{0:T(1024)}, u32[]{:S(2)}) copy-start(f32[20498]{0:T(1024)} %param.47) | copy-start | bytes 245980
  7.2 133.6 %copy-start.5 = (f32[128,1024]{1,0:T(8,128)S(1)}, f32[128,1024]{1,0:T(8,128)}, u32[]{:S(2)}) copy-start(f32[128,1024]{1,0:T(8,128)} %down_master.3) | copy-start | bytes 1572868
  7.2 151.0 %all-gather.2.cloned.1.call-start = ((), (), s32[]{:S(2)}) async-start(), calls=%async_computation | async-start | bytes 8912896 | tf_op jit(solution)/shard_map/all_gather | solution.py:1586
  8.4 134.4 %copy-start.15 = (s32[1024]{0:T(1024)S(1)}, s32[1024]{0:T(1024)}, u32[]{:S(2)}) copy-start(s32[1024]{0:T(1024)} %param.26) | copy-start | bytes 12292
  9.5 134.3 %copy-start.18 = (f32[32]{0:T(128)S(1)}, f32[32]{0:T(128)}, u32[]{:S(2)}) copy-start(f32[32]{0:T(128)} %param.39) | copy-start | bytes 388
  9.5 134.3 %copy-start.19 = (f32[32]{0:T(128)S(1)}, f32[32]{0:T(128)}, u32[]{:S(2)}) copy-start(f32[32]{0:T(128)} %param.40) | copy-start | bytes 388
  9.5 134.3 %copy-start.20 = (f32[32]{0:T(128)S(1)}, f32[32]{0:T(128)}, u32[]{:S(2)}) copy-start(f32[32]{0:T(128)} %param.41) | copy-start | bytes 388
  9.5 134.3 %copy-start.21 = (f32[32]{0:T(128)S(1)}, f32[32]{0:T(128)}, u32[]{:S(2)}) copy-start(f32[32]{0:T(128)} %param.42) | copy-start | bytes 388
  9.6 134.3 %copy-start.22 = (f32[32]{0:T(128)S(1)}, f32[32]{0:T(128)}, u32[]{:S(2)}) copy-start(f32[32]{0:T(128)} %param.43) | copy-start | bytes 388
  9.6 134.3 %copy-start.23 = (f32[32]{0:T(128)S(1)}, f32[32]{0:T(128)}, u32[]{:S(2)}) copy-start(f32[32]{0:T(128)} %param.45) | copy-start | bytes 388
  9.6 134.3 %copy-start.24 = (f32[128]{0:T(128)S(1)}, f32[128]{0:T(128)}, u32[]{:S(2)}) copy-start(f32[128]{0:T(128)} %param.44) | copy-start | bytes 1540
  9.6 135.3 %copy-start.16 = (f32[32,9]{0,1:T(8,128)S(1)}, f32[32,9]{0,1:T(8,128)}, u32[]{:S(2)}) copy-start(f32[32,9]{0,1:T(8,128)} %param.46) | copy-start | bytes 3460
  9.6 135.9 %slice-start.2 = ((f32[20498]{0:T(1024)}), f32[1042]{0:T(1024)S(1)}, s32[]{:S(2)}) async-start(f32[20498]{0:T(1024)} %param.47), calls=%async_computation.3 | async-start | bytes 16384 | tf_op jit(solution)/shard_map/slice | solution.py:1749
  17.5 3.9 copy-start.8
  158.2 64.6 %copy-start.2 = (f32[1024,1024]{1,0:T(8,128)S(1)}, f32[1024,1024]{1,0:T(8,128)}, u32[]{:S(2)}) copy-start(f32[1024,1024]{1,0:T(8,128)} %get-tuple-element.85.embedded_ref) | copy-start | bytes 12582916
  222.8 12.6 %slice-start = ((s8[8388608]{0:T(1024)(128)(4,1)}), s8[4194304]{0:T(1024)(128)(4,1)S(1)}, s32[]{:S(2)}) async-start(s8[8388608]{0:T(1024)(128)(4,1)} %bitcast.53), calls=%async_computation.1 | async-start | bytes 8388608
  222.8 12.6 %slice-start.1 = ((s8[8388608]{0:T(1024)(128)(4,1)}), s8[4194304]{0:T(1024)(128)(4,1)S(1)}, s32[]{:S(2)}) async-start(s8[8388608]{0:T(1024)(128)(4,1)} %bitcast.53), calls=%async_computation.2 | async-start | bytes 8388608
  229.9 17.2 %copy-start = (f32[1024,1024]{1,0:T(8,128)}, f32[1024,1024]{1,0:T(8,128)S(1)}, u32[]{:S(2)}) copy-start(f32[1024,1024]{1,0:T(8,128)S(1)} %get-tuple-element.266.residual_ref) | copy-start | bytes 12582916
  235.4 11.7 %copy-start.4 = (bf16[1024,1024]{1,0:T(8,128)(2,1)}, bf16[1024,1024]{1,0:T(8,128)(2,1)S(1)}, u32[]{:S(2)}) copy-start(bf16[1024,1024]{1,0:T(8,128)(2,1)S(1)} %add_convert_fusion.normed_ref) | copy-start | bytes 6291460
  266.1 11.8 %copy-start.13 = (s32[1024]{0:T(1024)S(1)}, s32[1024]{0:T(1024)}, u32[]{:S(2)}) copy-start(s32[1024]{0:T(1024)} %param.29) | copy-start | bytes 12292
  277.9 5.6 copy-start.14
  292.6 15.7 %copy-start.3 = (bf16[1024,4096]{1,0:T(8,128)(2,1)S(1)}, bf16[1024,4096]{1,0:T(8,128)(2,1)}, u32[]{:S(2)}) copy-start(bf16[1024,4096]{1,0:T(8,128)(2,1)} %multiply_convert_fusion) | copy-start | bytes 25165828
  320.8 2.2 copy-start.6
  324.3 2.7 copy-start.1
  408.9 6.1 copy-start.7
  408.9 6.1 copy-start.25
  415.0 3.8 copy-start.12
  418.9 100.1 %copy-start.10 = (f32[2,6144]{1,0:T(2,128)}, f32[2,6144]{1,0:T(2,128)S(1)}, u32[]{:S(2)}) copy-start(f32[2,6144]{1,0:T(2,128)S(1)} %constant_dynamic-update-slice_fusion.known_ref) | copy-start | bytes 147460
  418.9 100.8 %copy-start.17 = (f32[8]{0:T(128)S(1)}, f32[8]{0:T(128)}, u32[]{:S(2)}) copy-start(f32[8]{0:T(128)} %get-tuple-element.279) | copy-start | bytes 100
Sparse Core Ops, SparseCore 0:
  11.4 146.7 all-gather.1

commit v6 on v5

--- a/solution.py
+++ b/solution.py
@@ -574,20 +574,15 @@
 
 def attend_kernel(linked, q_ref, k_ref, v_ref, gain_ref, bias_ref, *refs):
     if linked:
-        down_own, half_ref, mixed_ref, exact_ref, total_ref, down_full, up_full, head_full = refs[:8]
-        qn, kn, vn, pair_sems, passing, pass_sems = refs[8:14]
-        sems = refs[14:]
+        down_own, half_ref, mixed_ref, exact_ref, total_ref, down_full, up_full = refs[:7]
+        qn, kn, vn, pair_sems, passing, pass_sems = refs[7:13]
+        sems = refs[13:]
         place = Place()
         core = place.bit["c"]
 
         def pair_copies():
-            start = 0
-            for order, full in enumerate((up_full, head_full)):
-                size = full.shape[6]
-                source = half_ref.at[:, :, :, :, :, start : start + size]
-                target = full.at[:, :, :, :, core]
-                yield place.send(source, target, pair_sems.at[0, order], pair_sems.at[1, order], "c")
-                start += size
+            target = up_full.at[:, :, :, :, core]
+            yield place.send(half_ref, target, pair_sems.at[0, 0], pair_sems.at[1, 0], "c")
 
         chunks = HEADS // 2
         piece = passing.shape[6]
@@ -598,10 +593,9 @@
             )
 
         def save(i):
-            full = (up_full, head_full)[i // (chunks // 2)]
-            at = (i % (chunks // 2)) * piece
+            at = i * piece
             return pltpu.make_async_copy(
-                passing.at[i % 2], full.at[:, :, :, :, core, :, at : at + piece], pass_sems.at[1, i % 2]
+                passing.at[i % 2], up_full.at[:, :, :, :, core, :, at : at + piece], pass_sems.at[1, i % 2]
             )
 
         def each_chunk(body):
@@ -703,8 +697,8 @@
         specs += [ANY, ANY]
         operands += [down_own, half]
         outs += [jax.ShapeDtypeStruct(FIVE + (down_own.shape[0] // depth, depth, D), jnp.bfloat16)]
-        outs += [jax.ShapeDtypeStruct(FIVE + (depth, half.shape[5] // 2), jnp.bfloat16)] * 2
-        out_specs += [ANY] * 3
+        outs += [jax.ShapeDtypeStruct(FIVE + (depth, half.shape[5]), jnp.bfloat16)]
+        out_specs += [ANY] * 2
         scratch = scratch + [pltpu.SemaphoreType.DMA((2, 2))]
         scratch += [pltpu.VMEM((2,) + half.shape[:5] + (half.shape[5] // (HEADS // 2),), jnp.bfloat16)]
         scratch += [pltpu.SemaphoreType.DMA((2, 2))] + Gather.scratch(ATTEND_LAG)
@@ -1583,8 +1577,8 @@
 
     if linked:
         cores = [[core + 2 * chip for chip in range(devices // 2)] for core in range(2)]
-        up_head = lax.all_gather(
-            jnp.concatenate([up_weight, head_weight], axis=1).astype(low),
+        up_half = lax.all_gather(
+            up_weight.astype(low),
             AXES,
             axis_index_groups=cores,
             axis=0,
@@ -1592,7 +1586,7 @@
         ).reshape(2, 2, 2, 2, depth, -1)
     else:
         full_up = gathered(up_weight.astype(low))
-        full_head = gathered(head_weight.astype(low))
+    full_head = gathered(head_weight.astype(low))
     small_rows = jnp.concatenate(
         [vectors.astype(low), tables_low[:, CLASSES:], jnp.zeros((depth, 128 - SMALL_LANES), low)], axis=1
     )
@@ -1649,11 +1643,9 @@
         of_token(block) for block in range(6)
     )
     if linked:
-        mixed_heads, exact, totals, full_down, full_up, full_head = attend(
-            projected, gains, bias, down_low, up_head
-        )
+        mixed_heads, exact, totals, full_down, full_up = attend(projected, gains, bias, down_low, up_half)
         full_down = full_down.reshape(-1, D)
-        full_up, full_head = full_up.reshape(D, -1), full_head.reshape(D, -1)
+        full_up = full_up.reshape(D, -1)
     else:
         normed = modulate(embedded, scale_one, shift_one).astype(low)
         projected = bfloat_product(normed, full_qkv)

time: 661 us -> 665 us (level)
  Pallas kernels: 482 us -> 492 us
  waiting for transfers between devices: 8.97 us -> 0.08 us
    pallas_call x1, Pallas kernels: 64.6 us -> 83.2 us  [attend(): pl.pallas_call(partial(attend_kernel, linked), grid=(HEADS // 2,), out_sh...]
    all_gather x1 -> x2, waiting for transfers between devices: 8.95 us -> 0.04 us  [the longest x1 0.02 us: gathered(): return lax.all_gather(values, AXES, axis=0, tiled=True)]
    pallas_call x1, Pallas kernels: 116 us -> 108 us  [begin(): pl.pallas_call(begin_kernel, out_shape=(shape((tokens, 3 * D), f32), shap...]
  transfers between devices with their start and end apart: 1 -> 2, of which waited for: 1 -> 0; matrix products, arithmetic and copies ran while one was open for 3% -> 10% of each run, Pallas kernels for 18% -> 29%
where the time goes in v6:
time: 665 us; the launch traced here: 661 us
  Pallas kernels  492 us (74%)
  matrix products  87 us (13%)
  other arithmetic  38 us (6%)
  local copies, waits for them, and re-layouts  29 us (4%)
  between operations  15.5 us (2%)
    pallas_call x1, Pallas kernels, last_exchange(): pl.pallas_call(last_kernel, out_shape=(jax.ShapeDtypeStruct((pairs, depth...  112 us
    pallas_call x1, Pallas kernels, begin(): pl.pallas_call(begin_kernel, out_shape=(shape((tokens, 3 * D), f32), shap...  108 us
    pallas_call x1, Pallas kernels, attend_back(): pl.pallas_call(partial(attend_back_kernel, linked), grid=(HEADS // 2,), o...  101 us
    dot_general x8, matrix products, bfloat_product(): return jnp.dot(left_side, right_side, preferred_element_type=jnp.float32)  87 us
    pallas_call x1, Pallas kernels, attend(): pl.pallas_call(partial(attend_kernel, linked), grid=(HEADS // 2,), out_sh...  83.2 us
    pallas_call x1, Pallas kernels, dense_back(): pl.pallas_call(dense_back_kernel, grid=(wide // width,), out_shape=(shape...  81.2 us
  transfers between devices with their start and end apart: 2, of which 0 were waited for; matrix products, arithmetic and copies ran while one was open for 10% of the time, Pallas kernels for 29%

profile of v6, /device:TPU:0, one launch (start us, length us, event | category | flops | bytes accessed | tf_op | source)
XLA Modules:
  0.0 661.2 jit_solution(8415227764673899664)
XLA Ops:
  7.3 1.8 convert_element_type.73
  9.3 1.8 convert_element_type.77
  11.1 0.8 slice.195
  11.9 0.7 convert_element_type.66
  12.7 1.3 reduce_sum.113
  14.7 0.7 convert_element_type.68
  15.3 0.7 fusion.12
  16.0 0.9 pad_maximum_fusion
  17.1 1.0 stack.29
  18.3 0.8 pad.8.codes_ref
  19.3 0.8 pad.9.token_columns
  20.1 0.6 fusion.26
  20.7 0.7 maximum_maximum_fusion.2.rows_ref
  21.4 0.7 broadcast_in_dim.158.tags_ref
  22.0 108.4 %begin.1 = (f32[1024,3072]{1,0:T(8,128)}, bf16[2,2,2,2,2,32,3072]{6,5,4,3,2,1,0:T(8,128)(2,1)}, bf16[2,2,2,2,2,32,1024]{6,5,4,3,2,1,0:T(8,128)(2,1)}, f32[1024,1...) custom-call(bf16[32,128]{1,0:T(8,128)(2,1)} %maximum_maximum_fusion., ...), custom_call_target="tpu_custom_call" | custom-call | tf_op jit(solution)/shard_map/begin/pallas_call | solution.py:502
  130.4 1.5 slice.140.gain_ref
  131.8 0.8 slice.149
  132.6 0.7 copy.115.vectors_ref
  133.4 0.7 convert_element_type.72.refs_0_
  134.1 1.2 slice.150
  135.3 1.0 copy.114.second_ref
  136.5 0.9 reshape.169.moments_ref
  137.4 0.7 copy.117.vector_moment_ref
  138.1 0.7 broadcast_in_dim.186.column_moment_ref
  138.9 1.3 fusion.24
  140.2 0.7 maximum_maximum_fusion.mods_ref
  140.9 0.8 fusion.25
  141.8 83.2 %attention_forward.1 = (bf16[1024,1024]{1,0:T(8,128)(2,1)}, f32[1024,1024]{1,0:T(8,128)}, f32[1024,1024]{1,0:T(8,128)}, bf16[2,2,2,2,2,4,32,1024]{7,6,5,4,3,2,1,...) custom-call(f32[1024,3072]{1,0:T(8,128)} %get-tuple-element.79.q_ref.k_ref.v_ref, ...), custom_call_target="tpu_custom_call" | custom-call | tf_op jit(solution)/shard_map/attention_forward/pallas_call | solution.py:705
  225.0 7.0 %fusion.23 = (f32[1024]{0:T(1024)S(1)}, f32[1024,1024]{1,0:T(8,128)S(1)}, f32[1024,1024]{1,0:T(8,128)}) fusion(f32[1024,1024]{1,0:T(8,128)S(1)} %copy-done.2, f32[1024]{0:T(1024)S(1)} %bitcast.71, f32[1024]{0:T(1024)S(1)} %bitcast.72, pred[1024]{0:T(1024)(128)(4,1)S(1)} %get-tuple-element.258, bf16[1024,1024]{1,0:T(8,128)(2,1)} %get-tuple-element.82, ...), kind=kOutput, calls=%fused_computation.76 | convolution fusion | flops 2151676928 | bytes 16790528 | tf_op jit(solution)/shard_map/dot_general | solution.py:46
  232.1 0.6 multiply_reduce_fusion.3
  232.6 5.0 add_convert_fusion.normed_ref
  237.6 11.6 %fusion.28.pre_ref = f32[1024,4096]{1,0:T(8,128)} fusion(bf16[1024,1024]{1,0:T(8,128)(2,1)S(1)} %add_convert_fusion.normed_ref, bf16[1024,4096]{1,0:T(8,128)(2,1)S(1)} %bitcast.54), kind=kOutput, calls=%fused_computation.81 | convolution fusion | flops 8589934592 | bytes 27262976 | tf_op jit(solution)/shard_map/dot_general | solution.py:46
  249.3 18.4 %fusion.21 = (f32[1024]{0:T(1024)S(1)}, f32[1024,1024]{1,0:T(8,128)S(1)}, f32[1024,1024]{1,0:T(8,128)}) fusion(f32[1024,1024]{1,0:T(8,128)S(1)} %get-tuple-element.264.residual_ref, f32[1024]{0:T(1024)S(1)} %bitcast.84, f32[1024]{0:T(1024)S(1)} %bitcast.82, pred[1024]{0:T(1024)(128)(4,1)S(1)} %get-tuple-element.258, bf16[4096,1024]{1,0:T(8,128)(2,1)} %bitcast.49, ...), kind=kOutput, calls=%fused_computation.75 | convolution fusion | flops 8631876608 | bytes 37762048 | tf_op jit(solution)/shard_map/dot_general | solution.py:46
  267.7 1.9 copy-done.3
  269.6 0.6 multiply_reduce_fusion.2
  270.2 12.9 %fusion.27 = (f32[1024]{0:T(1024)S(1)}, f32[1024,4096]{1,0:T(8,128)S(1)}) fusion(bf16[1024,4096]{1,0:T(8,128)(2,1)} %all-gather.5.cloned.1.call-done, f32[1024,1024]{1,0:T(8,128)} %copy-done.3, f32[1024]{0:T(1024)S(1)} %bitcast.73, f32[1024]{0:T(1024)S(1)} %fusion.13, f32[1024]{0:T(1024)S(1)} %broadcast_multiply_fusion), kind=kOutput, calls=%fused_computation.80 | convolution fusion | flops 8598322176 | bytes 29376512 | tf_op jit(solution)/shard_map/dot_general | solution.py:46
  283.2 5.6 select_reduce_fusion
  288.8 1.3 multiply_reduce_fusion.4
  290.1 7.8 %multiply_convert_fusion = bf16[1024,4096]{1,0:T(8,128)(2,1)} fusion(f32[1024,4096]{1,0:T(8,128)S(1)} %get-tuple-element.282, f32[1024]{0:T(1024)S(1)} %get-tuple-element.276, s32[1024]{0:T(1024)S(1)} %copy-done.15, f32[1024]{0:T(1024)S(1)} %get-tuple-element.255), kind=kLoop, calls=%fused_computation.10 | loop fusion | flops 25165824 | bytes 25178112 | tf_op jit(solution)/shard_map/convert_element_type | solution.py:1676
  297.9 15.2 %convolution_convert_fusion = bf16[1024,4096]{1,0:T(8,128)(2,1)} fusion(bf16[1024,4096]{1,0:T(8,128)(2,1)} %multiply_convert_fusion, f32[1024,1024]{1,0:T(8,128)S(1)} %copy-done.4, f32[1024]{0:T(1024)S(1)} %bitcast.74, f32[1024]{0:T(1024)S(1)} %fusion.13, f32[1024]{0:T(1024)S(1)} %broadcast_multiply_fusion), kind=kOutput, calls=%fused_computation.14 | convolution fusion | flops 8598323200 | bytes 20983808 | tf_op jit(solution)/shard_map/dot_general | solution.py:46
  313.1 12.0 %multiply_reduce_fusion = (f32[1024]{0:T(1024)S(1)}, f32[1024]{0:T(1024)S(1)}, f32[1024,1024]{1,0:T(8,128)S(1)}) fusion(f32[1024,1024]{1,0:T(8,128)S(1)} %copy-done.4, f32[1024]{0:T(1024)S(1)} %fusion.13, f32[1024]{0:T(1024)S(1)} %broadcast_multiply_fusion, f32[1024]{0:T(1024)S(1)} %bitcast.75, bf16[1024,4096]{1,0:T(8,128)(2,1)S(1)} %copy-done.5, ...), kind=kOutput, calls=%fused_computation.20 | convolution fusion | flops 8597272576 | bytes 25186304 | tf_op jit(solution)/shard_map/dot_general | solution.py:46
  325.2 1.8 fusion.20
  327.3 1.3 select_reduce_fusion.2
  328.6 2.1 fusion.11.branch_ref
  330.8 0.6 copy-done.1
  331.4 81.2 %dense_backward.1 = (bf16[1024,4096]{1,0:T(8,128)(2,1)}, bf16[4096,1024]{1,0:T(8,128)(2,1)}, f32[1024,1024]{1,0:T(8,128)}, bf16[1024,1024]{1,0:T(8,128)(2,1)}, f32[8,1024]{1,0:T(8,128)}, /*index=5*/f32[8,32,512]{2,1,0:T(8,128)}) custom-call(bf16[1024,1024]{1,0:T(8,128)(2,1)} %fusion.11.branch_ref, bf16[1024,1024]{1,0:T(8,128)(2,1)} %copy-done.6, ...), custom_call_target="tpu_custom_call" | custom-call | tf_op jit(solution)/shard_map/dense_backward/pallas_call | solution.py:968
  412.6 6.1 convolution_convert_fusion.2
  418.7 3.7 convolution_convert_fusion.1.m_ref
  422.5 101.2 %attention_backward.1 = (bf16[3,1024,1024]{2,1,0:T(8,128)(2,1)}, f32[8,1024]{1,0:T(8,128)}, f32[16,32,512]{2,1,0:T(8,128)}) custom-call(f32[1024,3072]{1,0:T(8,128)} %get-tuple-element.79.q_ref.k_ref.v_ref, f32[1024,3072]{1,0:T(8,128)} %get-tuple-element.79.q_ref.k_ref.v_ref, f32[1024,3072]{1,0:T(8,128)} %get-tuple-element.79.q_ref.k_ref.v_ref, ...), custom_call_target="tpu_custom_call" | custom-call | tf_op jit(solution)/shard_map/attention_backward/pallas_call | solution.py:839
  523.7 0.8 slice.157
  524.4 0.7 maximum_maximum_fusion.1.gains_ref
  525.1 111.6 %last_scatter.1 = (f32[8,32,512]{2,1,0:T(8,128)}, f32[32,128]{1,0:T(8,128)}, f32[32,1152]{1,0:T(8,128)}, f32[32,6144]{1,0:T(8,128)}, f32[10,32,1]{2,1,0:T(8,128)...) custom-call(bf16[2,2,2,2,2,32,1024]{6,5,4,3,2,1,0:T(8,128)(2,1)} %bitcast.62, bf16[1024,3072]{1,0:T(8,128)(2,1)} %bitcast.58, ...), custom_call_target="tpu_custom_call" | custom-call | tf_op jit(solution)/shard_map/last_scatter/pallas_call | solution.py:1381
  636.7 1.5 slice_reduce_fusion.1
  638.2 0.9 slice_reduce_fusion
  639.2 0.9 slice.177
  640.1 0.7 slice_reduce_fusion.7
  640.8 0.7 copy.127
  641.5 0.6 slice.160
  642.6 6.1 weight_step.1
  648.6 1.4 copy.120
  650.0 1.4 copy.121
  651.4 1.4 copy.122
  652.8 0.6 slice.172
  653.4 0.7 pad_maximum_fusion.1
  (96 shorter events, 2.2 us)
Async XLA Ops:
  7.2 125.4 %copy-start.13 = (f32[32,9]{0,1:T(8,128)S(1)}, f32[32,9]{0,1:T(8,128)}, u32[]{:S(2)}) copy-start(f32[32,9]{0,1:T(8,128)} %param.32) | copy-start | bytes 3460
  7.2 128.1 %copy-start.17 = (s32[1024]{0:T(1024)S(1)}, s32[1024]{0:T(1024)}, u32[]{:S(2)}) copy-start(s32[1024]{0:T(1024)} %param.26) | copy-start | bytes 12292
  7.2 126.1 %copy-start.11 = (f32[20498]{0:T(1024)S(1)}, f32[20498]{0:T(1024)}, u32[]{:S(2)}) copy-start(f32[20498]{0:T(1024)} %param.47) | copy-start | bytes 245980
  7.2 126.2 %copy-start.7 = (f32[128,1024]{1,0:T(8,128)S(1)}, f32[128,1024]{1,0:T(8,128)}, u32[]{:S(2)}) copy-start(f32[128,1024]{1,0:T(8,128)} %down_master.3) | copy-start | bytes 1572868
  7.2 134.6 %all-gather.3.cloned.1.call-start = ((), (), s32[]{:S(2)}) async-start(), calls=%async_computation | async-start | bytes 4456448 | tf_op jit(solution)/shard_map/all_gather | solution.py:1580
  9.1 127.2 %copy-start.20 = (f32[32]{0:T(128)S(1)}, f32[32]{0:T(128)}, u32[]{:S(2)}) copy-start(f32[32]{0:T(128)} %param.39) | copy-start | bytes 388
  9.1 127.2 %copy-start.21 = (f32[32]{0:T(128)S(1)}, f32[32]{0:T(128)}, u32[]{:S(2)}) copy-start(f32[32]{0:T(128)} %param.40) | copy-start | bytes 388
  9.1 127.2 %copy-start.22 = (f32[32]{0:T(128)S(1)}, f32[32]{0:T(128)}, u32[]{:S(2)}) copy-start(f32[32]{0:T(128)} %param.41) | copy-start | bytes 388
  9.1 127.2 %copy-start.23 = (f32[32]{0:T(128)S(1)}, f32[32]{0:T(128)}, u32[]{:S(2)}) copy-start(f32[32]{0:T(128)} %param.42) | copy-start | bytes 388
  9.1 127.2 %copy-start.24 = (f32[32]{0:T(128)S(1)}, f32[32]{0:T(128)}, u32[]{:S(2)}) copy-start(f32[32]{0:T(128)} %param.43) | copy-start | bytes 388
  9.1 127.2 %copy-start.25 = (f32[32]{0:T(128)S(1)}, f32[32]{0:T(128)}, u32[]{:S(2)}) copy-start(f32[32]{0:T(128)} %param.45) | copy-start | bytes 388
  9.2 127.2 %copy-start.26 = (f32[128]{0:T(128)S(1)}, f32[128]{0:T(128)}, u32[]{:S(2)}) copy-start(f32[128]{0:T(128)} %param.44) | copy-start | bytes 1540
  9.2 128.2 %copy-start.18 = (f32[32,9]{0,1:T(8,128)S(1)}, f32[32,9]{0,1:T(8,128)}, u32[]{:S(2)}) copy-start(f32[32,9]{0,1:T(8,128)} %param.46) | copy-start | bytes 3460
  9.2 128.9 %slice-start.2 = ((f32[20498]{0:T(1024)}), f32[1042]{0:T(1024)S(1)}, s32[]{:S(2)}) async-start(f32[20498]{0:T(1024)} %param.47), calls=%async_computation.4 | async-start | bytes 16384 | tf_op jit(solution)/shard_map/slice | solution.py:1741
  9.2 261.0 %all-gather.5.cloned.1.call-start = ((), (), s32[]{:S(2)}) async-start(), calls=%async_computation.1 | async-start | bytes 8650752 | tf_op jit(solution)/shard_map/all_gather | solution.py:1498
  18.1 3.9 copy-start.10
  141.8 83.2 %copy-start.2 = (f32[1024,1024]{1,0:T(8,128)S(1)}, f32[1024,1024]{1,0:T(8,128)}, u32[]{:S(2)}) copy-start(f32[1024,1024]{1,0:T(8,128)} %get-tuple-element.84.embedded_ref) | copy-start | bytes 12582916
  225.0 12.6 %slice-start = ((s8[8388608]{0:T(1024)(128)(4,1)}), s8[4194304]{0:T(1024)(128)(4,1)S(1)}, s32[]{:S(2)}) async-start(s8[8388608]{0:T(1024)(128)(4,1)} %bitcast.52), calls=%async_computation.2 | async-start | bytes 8388608
  225.0 12.6 %slice-start.1 = ((s8[8388608]{0:T(1024)(128)(4,1)}), s8[4194304]{0:T(1024)(128)(4,1)S(1)}, s32[]{:S(2)}) async-start(s8[8388608]{0:T(1024)(128)(4,1)} %bitcast.52), calls=%async_computation.3 | async-start | bytes 8388608
  232.0 17.2 %copy-start = (f32[1024,1024]{1,0:T(8,128)}, f32[1024,1024]{1,0:T(8,128)S(1)}, u32[]{:S(2)}) copy-start(f32[1024,1024]{1,0:T(8,128)S(1)} %get-tuple-element.264.residual_ref) | copy-start | bytes 12582916
  237.6 11.7 %copy-start.6 = (bf16[1024,1024]{1,0:T(8,128)(2,1)}, bf16[1024,1024]{1,0:T(8,128)(2,1)S(1)}, u32[]{:S(2)}) copy-start(bf16[1024,1024]{1,0:T(8,128)(2,1)S(1)} %add_convert_fusion.normed_ref) | copy-start | bytes 6291460
  267.7 1.9 copy-start.3
  270.2 12.9 %copy-start.15 = (s32[1024]{0:T(1024)S(1)}, s32[1024]{0:T(1024)}, u32[]{:S(2)}) copy-start(s32[1024]{0:T(1024)} %param.29) | copy-start | bytes 12292
  283.2 5.6 copy-start.16
  290.1 7.8 %copy-start.4 = (f32[1024,1024]{1,0:T(8,128)S(1)}, f32[1024,1024]{1,0:T(8,128)}, u32[]{:S(2)}) copy-start(f32[1024,1024]{1,0:T(8,128)} %copy-done.3) | copy-start | bytes 12582916
  297.9 15.2 %copy-start.5 = (bf16[1024,4096]{1,0:T(8,128)(2,1)S(1)}, bf16[1024,4096]{1,0:T(8,128)(2,1)}, u32[]{:S(2)}) copy-start(bf16[1024,4096]{1,0:T(8,128)(2,1)} %multiply_convert_fusion) | copy-start | bytes 25165828
  325.2 2.2 copy-start.8
  328.6 2.7 copy-start.1
  412.6 6.1 copy-start.9
  412.6 6.1 copy-start.27
  418.7 3.7 copy-start.14
  422.5 101.2 %copy-start.12 = (f32[2,6144]{1,0:T(2,128)}, f32[2,6144]{1,0:T(2,128)S(1)}, u32[]{:S(2)}) copy-start(f32[2,6144]{1,0:T(2,128)S(1)} %constant_dynamic-update-slice_fusion.known_ref) | copy-start | bytes 147460
  422.5 101.9 %copy-start.19 = (f32[8]{0:T(128)S(1)}, f32[8]{0:T(128)}, u32[]{:S(2)}) copy-start(f32[8]{0:T(128)} %get-tuple-element.277) | copy-start | bytes 100
Sparse Core Ops, SparseCore 0:
  11.4 102.1 all-gather.2
  117.0 98.2 all-gather.4
